TPU v7x, 32 devices: a whole 2x2x4 slice. The times are simulated.
32 devices in a mesh: section: 2 (over core), row: 4 (over y, x), col: 4 (over z).
Axes of the slice: x: 2, y: 2, z: 4, core: 2. Of those that a mesh axis runs over, the one named last changes fastest.
Arguments:
- section_input: bfloat16 [64, 61440], P('row', ('section', 'col')), may hold values from -6 to 6
- cache_three: bfloat16 [64, 30720], P('row', ('section', 'col')), may hold values from -6 to 6
- gain_three: float32 [192], replicated, may hold values from 0.25 to 1.75
- bias_three: float32 [192], replicated, may hold values from -2 to 2
- weight_three: bfloat16 [27, 36864], replicated, may hold values from -0.078125 to 0.078125
- weight_up: bfloat16 [9, 18432], replicated, may hold values from -0.15625 to 0.15625
- bias_up: float32 [96], replicated, may hold values from -2 to 2
- cache_four: bfloat16 [128, 30720], P('row', ('section', 'col')), may hold values from -6 to 6
- gain_four: float32 [96], replicated, may hold values from 0.25 to 1.75
- weight_four: bfloat16 [27, 9216], replicated, may hold values from -0.125 to 0.125
- bias_four: float32 [96], replicated, may hold values from -2 to 2
Outputs:
- frame_out: bfloat16 [128, 61440], P('row', ('section', 'col'))
All inputs are finite; a program needn't handle non-finite values.
Results may differ from a plain program's by a relative error of at most 0.0085.
Values may be sent and summed in bfloat16 or wider, within the bound.
No kernel may reach another device: no remote copies, remote signals or barrier semaphores. Data moves between devices by JAX's collectives and lax.ppermute only.
A program may use at most 64 MiB of HBM per device.

v0:
```python
import jax
import jax.numpy as jnp
from jax import lax
from jax.experimental import pallas as pl
from jax.experimental.pallas import tpu as pltpu
from jax.sharding import PartitionSpec as P

EPSILON = 1e-06
BF16 = jnp.bfloat16
F32 = jnp.float32

ROWS = 16
COLS = 10
C3 = 192
C4 = 96
FRAMES = 4
WIDE = COLS + 4
MID = COLS + 2
CHUNKS = 4
EXT = 24
FINE = 2 * COLS + 2
FROWS = 2 * ROWS
FEXT = 40
XW = COLS * FRAMES * C3
PW = COLS * 2 * C3
QW = 2 * COLS * 2 * C4
COLX = FRAMES * C3
COLP = 2 * C3
COLQ = 2 * C4
QAT = 2 * COLX + 2 * COLP


def nt_dot(lhs, rhs):
    return lax.dot_general(lhs, rhs, (((1,), (1,)), ((), ())), preferred_element_type=F32)


def silu(value):
    half = 0.5 * value
    return half + half * jnp.tanh(half)


def lane_mask(rows, below):
    return lax.broadcasted_iota(jnp.int32, (rows, 128), 1) < below


def split_pair(v0, v1, v2):
    low = lane_mask(v0.shape[0], 64)
    r1 = pltpu.roll(v1, 64, 1)
    r2 = pltpu.roll(v2, 64, 1)
    zero = jnp.zeros_like(v1)
    return (v0, jnp.where(low, v1, zero)), (jnp.where(low, r1, r2), jnp.where(low, r2, zero))


def norm_pair(v0, v1, v2, gains):
    low = lane_mask(v0.shape[0], 64)
    sq1 = v1 * v1
    zero = jnp.zeros_like(v1)
    sum_a = jnp.sum(v0 * v0 + jnp.where(low, sq1, zero), axis=1, keepdims=True)
    sum_b = jnp.sum(v2 * v2 + jnp.where(low, zero, sq1), axis=1, keepdims=True)
    inv_a = lax.rsqrt(sum_a * (1.0 / C3) + EPSILON)
    inv_b = lax.rsqrt(sum_b * (1.0 / C3) + EPSILON)
    return (
        silu(v0 * inv_a * gains[0]),
        silu(v1 * jnp.where(low, inv_a, inv_b) * gains[1]),
        silu(v2 * inv_b * gains[2]),
    )


def weave(*streams):
    lists = []
    for stream in streams:
        lists.append(list(stream))
    order = []
    for place, steps in enumerate(lists):
        order += [((n + 0.5) / len(steps), place, step) for n, step in enumerate(steps)]
    for _, _, step in sorted(order, key=lambda entry: entry[:2]):
        step()


def up_slots():
    slots = {}
    count = 0
    for di in range(3):
        for dj in range(3):
            phases = [(a, b) for a in range(2) for b in range(2) if 0 <= di - a < 2 and 0 <= dj - b < 2]
            slots[di, dj] = (count, phases)
            count += len(phases)
    return slots


def main_kernel(
    x_ref, p_ref, q_ref, even_row, odd_row, even_col, odd_col,
    g3_ref, b3_ref, w3_ref, wu_ref, bu_ref, g4_ref, w4_ref, b4_ref,
    out_ref,
    raw0, raw1, raw2, act0, act1, act2, actd0, actd1, actd2, halo0, halo1, halo2,
    res0, res1, resd0, resd1, resh0, resh1, z0, z1, z2, s0, s1, fine0, fine1, fine2,
    *, row_count, col_count, col_size,
):
    raw, act, act_d, halo_d = (raw0, raw1, raw2), (act0, act1, act2), (actd0, actd1, actd2), (halo0, halo1, halo2)
    res, res_d, res_h = (res0, res1), (resd0, resd1), (resh0, resh1)
    z4, s4, act4_d = (z0, z1, z2), (s0, s1), (fine0, fine1, fine2)
    row = lax.axis_index("row")
    col = lax.axis_index("section") * col_size + lax.axis_index("col")
    row_odd = lax.rem(row, 2) == 1
    col_odd = lax.rem(col, 2) == 1
    first_row, last_row = row == 0, row == row_count - 1
    first_col, last_col = col == 0, col == col_count - 1

    def wide(value):
        return value.astype(F32)

    def pick(flag, one, other, *index):
        return wide(jnp.where(flag, one[index], other[index]))

    def above(lanes):
        return pick(row_odd, even_row, odd_row, slice(0, 2), lanes)

    def below(lanes):
        return pick(row_odd, odd_row, even_row, slice(0, 2), lanes)

    def left(lanes):
        return pick(col_odd, even_col, odd_col, slice(0, ROWS + 4), lanes)

    def right(lanes):
        return pick(col_odd, odd_col, even_col, slice(0, ROWS + 4), lanes)

    def keep(inside, value):
        return jnp.where(inside, value, jnp.zeros_like(value))

    def rounded(value):
        return value.astype(BF16).astype(F32)

    def pair_of(ref, *index):
        return jnp.concatenate([ref[(0,) + index], ref[(1,) + index]], axis=1).astype(BF16)

    g3 = g3_ref[...]
    gains = (
        g3[:, 0:128],
        jnp.concatenate([g3[:, 128:192], g3[:, 0:64]], axis=1),
        g3[:, 64:192],
    )

    def load_column(group, jj):
        base = jj * EXT
        for q in range(3):
            if 2 <= jj < WIDE - 2:
                at = (jj - 2) * COLX + (3 * (group - 1) + q) * 128
                if group == 0:
                    at = (jj - 2) * COLP + q * 128
                src, strip_at = (x_ref, at) if group else (p_ref, XW + at)
                strip = slice(strip_at, strip_at + 128)
                raw[group][q, base : base + 16, :] = wide(src[:, at : at + 128])
                raw[group][q, base + 16 : base + 18, :] = above(strip)
                raw[group][q, base + 18 : base + 20, :] = below(strip)
            else:
                side, lane = (left, jj) if jj < 2 else (right, jj - WIDE + 2)
                at = lane * COLX + (3 * (group - 1) + q) * 128
                if group == 0:
                    at = 2 * COLX + lane * COLP + q * 128
                raw[group][q, base : base + 20, :] = side(slice(at, at + 128))
        tiles = [raw[group][q, base : base + EXT, :] for q in range(3)]
        if group:
            tiles = norm_pair(*tiles, gains)
        for half, pair in enumerate(split_pair(*tiles)):
            at = (half * WIDE + jj) * EXT
            for q in range(2):
                act[group][q, at : at + 2, :] = pair[q][16:18]
                act[group][q, at + 2 : at + 18, :] = pair[q][0:16]
                act[group][q, at + 18 : at + 20, :] = pair[q][18:20]

    def shift_column(group, jj):
        for half in range(2):
            slab = half * WIDE + jj
            for dy in range(3):
                rows = slice(slab * EXT + 1 + dy, slab * EXT + 1 + dy + ROWS)
                act_d[group][dy, slab * ROWS : (slab + 1) * ROWS, :] = pair_of(act[group], rows, slice(None))

    def gather_rows(group, place):
        ext = (0, 1, 2, 17, 18, 19)[place]
        for half in range(2):
            rows = pl.ds(half * WIDE * EXT + ext, 16, stride=EXT)
            halo_d[group][place, half * 16 : (half + 1) * 16, :] = pair_of(act[group], rows, slice(None))

    def coarse_steps(group):
        for jj in range(WIDE):
            yield lambda jj=jj: (load_column(group, jj), shift_column(group, jj))
        for place in range(6):
            yield lambda place=place: gather_rows(group, place)

    mid = 2 * MID * ROWS
    center = [None, None]
    edges = [[None] * 3, [None] * 3]

    def conv_three(p, dy, dx, t):
        parts = []
        halos = []
        for k in range(2):
            group, half = p + (k + t) // 2, (k + t) % 2
            at = (half * WIDE + dx) * ROWS
            parts.append(act_d[group][dy, at : at + MID * ROWS, 0:C3])
            for side in range(2):
                halos.append(halo_d[group][3 * side + dy, half * 16 : (half + 1) * 16, 0:C3])
        kernel = w3_ref[9 * t + 3 * dy + dx, :, 0:C3]
        got = nt_dot(jnp.concatenate(parts + halos, axis=0), kernel)
        center[p] = got[:mid] if center[p] is None else center[p] + got[:mid]
        edges[p][dx] = got[mid:] if edges[p][dx] is None else edges[p][dx] + got[mid:]

    def conv_three_steps(p):
        for dy in range(3):
            for dx in range(3):
                for t in range(3):
                    yield lambda dy=dy, dx=dx, t=t: conv_three(p, dy, dx, t)

    b3 = b3_ref[...]
    column = lax.broadcasted_iota(jnp.int32, (MID, 1), 0)
    cols_in = jnp.logical_and(
        jnp.logical_or(column > 0, jnp.logical_not(first_col)),
        jnp.logical_or(column < MID - 1, jnp.logical_not(last_col)),
    )

    def put_res(p, rows, value):
        res[p][0, rows, :] = value[:, 0:128]
        res[p][1, rows, 0:64] = value[:, 128:192]

    def result_column(p, jm):
        at = (jm + 1) * EXT
        tiles = [raw[p + 1][q, at : at + ROWS, :] for q in range(3)]
        for k, skip in enumerate(split_pair(*tiles)):
            slab = k * MID + jm
            value = center[p][slab * ROWS : (slab + 1) * ROWS] + b3
            value = rounded(value + jnp.concatenate([skip[0], skip[1][:, 0:64]], axis=1))
            if jm == 0:
                value = keep(jnp.logical_not(first_col), value)
            if jm == MID - 1:
                value = keep(jnp.logical_not(last_col), value)
            put_res(p, pl.ds(slab * EXT + 1, ROWS), value)

    def result_rows(p, side):
        rows_in = jnp.logical_not(last_row if side else first_row)
        ext = 18 if side else 17
        tiles = [raw[p + 1][q, pl.ds(EXT + ext, MID, stride=EXT), :] for q in range(3)]
        for k, skip in enumerate(split_pair(*tiles)):
            at = (2 * k + side) * 16
            value = b3 + edges[p][0][at : at + MID] + edges[p][1][at + 1 : at + 1 + MID]
            value = value + edges[p][2][at + 2 : at + 2 + MID]
            value = rounded(value + jnp.concatenate([skip[0], skip[1][:, 0:64]], axis=1))
            value = keep(jnp.logical_and(cols_in, rows_in), value)
            put_res(p, pl.ds(k * MID * EXT + (17 if side else 0), MID, stride=EXT), value)

    def shift_result(p, jm):
        for k in range(2):
            slab = k * MID + jm
            for di in range(3):
                rows = slice(slab * EXT + di, slab * EXT + di + ROWS)
                res_d[p][di, slab * ROWS : (slab + 1) * ROWS, :] = pair_of(res[p], rows, slice(None))

    def gather_result(p, place):
        ext = (0, 1, 16, 17)[place]
        for k in range(2):
            rows = pl.ds(k * MID * EXT + ext, 16, stride=EXT)
            res_h[p][place, k * 16 : (k + 1) * 16, :] = pair_of(res[p], rows, slice(None))

    def result_steps(p):
        for side in range(2):
            yield lambda side=side: result_rows(p, side)
        for jm in range(MID):
            yield lambda jm=jm: (result_column(p, jm), shift_result(p, jm))
        for place in range(4):
            yield lambda place=place: gather_result(p, place)

    span = COLS + 1
    slots = up_slots()
    total = [{}, {}]
    rim = [{}, {}]

    def conv_up(p, di, dj):
        start, phases = slots[di, dj]
        low = min(dj - b for _, b in phases)
        wide_cols = span + max(dj - b for _, b in phases) - low
        sides = sorted({a for a, _ in phases})
        parts = []
        for k in range(2):
            at = (k * MID + low) * ROWS
            parts.append(res_d[p][di, at : at + wide_cols * ROWS, 0:C3])
        for a in sides:
            parts.append(res_h[p][(di - 1) if a else (2 + di), :, 0:C3])
        kernel = wu_ref[start * 128 : (start + len(phases)) * 128, 0:C3]
        got = nt_dot(jnp.concatenate(parts, axis=0), kernel)
        for n, (a, b) in enumerate(phases):
            lanes = slice(n * 128, (n + 1) * 128)
            for k in range(2):
                at = (k * wide_cols + dj - b - low) * ROWS
                value = got[at : at + span * ROWS, lanes]
                at = 2 * wide_cols * ROWS + sides.index(a) * 32 + k * 16 + dj - b
                edge = got[at : at + span, lanes]
                if (a, b, k) in total[p]:
                    value = value + total[p][a, b, k]
                    edge = edge + rim[p][a, b, k]
                total[p][a, b, k] = value
                rim[p][a, b, k] = edge

    def conv_up_steps(p):
        for di in range(3):
            for dj in range(3):
                yield lambda di=di, dj=dj: conv_up(p, di, dj)

    bias_up = jnp.concatenate([bu_ref[...], jnp.zeros((1, 32), F32)], axis=1)
    g4 = jnp.concatenate([g4_ref[...], jnp.zeros((1, 32), F32)], axis=1)

    def act_four(value):
        square = jnp.sum(value * value, axis=1, keepdims=True)
        return silu(value * lax.rsqrt(square * (1.0 / C4) + EPSILON) * g4)

    def fine_rows(p, a, b, k):
        value = act_four(rounded(rim[p][a, b, k] + bias_up))
        index = lax.broadcasted_iota(jnp.int32, (span, 1), 0)
        if b:
            inside = jnp.logical_or(index > 0, jnp.logical_not(first_col))
        else:
            inside = jnp.logical_or(index < span - 1, jnp.logical_not(last_col))
        value = keep(jnp.logical_and(inside, jnp.logical_not(first_row if a else last_row)), value)
        start = (0 if b else FEXT) + (0 if a else FROWS + 1)
        z4[p + 1][k, pl.ds(start, span, stride=2 * FEXT), :] = value

    def fine_column(p, b, j):
        fx = 2 * j if b else 2 * j + 1
        for k in range(2):
            for a in range(2):
                value = rounded(total[p][a, b, k][j * ROWS : (j + 1) * ROWS] + bias_up)
                if 1 <= fx <= 2 * COLS:
                    s4[p][k, pl.ds((fx - 1) * FROWS + a, ROWS, stride=2), :] = value
                value = act_four(value)
                if fx == 0:
                    value = keep(jnp.logical_not(first_col), value)
                if fx == FINE - 1:
                    value = keep(jnp.logical_not(last_col), value)
                z4[p + 1][k, pl.ds(fx * FEXT + 1 + a, ROWS, stride=2), :] = value
        shift_fine(p + 1, fx)

    def shift_fine(group, fx):
        for dy in range(3):
            rows = slice(fx * FEXT + dy, fx * FEXT + dy + FROWS)
            act4_d[group][dy, fx * FROWS : (fx + 1) * FROWS, :] = pair_of(z4[group], rows, slice(None))

    def fine_steps(p):
        for a in range(2):
            for b in range(2):
                for k in range(2):
                    yield lambda a=a, b=b, k=k: fine_rows(p, a, b, k)
        for j in range(span):
            for b in (1, 0):
                yield lambda b=b, j=j: fine_column(p, b, j)

    def put_cached(fx, row0, joined, first):
        rows = joined.shape[0]
        for t in range(2):
            at = first + t * C4
            value = jnp.concatenate([joined[:, at : at + C4], jnp.zeros((rows, 32), F32)], axis=1)
            z4[0][t, fx * FEXT + row0 : fx * FEXT + row0 + rows, :] = value

    def cached_column(fx):
        if 0 < fx < FINE - 1:
            at = (fx - 1) * COLQ
            start = at // 128 * 128
            first = at - start
            strip = slice(XW + PW + start, XW + PW + start + 256)
            put_cached(fx, 1, wide(q_ref[:, start : start + 256]), first)
            put_cached(fx, 0, above(strip)[1:2], first)
            put_cached(fx, FROWS + 1, below(strip)[0:1], first)
        else:
            lanes = (right if fx else left)(slice(QAT, QAT + 384))
            put_cached(fx, 0, lanes[17:18], 0)
            put_cached(fx, 1, lanes[0:16], 0)
            put_cached(fx, 1 + ROWS, lanes[0:16], COLQ)
            put_cached(fx, FROWS + 1, lanes[18:19], 0)
        shift_fine(0, fx)

    def cached_steps():
        for fx in range(FINE):
            yield lambda fx=fx: cached_column(fx)

    size = 2 * COLS * FROWS
    done = [None, None]

    def conv_four(p, dy, dx):
        at = dx * FROWS
        parts = [act4_d[group][dy, at : at + size, :] for group in (p, p + 1)]
        got = nt_dot(jnp.concatenate(parts, axis=1), w4_ref[3 * dy + dx])
        done[p] = got if done[p] is None else done[p] + got

    def conv_four_steps(p):
        for dy in range(3):
            for dx in range(3):
                yield lambda dy=dy, dx=dx: conv_four(p, dy, dx)

    b4 = b4_ref[...]
    bias_four = jnp.concatenate([b4, b4], axis=1)
    first = lane_mask(FROWS, C4)

    def out_column(p, fx):
        rows = slice(fx * FROWS, (fx + 1) * FROWS)
        other = pltpu.roll(s4[p][1, rows, :], C4, 1)
        skip = jnp.concatenate([jnp.where(first, s4[p][0, rows, :], other), other[:, 0:64]], axis=1)
        value = (done[p][rows] + bias_four + skip).astype(BF16)
        out_ref[:, fx * 384 + p * 192 : fx * 384 + (p + 1) * 192] = value

    def out_steps(p):
        for fx in range(2 * COLS):
            yield lambda fx=fx: out_column(p, fx)

    weave(coarse_steps(0), coarse_steps(1))
    weave(conv_three_steps(0), coarse_steps(2), cached_steps())
    later = list(conv_three_steps(1))
    weave(later[:13], result_steps(0))
    weave(conv_up_steps(0))
    weave(later[13:], fine_steps(0))
    later = list(conv_four_steps(0))
    weave(later[:4], result_steps(1))
    weave(conv_up_steps(1))
    weave(later[4:], fine_steps(1))
    weave(conv_four_steps(1), out_steps(0))
    weave(out_steps(1))


def prep_three_kernel(source_ref, out_ref, flat_ref, parts, mixed, sems):
    low = lane_mask(C3 // 2, 64)
    zero = jnp.zeros((C3 // 2, 128), F32)
    size = source_ref.shape[1] // CHUNKS
    copies = []
    for chunk in range(CHUNKS):
        lanes = pl.ds(chunk * size, size)
        copies.append(
            pltpu.make_async_copy(source_ref.at[:, lanes], flat_ref.at[:, lanes], sems.at[chunk])
        )
        copies[-1].start()
    for pair in range(C3 // 2):
        if pair % (C3 // 2 // CHUNKS) == 0:
            copies[pair // (C3 // 2 // CHUNKS)].wait()
        for q in range(3):
            at = (3 * pair + q) * 128
            parts[q, pair * 32 : pair * 32 + 27, :] = flat_ref[:, at : at + 128].astype(F32)
    for tap in range(27):
        v0, v1, v2 = [parts[q, pl.ds(tap, C3 // 2, stride=32), :] for q in range(3)]
        r1, r2 = pltpu.roll(v1, 64, 1), pltpu.roll(v2, 64, 1)
        slot = tap % 2
        mixed[slot, 0, pl.ds(0, C3 // 2, stride=2), :] = v0
        mixed[slot, 1, pl.ds(0, C3 // 2, stride=2), :] = jnp.where(low, v1, zero)
        mixed[slot, 0, pl.ds(1, C3 // 2, stride=2), :] = jnp.where(low, r1, r2)
        mixed[slot, 1, pl.ds(1, C3 // 2, stride=2), :] = jnp.where(low, r2, zero)
        both = jnp.concatenate([mixed[slot, 0], mixed[slot, 1]], axis=1)
        out_ref[tap] = both.astype(BF16)


def prep_four_kernel(up_ref, four_ref, up_out, four_out, parts_u, mixed_u, parts_f, mixed_f):
    half = C4 // 2
    low = lane_mask(half, 64)
    zero = jnp.zeros((half, 128), F32)
    for pair in range(half):
        for q in range(3):
            at = (3 * pair + q) * 128
            parts_u[q, pair * 16 : pair * 16 + 9, :] = up_ref[:, at : at + 128].astype(F32)
    for tap in range(9):
        v0, v1, v2 = [parts_u[q, pl.ds(tap, half, stride=16), :] for q in range(3)]
        r1, r2 = pltpu.roll(v1, 64, 1), pltpu.roll(v2, 64, 1)
        mixed_u[tap, 0, pl.ds(0, half, stride=2), :] = v0
        mixed_u[tap, 1, pl.ds(0, half, stride=2), :] = jnp.where(low, v1, zero)
        mixed_u[tap, 0, pl.ds(1, half, stride=2), :] = jnp.where(low, r1, r2)
        mixed_u[tap, 1, pl.ds(1, half, stride=2), :] = jnp.where(low, r2, zero)
    spans = {(0, 0): (0,), (0, 1): (1, 2), (1, 0): (0, 1), (1, 1): (2,)}
    rest = jnp.zeros((32, 256), BF16)
    for (di, dj), (start, phases) in up_slots().items():
        for n, (a, b) in enumerate(phases):
            tiles = []
            for q in range(2):
                total = None
                for dy in spans[a, di - a]:
                    for dx in spans[b, dj - b]:
                        one = mixed_u[3 * dy + dx, q]
                        total = one if total is None else total + one
                tiles.append(total)
            at = (start + n) * 128
            up_out[at : at + C4, :] = jnp.concatenate(tiles, axis=1).astype(BF16)
            up_out[at + C4 : at + 128, :] = rest
    quarter = C4 // 4
    lane = lax.broadcasted_iota(jnp.int32, (quarter, 128), 1)
    empty = jnp.zeros((quarter, 128), F32)
    for four in range(quarter):
        for q in range(3):
            at = (3 * four + q) * 128
            parts_f[q, four * 32 : four * 32 + 27, :] = four_ref[:, at : at + 128].astype(F32)
    none = jnp.zeros((C4, 128), BF16)
    for place in range(9):
        four_out[place, 0:C4, 384:512] = none
        four_out[place, C4 : 2 * C4, 0:128] = none
        for t in range(3):
            rows = pl.ds(9 * t + place, quarter, stride=32)
            v0, v1, v2 = [parts_f[q, rows, :] for q in range(3)]
            second = jnp.where(lane < 32, pltpu.roll(v0, 32, 1), pltpu.roll(v1, 32, 1))
            third = jnp.where(lane < 64, pltpu.roll(v1, 64, 1), pltpu.roll(v2, 64, 1))
            slot = t % 2
            for m, value in enumerate((v0, second, third, pltpu.roll(v2, 96, 1))):
                rows = pl.ds(m, quarter, stride=4)
                mixed_f[slot, rows, :] = jnp.where(lane < C4, value, empty)
            kernel = mixed_f[slot].astype(BF16)
            four_out[place, 0:C4, t * 128 : (t + 1) * 128] = kernel
            four_out[place, C4 : 2 * C4, (t + 1) * 128 : (t + 2) * 128] = kernel


def row_strips(refs, low_flag, out_ref):
    at = 0
    for ref in refs:
        rows, width = ref.shape
        out_ref[:, at : at + width] = jnp.where(low_flag, ref[0:2, :], ref[rows - 2 : rows, :])
        at += width


def row_strips_kernel(x_ref, p_ref, q_ref, even_ref, odd_ref, x_own, p_own, q_own, sems):
    own = (x_own, p_own, q_own)
    copies = [
        pltpu.make_async_copy(source, target, sems.at[n])
        for n, (source, target) in enumerate(zip((x_ref, p_ref, q_ref), own))
    ]
    for copy in copies:
        copy.start()
    for copy in copies:
        copy.wait()
    row_odd = lax.rem(lax.axis_index("row"), 2) == 1
    row_strips(own, row_odd, even_ref)
    row_strips(own, jnp.logical_not(row_odd), odd_ref)


def col_strips_kernel(x_ref, p_ref, q_ref, even_row, odd_row, _, out_ref, *, col_size, parity):
    row_odd = lax.rem(lax.axis_index("row"), 2) == 1
    col = lax.axis_index("section") * col_size + lax.axis_index("col")
    take_low = lax.rem(col, 2) == parity
    strips = (
        jnp.where(row_odd, even_row[...], odd_row[...]),
        jnp.where(row_odd, odd_row[...], even_row[...]),
    )

    def put(rows, at, low, high):
        out_ref[rows, at : at + low.shape[1]] = jnp.where(take_low, low, high)

    start = 0
    for ref, at, width, lanes in (
        (x_ref, 0, XW, 2 * COLX), (p_ref, 2 * COLX, PW, 2 * COLP), (q_ref, QAT, QW, COLQ)
    ):
        high = width - lanes
        if ref is q_ref:
            for half in range(2):
                rows = slice(half * ROWS, (half + 1) * ROWS)
                put(slice(0, ROWS), at + half * lanes, ref[rows, 0:lanes], ref[rows, high:width])
        else:
            put(slice(0, ROWS), at, ref[:, 0:lanes], ref[:, high:width])
        for place, strip in enumerate(strips):
            rows = slice(ROWS + 2 * place, ROWS + 2 * place + 2)
            put(rows, at, strip[:, start : start + lanes], strip[:, start + high : start + width])
            if ref is q_ref:
                out_ref[rows, at + lanes : at + 2 * lanes] = jnp.zeros((2, lanes), BF16)
        start += width


def call(kernel, operands, outputs, scratch, megabytes, moved=0, unread=0, space=pl.ANY):
    cost = pl.CostEstimate(flops=moved, bytes_accessed=moved, transcendentals=0) if moved else None
    vmem = pl.BlockSpec(memory_space=pltpu.VMEM)
    shapes = [jax.ShapeDtypeStruct(shape, BF16) for shape in outputs]
    got = pl.pallas_call(
        kernel,
        out_shape=shapes,
        in_specs=[vmem] * (len(operands) - unread) + [pl.BlockSpec(memory_space=space)] * unread,
        out_specs=[vmem] * len(outputs),
        scratch_shapes=scratch,
        cost_estimate=cost,
        compiler_params=pltpu.CompilerParams(vmem_limit_bytes=megabytes * 1024 * 1024),
    )(*operands)
    return got[0] if len(outputs) == 1 else got


def swap_pairs(count, start):
    out = []
    for low in range(start, count - 1, 2):
        out += [(low, low + 1), (low + 1, low)]
    return out


def shards(
    section_input,
    cache_three,
    gain_three,
    bias_three,
    weight_three,
    weight_up,
    bias_up,
    cache_four,
    gain_four,
    weight_four,
    bias_four,
):
    row_count = lax.axis_size("row")
    col_size = lax.axis_size("col")
    col_count = lax.axis_size("section") * col_size
    tile = (section_input, cache_three, cache_four)

    row_strip = (2, XW + PW + QW)
    own = [pltpu.VMEM(block.shape, BF16) for block in tile]
    even_strip, odd_strip = call(
        row_strips_kernel,
        tile,
        [row_strip] * 2,
        [*own, pltpu.SemaphoreType.DMA((3,))],
        62, unread=3, space=pltpu.HBM,
    )
    even_row = lax.ppermute(even_strip, "row", swap_pairs(row_count, 0))
    odd_row = lax.ppermute(odd_strip, "row", swap_pairs(row_count, 1))

    w3 = call(
        prep_three_kernel,
        (weight_three,),
        [(27, C3, 256)],
        [
            pltpu.VMEM(weight_three.shape, BF16),
            pltpu.VMEM((3, 32 * C3 // 2, 128), F32),
            pltpu.VMEM((2, 2, C3, 128), F32),
            pltpu.SemaphoreType.DMA((CHUNKS,)),
        ],
        16, 8_000_000, unread=1, space=pltpu.HBM,
    )
    wu, w4 = call(
        prep_four_kernel,
        (weight_up, weight_four),
        [(16 * 128, 256), (9, 2 * C4, 512)],
        [
            pltpu.VMEM((3, 16 * C4 // 2, 128), F32),
            pltpu.VMEM((9, 2, C4, 128), F32),
            pltpu.VMEM((3, 32 * C4 // 4, 128), F32),
            pltpu.VMEM((2, C4, 128), F32),
        ],
        16, 8_000_000,
    )

    col_strip = (ROWS + 4, QAT + 2 * COLQ)

    def swap_columns(parity):
        def col_kernel(*refs):
            col_strips_kernel(*refs, col_size=col_size, parity=1 - parity)

        strip = call(col_kernel, (*tile, even_row, odd_row, w3), [col_strip], [], 4, unread=1)
        return lax.ppermute(strip, ("section", "col"), swap_pairs(col_count, parity))

    even_col = swap_columns(0)
    odd_col = swap_columns(1)

    def kernel(*refs):
        main_kernel(*refs, row_count=row_count, col_count=col_count, col_size=col_size)

    operands = (
        *tile, even_row, odd_row, even_col, odd_col,
        gain_three.reshape(1, C3), bias_three.reshape(1, C3), w3, wu, bias_up.reshape(1, C4),
        gain_four.reshape(1, C4), w4, bias_four.reshape(1, C4),
    )
    scratch = [pltpu.VMEM((3, 16 * EXT, 128), F32)] * 3
    scratch += [pltpu.VMEM((2, (2 * WIDE + 2) * EXT, 128), F32)] * 3
    scratch += [pltpu.VMEM((3, 2 * WIDE * ROWS, 256), BF16)] * 3
    scratch += [pltpu.VMEM((6, 2 * 16, 256), BF16)] * 3
    scratch += [pltpu.VMEM((2, (2 * MID + 4) * EXT, 128), F32)] * 2
    scratch += [pltpu.VMEM((3, 2 * MID * ROWS, 256), BF16)] * 2
    scratch += [pltpu.VMEM((4, 2 * 16, 256), BF16)] * 2
    scratch += [pltpu.VMEM((2, FINE * FEXT, 128), F32)] * 3
    scratch += [pltpu.VMEM((2, 2 * COLS * FROWS, 128), F32)] * 2
    scratch += [pltpu.VMEM((3, FINE * FROWS, 256), BF16)] * 3
    return call(kernel, operands, [(FROWS, 2 * COLS * FRAMES * C4)], scratch, 32)


def solution(mesh):
    tiled = P("row", ("section", "col"))
    return jax.shard_map(
        shards,
        mesh=mesh,
        in_specs=(tiled, tiled, P(), P(), P(), P(), P(), tiled, P(), P(), P()),
        out_specs=tiled,
        check_vma=False,
    )
```

profile of v0, /device:TPU:18, one launch (start us, length us, event | category | flops | bytes accessed | tf_op | source)
XLA Modules:
  0.0 33.7 jit_solution(6199103228740554039)
XLA Ops:
  0.0 1.8 %shard_map.109 = (bf16[2,15360]{1,0:T(2,128)(2,1)}, bf16[2,15360]{1,0:T(2,128)(2,1)}) custom-call(bf16[16,7680]{1,0:T(8,128)(2,1)} %refs_0_.5, bf16[16,3840]{1,0:T(8,128)(2,1)} %refs_1_.5, bf16[32,3840]{1,0:T(8,128)(2,1)} %refs_2_.5), custom_call_target="tpu_custom_call" | custom-call | tf_op jit(solution)/shard_map/pallas_call | solution.py:567
  1.9 0.6 %collective-permute-start = (bf16[2,15360]{1,0:T(2,128)(2,1)}, bf16[2,15360]{1,0:T(2,128)(2,1)S(1)}, u32[]{:S(2)}, u32[]{:S(2)}) collective-permute-start(bf16[2,15360]{1,0:T(2,128)(2,1)} %get-tuple-element.9), channel_id=1, source_target_pairs={{0,4},{4,0},{8,12},{12,8},{1,5},{5,1},{9,13},{13,9},{2,6},{6,2},{1... | collective-permute-start | bytes 184328 | tf_op jit(solution)/shard_map/ppermute | solution.py:613
  2.5 0.0 copy-start
  2.5 0.0 copy-start.1
  2.5 4.5 %collective-permute-start.1 = (bf16[2,15360]{1,0:T(2,128)(2,1)}, bf16[2,15360]{1,0:T(2,128)(2,1)S(1)}, u32[]{:S(2)}, u32[]{:S(2)}) collective-permute-start(bf16[2,15360]{1,0:T(2,128)(2,1)} %get-tuple-element.10), channel_id=1, source_target_pairs={{4,8},{8,4},{5,9},{9,5},{6,10},{10,6},{7,11},{11,7},{20,24},{24,20... | collective-permute-start | bytes 184328 | tf_op jit(solution)/shard_map/ppermute | solution.py:614
  6.9 0.0 copy-start.2
  7.0 1.7 %copy-done.2 = bf16[27,36864]{1,0:T(8,128)(2,1)S(1)} copy-done((bf16[27,36864]{1,0:T(8,128)(2,1)S(1)}, bf16[27,36864]{1,0:T(8,128)(2,1)}, u32[]{:S(2)}) %copy-start.2) | copy-done | bytes 1990680
  8.6 0.0 copy-start.3
  8.6 3.8 %shard_map.110.refs_5_.refs_9_ = bf16[27,192,256]{2,1,0:T(8,128)(2,1)S(1)} custom-call(bf16[27,36864]{1,0:T(8,128)(2,1)S(1)} %copy-done.2), custom_call_target="tpu_custom_call" | custom-call | flops 8000000 | bytes 8000000 | tf_op jit(solution)/shard_map/pallas_call | solution.py:567
  12.4 0.0 collective-permute-done.refs_3_
  12.5 0.0 collective-permute-done.1.refs_4_
  12.5 0.0 copy-done
  12.5 0.0 copy-done.1
  12.5 0.0 copy-done.3
  12.5 0.1 shard_map.111
  12.6 0.0 copy-start.4
  12.6 0.0 copy-start.5
  12.6 0.0 copy-start.6
  12.7 0.0 copy-start.7
  12.7 0.0 copy-start.8
  12.7 0.0 copy-start.9
  12.7 0.0 copy-start.10
  12.7 1.6 %collective-permute-start.2 = (bf16[20,2688]{1,0:T(8,128)(2,1)S(1)}, bf16[20,2688]{1,0:T(8,128)(2,1)S(1)}, u32[]{:S(2)}, u32[]{:S(2)}) collective-permute-start(bf16[20,2688]{1,0:T(8,128)(2,1)S(1)} %shard_map.111), channel_id=1, source_target_pairs={{0,1},{1,0},{2,3},{3,2},{16,17},{17,16},{18,19},{19,18},{4,5},{5,4... | collective-permute-start | bytes 322568 | tf_op jit(solution)/shard_map/ppermute | solution.py:648
  14.3 0.1 shard_map.112
  14.5 2.1 %collective-permute-start.3 = (bf16[20,2688]{1,0:T(8,128)(2,1)S(1)}, bf16[20,2688]{1,0:T(8,128)(2,1)S(1)}, u32[]{:S(2)}, u32[]{:S(2)}) collective-permute-start(bf16[20,2688]{1,0:T(8,128)(2,1)S(1)} %shard_map.112), channel_id=1, source_target_pairs={{1,2},{2,1},{3,16},{16,3},{17,18},{18,17},{5,6},{6,5},{7,20},{20,7... | collective-permute-start | bytes 322568 | tf_op jit(solution)/shard_map/ppermute | solution.py:648
  16.6 0.0 copy-done.4
  16.6 0.0 copy-done.5
  16.6 1.6 %shard_map.113 = (bf16[2048,256]{1,0:T(8,128)(2,1)S(1)}, bf16[9,192,512]{2,1,0:T(8,128)(2,1)S(1)}) custom-call(bf16[9,18432]{1,0:T(8,128)(2,1)S(1)} %copy-done.4, bf16[27,9216]{1,0:T(8,128)(2,1)S(1)} %copy-done.5), custom_call_target="tpu_custom_call" | custom-call | flops 8000000 | bytes 8000000 | tf_op jit(solution)/shard_map/pallas_call | solution.py:567
  18.2 0.0 collective-permute-done.2.refs_5_
  18.2 4.5 %collective-permute-done.3.refs_6_ = bf16[20,2688]{1,0:T(8,128)(2,1)S(1)} collective-permute-done((bf16[20,2688]{1,0:T(8,128)(2,1)S(1)}, bf16[20,2688]{1,0:T(8,128)(2,1)S(1)}, u32[]{:S(2)}, u32[]{:S(2)}) %collective-permute-start.3) | collective-permute-done | bytes 107552 | tf_op jit(solution)/shard_map/ppermute | solution.py:648
  22.7 0.0 copy-done.6
  22.7 0.0 copy-done.7
  22.7 0.0 copy-done.8
  22.7 0.0 copy-done.9
  22.7 0.0 copy-done.10
  22.7 11.0 %shard_map.114 = bf16[32,7680]{1,0:T(8,128)(2,1)} custom-call(bf16[16,7680]{1,0:T(8,128)(2,1)S(1)} %copy-done, bf16[16,3840]{1,0:T(8,128)(2,1)S(1)} %copy-done.3, bf16[32,3840]{1,0:T(8,128)(2,1)S(1)} %copy-done.1, bf16[2,15360]{1,0:T(2,128)(2,1)S(1)} %collective-permute-done.refs_3_, bf16[2,15360]{1,0:T(2,128)(2,1)S(1)} %collective-permute-done.1.refs_4_, ...), custom_call_target="tpu_custom_call" | custom-call | tf_op jit(solution)/shard_map/pallas_call | solution.py:567
Async XLA Ops:
  1.9 10.6 %collective-permute-start = (bf16[2,15360]{1,0:T(2,128)(2,1)}, bf16[2,15360]{1,0:T(2,128)(2,1)S(1)}, u32[]{:S(2)}, u32[]{:S(2)}) collective-permute-start(bf16[2,15360]{1,0:T(2,128)(2,1)} %get-tuple-element.9), channel_id=1, source_target_pairs={{0,4},{4,0},{8,12},{12,8},{1,5},{5,1},{9,13},{13,9},{2,6},{6,2},{1... | collective-permute-start | bytes 184328 | tf_op jit(solution)/shard_map/ppermute | solution.py:613
  2.5 10.0 %copy-start = (bf16[16,7680]{1,0:T(8,128)(2,1)S(1)}, bf16[16,7680]{1,0:T(8,128)(2,1)}, u32[]{:S(2)}) copy-start(bf16[16,7680]{1,0:T(8,128)(2,1)} %refs_0_.5) | copy-start | bytes 737284
  2.5 10.0 %copy-start.1 = (bf16[32,3840]{1,0:T(8,128)(2,1)S(1)}, bf16[32,3840]{1,0:T(8,128)(2,1)}, u32[]{:S(2)}) copy-start(bf16[32,3840]{1,0:T(8,128)(2,1)} %refs_2_.5) | copy-start | bytes 737284
  2.5 10.0 %collective-permute-start.1 = (bf16[2,15360]{1,0:T(2,128)(2,1)}, bf16[2,15360]{1,0:T(2,128)(2,1)S(1)}, u32[]{:S(2)}, u32[]{:S(2)}) collective-permute-start(bf16[2,15360]{1,0:T(2,128)(2,1)} %get-tuple-element.10), channel_id=1, source_target_pairs={{4,8},{8,4},{5,9},{9,5},{6,10},{10,6},{7,11},{11,7},{20,24},{24,20... | collective-permute-start | bytes 184328 | tf_op jit(solution)/shard_map/ppermute | solution.py:614
  6.9 1.7 %copy-start.2 = (bf16[27,36864]{1,0:T(8,128)(2,1)S(1)}, bf16[27,36864]{1,0:T(8,128)(2,1)}, u32[]{:S(2)}) copy-start(bf16[27,36864]{1,0:T(8,128)(2,1)} %source_ref.1) | copy-start | bytes 5971972
  8.6 3.9 %copy-start.3 = (bf16[16,3840]{1,0:T(8,128)(2,1)S(1)}, bf16[16,3840]{1,0:T(8,128)(2,1)}, u32[]{:S(2)}) copy-start(bf16[16,3840]{1,0:T(8,128)(2,1)} %refs_1_.5) | copy-start | bytes 368644
  12.6 3.9 %copy-start.4 = (bf16[9,18432]{1,0:T(8,128)(2,1)S(1)}, bf16[9,18432]{1,0:T(8,128)(2,1)}, u32[]{:S(2)}) copy-start(bf16[9,18432]{1,0:T(8,128)(2,1)} %up_ref.1) | copy-start | bytes 995332
  12.6 4.0 %copy-start.5 = (bf16[27,9216]{1,0:T(8,128)(2,1)S(1)}, bf16[27,9216]{1,0:T(8,128)(2,1)}, u32[]{:S(2)}) copy-start(bf16[27,9216]{1,0:T(8,128)(2,1)} %four_ref.1) | copy-start | bytes 1492996
  12.6 10.1 %copy-start.6 = (f32[192]{0:T(256)S(1)}, f32[192]{0:T(256)}, u32[]{:S(2)}) copy-start(f32[192]{0:T(256)} %param.13) | copy-start | bytes 2308
  12.7 10.1 %copy-start.7 = (f32[192]{0:T(256)S(1)}, f32[192]{0:T(256)}, u32[]{:S(2)}) copy-start(f32[192]{0:T(256)} %param.14) | copy-start | bytes 2308
  12.7 10.0 %copy-start.8 = (f32[96]{0:T(128)S(1)}, f32[96]{0:T(128)}, u32[]{:S(2)}) copy-start(f32[96]{0:T(128)} %param.17) | copy-start | bytes 1156
  12.7 10.0 %copy-start.9 = (f32[96]{0:T(128)S(1)}, f32[96]{0:T(128)}, u32[]{:S(2)}) copy-start(f32[96]{0:T(128)} %param.19) | copy-start | bytes 1156
  12.7 10.0 %copy-start.10 = (f32[96]{0:T(128)S(1)}, f32[96]{0:T(128)}, u32[]{:S(2)}) copy-start(f32[96]{0:T(128)} %param.21) | copy-start | bytes 1156
  12.7 5.5 %collective-permute-start.2 = (bf16[20,2688]{1,0:T(8,128)(2,1)S(1)}, bf16[20,2688]{1,0:T(8,128)(2,1)S(1)}, u32[]{:S(2)}, u32[]{:S(2)}) collective-permute-start(bf16[20,2688]{1,0:T(8,128)(2,1)S(1)} %shard_map.111), channel_id=1, source_target_pairs={{0,1},{1,0},{2,3},{3,2},{16,17},{17,16},{18,19},{19,18},{4,5},{5,4... | collective-permute-start | bytes 322568 | tf_op jit(solution)/shard_map/ppermute | solution.py:648
  14.5 8.2 %collective-permute-start.3 = (bf16[20,2688]{1,0:T(8,128)(2,1)S(1)}, bf16[20,2688]{1,0:T(8,128)(2,1)S(1)}, u32[]{:S(2)}, u32[]{:S(2)}) collective-permute-start(bf16[20,2688]{1,0:T(8,128)(2,1)S(1)} %shard_map.112), channel_id=1, source_target_pairs={{1,2},{2,1},{3,16},{16,3},{17,18},{18,17},{5,6},{6,5},{7,20},{20,7... | collective-permute-start | bytes 322568 | tf_op jit(solution)/shard_map/ppermute | solution.py:648
where the time goes:
time: 33.9 us; the launch traced here: 33.7 us
  Pallas kernels  18.6 us (55%)
  starting transfers between devices  8.81 us (26%)
  waiting for transfers between devices  4.49 us (13%)
  local copies, waits for them, and re-layouts  1.71 us (5%)
    pallas_call x6, Pallas kernels, call(): pl.pallas_call(kernel, out_shape=shapes, in_specs=[vmem] * (len(operands)...  18.6 us
    ppermute x2, waiting for transfers between devices, swap_columns(): lax.ppermute(strip, ('section', 'col'), swap_pairs(col_count, parity))  4.48 us
    ppermute x1, starting transfers between devices, shards(): odd_row = lax.ppermute(odd_strip, 'row', swap_pairs(row_count, 1))  4.47 us
    ppermute x2, starting transfers between devices, swap_columns(): lax.ppermute(strip, ('section', 'col'), swap_pairs(col_count, parity))  3.73 us
    unnamed x22, local copies, waits for them, and re-layouts  1.71 us
  transfers between devices with their start and end apart: 4, of which 1 were waited for; matrix products, arithmetic and copies ran while one was open for 0% of the time, Pallas kernels for 16%

commit v1 on v0

--- a/solution.py
+++ b/solution.py
@@ -16,7 +16,6 @@
 FRAMES = 4
 WIDE = COLS + 4
 MID = COLS + 2
-CHUNKS = 4
 EXT = 24
 FINE = 2 * COLS + 2
 FROWS = 2 * ROWS
@@ -89,7 +88,7 @@
 
 
 def main_kernel(
-    x_ref, p_ref, q_ref, even_row, odd_row, even_col, odd_col,
+    x_ref, p_ref, q_ref, odd_row, even_row, even_col, odd_col,
     g3_ref, b3_ref, w3_ref, wu_ref, bu_ref, g4_ref, w4_ref, b4_ref,
     out_ref,
     raw0, raw1, raw2, act0, act1, act2, actd0, actd1, actd2, halo0, halo1, halo2,
@@ -422,50 +421,32 @@
     weave(out_steps(1))
 
 
-def prep_three_kernel(source_ref, out_ref, flat_ref, parts, mixed, sems):
-    low = lane_mask(C3 // 2, 64)
-    zero = jnp.zeros((C3 // 2, 128), F32)
-    size = source_ref.shape[1] // CHUNKS
-    copies = []
-    for chunk in range(CHUNKS):
-        lanes = pl.ds(chunk * size, size)
-        copies.append(
-            pltpu.make_async_copy(source_ref.at[:, lanes], flat_ref.at[:, lanes], sems.at[chunk])
-        )
-        copies[-1].start()
-    for pair in range(C3 // 2):
-        if pair % (C3 // 2 // CHUNKS) == 0:
-            copies[pair // (C3 // 2 // CHUNKS)].wait()
-        for q in range(3):
-            at = (3 * pair + q) * 128
-            parts[q, pair * 32 : pair * 32 + 27, :] = flat_ref[:, at : at + 128].astype(F32)
+def split_pairs(flat_ref, parts, pairs, taps, stride):
+    low = lane_mask(taps, 64)
+    zero = jnp.zeros((taps, 128), F32)
+    for pair in pairs:
+        v0, v1, v2 = [flat_ref[:, (3 * pair + q) * 128 : (3 * pair + q + 1) * 128].astype(F32) for q in range(3)]
+        r1, r2 = pltpu.roll(v1, 64, 1), pltpu.roll(v2, 64, 1)
+        at = 2 * pair * stride
+        parts[0, at : at + taps, :] = v0
+        parts[1, at : at + taps, :] = jnp.where(low, v1, zero)
+        parts[0, at + stride : at + stride + taps, :] = jnp.where(low, r1, r2)
+        parts[1, at + stride : at + stride + taps, :] = jnp.where(low, r2, zero)
+
+
+def prep_three_kernel(flat_ref, out_ref, parts):
+    split_pairs(flat_ref, parts, range(C3 // 2), 27, 40)
     for tap in range(27):
-        v0, v1, v2 = [parts[q, pl.ds(tap, C3 // 2, stride=32), :] for q in range(3)]
-        r1, r2 = pltpu.roll(v1, 64, 1), pltpu.roll(v2, 64, 1)
-        slot = tap % 2
-        mixed[slot, 0, pl.ds(0, C3 // 2, stride=2), :] = v0
-        mixed[slot, 1, pl.ds(0, C3 // 2, stride=2), :] = jnp.where(low, v1, zero)
-        mixed[slot, 0, pl.ds(1, C3 // 2, stride=2), :] = jnp.where(low, r1, r2)
-        mixed[slot, 1, pl.ds(1, C3 // 2, stride=2), :] = jnp.where(low, r2, zero)
-        both = jnp.concatenate([mixed[slot, 0], mixed[slot, 1]], axis=1)
-        out_ref[tap] = both.astype(BF16)
-
-
-def prep_four_kernel(up_ref, four_ref, up_out, four_out, parts_u, mixed_u, parts_f, mixed_f):
-    half = C4 // 2
-    low = lane_mask(half, 64)
-    zero = jnp.zeros((half, 128), F32)
-    for pair in range(half):
-        for q in range(3):
-            at = (3 * pair + q) * 128
-            parts_u[q, pair * 16 : pair * 16 + 9, :] = up_ref[:, at : at + 128].astype(F32)
+        both = [parts[q, pl.ds(tap, C3, stride=40), :] for q in range(2)]
+        out_ref[tap] = jnp.concatenate(both, axis=1).astype(BF16)
+
+
+def prep_four_kernel(up_ref, four_ref, up_out, four_out, parts_u, parts_f):
+    split_pairs(up_ref, parts_u, range(C4 // 2), 9, 24)
+    taps = {}
     for tap in range(9):
-        v0, v1, v2 = [parts_u[q, pl.ds(tap, half, stride=16), :] for q in range(3)]
-        r1, r2 = pltpu.roll(v1, 64, 1), pltpu.roll(v2, 64, 1)
-        mixed_u[tap, 0, pl.ds(0, half, stride=2), :] = v0
-        mixed_u[tap, 1, pl.ds(0, half, stride=2), :] = jnp.where(low, v1, zero)
-        mixed_u[tap, 0, pl.ds(1, half, stride=2), :] = jnp.where(low, r1, r2)
-        mixed_u[tap, 1, pl.ds(1, half, stride=2), :] = jnp.where(low, r2, zero)
+        for q in range(2):
+            taps[tap, q] = parts_u[q, pl.ds(tap, C4, stride=24), :]
     spans = {(0, 0): (0,), (0, 1): (1, 2), (1, 0): (0, 1), (1, 1): (2,)}
     rest = jnp.zeros((32, 256), BF16)
     for (di, dj), (start, phases) in up_slots().items():
@@ -475,33 +456,28 @@
                 total = None
                 for dy in spans[a, di - a]:
                     for dx in spans[b, dj - b]:
-                        one = mixed_u[3 * dy + dx, q]
+                        one = taps[3 * dy + dx, q]
                         total = one if total is None else total + one
                 tiles.append(total)
             at = (start + n) * 128
             up_out[at : at + C4, :] = jnp.concatenate(tiles, axis=1).astype(BF16)
             up_out[at + C4 : at + 128, :] = rest
-    quarter = C4 // 4
-    lane = lax.broadcasted_iota(jnp.int32, (quarter, 128), 1)
-    empty = jnp.zeros((quarter, 128), F32)
-    for four in range(quarter):
-        for q in range(3):
-            at = (3 * four + q) * 128
-            parts_f[q, four * 32 : four * 32 + 27, :] = four_ref[:, at : at + 128].astype(F32)
+    lane = lax.broadcasted_iota(jnp.int32, (27, 128), 1)
+    empty = jnp.zeros((27, 128), F32)
+    for four in range(C4 // 4):
+        at = 3 * four * 128
+        v0, v1, v2 = [four_ref[:, at + q * 128 : at + (q + 1) * 128].astype(F32) for q in range(3)]
+        second = jnp.where(lane < 32, pltpu.roll(v0, 32, 1), pltpu.roll(v1, 32, 1))
+        third = jnp.where(lane < 64, pltpu.roll(v1, 64, 1), pltpu.roll(v2, 64, 1))
+        for m, value in enumerate((v0, second, third, pltpu.roll(v2, 96, 1))):
+            at = (4 * four + m) * 40
+            parts_f[at : at + 27, :] = jnp.where(lane < C4, value, empty)
     none = jnp.zeros((C4, 128), BF16)
     for place in range(9):
         four_out[place, 0:C4, 384:512] = none
         four_out[place, C4 : 2 * C4, 0:128] = none
         for t in range(3):
-            rows = pl.ds(9 * t + place, quarter, stride=32)
-            v0, v1, v2 = [parts_f[q, rows, :] for q in range(3)]
-            second = jnp.where(lane < 32, pltpu.roll(v0, 32, 1), pltpu.roll(v1, 32, 1))
-            third = jnp.where(lane < 64, pltpu.roll(v1, 64, 1), pltpu.roll(v2, 64, 1))
-            slot = t % 2
-            for m, value in enumerate((v0, second, third, pltpu.roll(v2, 96, 1))):
-                rows = pl.ds(m, quarter, stride=4)
-                mixed_f[slot, rows, :] = jnp.where(lane < C4, value, empty)
-            kernel = mixed_f[slot].astype(BF16)
+            kernel = parts_f[pl.ds(9 * t + place, C4, stride=40), :].astype(BF16)
             four_out[place, 0:C4, t * 128 : (t + 1) * 128] = kernel
             four_out[place, C4 : 2 * C4, (t + 1) * 128 : (t + 2) * 128] = kernel
 
@@ -529,7 +505,7 @@
     row_strips(own, jnp.logical_not(row_odd), odd_ref)
 
 
-def col_strips_kernel(x_ref, p_ref, q_ref, even_row, odd_row, _, out_ref, *, col_size, parity):
+def col_strips_kernel(x_ref, p_ref, q_ref, odd_row, even_row, _, out_ref, *, col_size, parity):
     row_odd = lax.rem(lax.axis_index("row"), 2) == 1
     col = lax.axis_index("section") * col_size + lax.axis_index("col")
     take_low = lax.rem(col, 2) == parity
@@ -617,23 +593,16 @@
         prep_three_kernel,
         (weight_three,),
         [(27, C3, 256)],
-        [
-            pltpu.VMEM(weight_three.shape, BF16),
-            pltpu.VMEM((3, 32 * C3 // 2, 128), F32),
-            pltpu.VMEM((2, 2, C3, 128), F32),
-            pltpu.SemaphoreType.DMA((CHUNKS,)),
-        ],
-        16, 8_000_000, unread=1, space=pltpu.HBM,
+        [pltpu.VMEM((2, 40 * C3, 128), F32)],
+        16, 8_000_000,
     )
     wu, w4 = call(
         prep_four_kernel,
         (weight_up, weight_four),
         [(16 * 128, 256), (9, 2 * C4, 512)],
         [
-            pltpu.VMEM((3, 16 * C4 // 2, 128), F32),
-            pltpu.VMEM((9, 2, C4, 128), F32),
-            pltpu.VMEM((3, 32 * C4 // 4, 128), F32),
-            pltpu.VMEM((2, C4, 128), F32),
+            pltpu.VMEM((2, 24 * C4, 128), F32),
+            pltpu.VMEM((40 * C4, 128), F32),
         ],
         16, 8_000_000,
     )
@@ -644,7 +613,7 @@
         def col_kernel(*refs):
             col_strips_kernel(*refs, col_size=col_size, parity=1 - parity)
 
-        strip = call(col_kernel, (*tile, even_row, odd_row, w3), [col_strip], [], 4, unread=1)
+        strip = call(col_kernel, (*tile, odd_row, even_row, w3), [col_strip], [], 4, unread=1)
         return lax.ppermute(strip, ("section", "col"), swap_pairs(col_count, parity))
 
     even_col = swap_columns(0)
@@ -654,7 +623,7 @@
         main_kernel(*refs, row_count=row_count, col_count=col_count, col_size=col_size)
 
     operands = (
-        *tile, even_row, odd_row, even_col, odd_col,
+        *tile, odd_row, even_row, even_col, odd_col,
         gain_three.reshape(1, C3), bias_three.reshape(1, C3), w3, wu, bias_up.reshape(1, C4),
         gain_four.reshape(1, C4), w4, bias_four.reshape(1, C4),
     )

time: 33.9 us -> 31.4 us (0.926)
  the two profiles are of different devices: /device:TPU:18 before, /device:TPU:1 now
where the time goes in v1:
time: 31.4 us; the launch traced here: 31.2 us
  Pallas kernels  15.3 us (49%)
  starting transfers between devices  12.2 us (39%)
  waiting for transfers between devices  1.83 us (6%)
  local copies, waits for them, and re-layouts  1.72 us (5%)
    pallas_call x6, Pallas kernels, call(): pl.pallas_call(kernel, out_shape=shapes, in_specs=[vmem] * (len(operands)...  15.3 us
    ppermute x2, starting transfers between devices, swap_columns(): lax.ppermute(strip, ('section', 'col'), swap_pairs(col_count, parity))  6.99 us
    ppermute x1, starting transfers between devices, shards(): even_row = lax.ppermute(even_strip, 'row', swap_pairs(row_count, 0))  4.56 us
    ppermute x2, waiting for transfers between devices, swap_columns(): lax.ppermute(strip, ('section', 'col'), swap_pairs(col_count, parity))  1.82 us
    unnamed x22, local copies, waits for them, and re-layouts  1.72 us
    ppermute x1, starting transfers between devices, shards(): odd_row = lax.ppermute(odd_strip, 'row', swap_pairs(row_count, 1))  0.66 us
  transfers between devices with their start and end apart: 4, of which 1 were waited for; matrix products, arithmetic and copies ran while one was open for 0% of the time, Pallas kernels for 7%

profile of v1, /device:TPU:1, one launch (start us, length us, event | category | flops | bytes accessed | tf_op | source)
XLA Modules:
  0.0 31.2 jit_solution(721400133176217498)
XLA Ops:
  0.0 1.8 %shard_map.109 = (bf16[2,15360]{1,0:T(2,128)(2,1)}, bf16[2,15360]{1,0:T(2,128)(2,1)}) custom-call(bf16[16,7680]{1,0:T(8,128)(2,1)} %refs_0_.5, bf16[16,3840]{1,0:T(8,128)(2,1)} %refs_1_.5, bf16[32,3840]{1,0:T(8,128)(2,1)} %refs_2_.5), custom_call_target="tpu_custom_call" | custom-call | tf_op jit(solution)/shard_map/pallas_call | solution.py:543
  1.9 0.7 %collective-permute-start = (bf16[2,15360]{1,0:T(2,128)(2,1)}, bf16[2,15360]{1,0:T(2,128)(2,1)S(1)}, u32[]{:S(2)}, u32[]{:S(2)}) collective-permute-start(bf16[2,15360]{1,0:T(2,128)(2,1)} %get-tuple-element.9), channel_id=1, source_target_pairs={{4,8},{8,4},{5,9},{9,5},{6,10},{10,6},{7,11},{11,7},{20,24},{24,20... | collective-permute-start | bytes 184328 | tf_op jit(solution)/shard_map/ppermute | solution.py:590
  2.5 0.0 copy-start
  2.5 0.0 copy-start.1
  2.6 4.6 %collective-permute-start.1 = (bf16[2,15360]{1,0:T(2,128)(2,1)}, bf16[2,15360]{1,0:T(2,128)(2,1)S(1)}, u32[]{:S(2)}, u32[]{:S(2)}) collective-permute-start(bf16[2,15360]{1,0:T(2,128)(2,1)} %get-tuple-element.10), channel_id=1, source_target_pairs={{0,4},{4,0},{8,12},{12,8},{1,5},{5,1},{9,13},{13,9},{2,6},{6,2},{1... | collective-permute-start | bytes 184328 | tf_op jit(solution)/shard_map/ppermute | solution.py:589
  7.1 0.0 copy-start.2
  7.1 1.7 %copy-done.2 = bf16[27,36864]{1,0:T(8,128)(2,1)S(1)} copy-done((bf16[27,36864]{1,0:T(8,128)(2,1)S(1)}, bf16[27,36864]{1,0:T(8,128)(2,1)}, u32[]{:S(2)}) %copy-start.2) | copy-done | bytes 1990680
  8.8 0.0 copy-start.3
  8.8 1.3 %shard_map.110.refs_5_.refs_9_ = bf16[27,192,256]{2,1,0:T(8,128)(2,1)S(1)} custom-call(bf16[27,36864]{1,0:T(8,128)(2,1)S(1)} %copy-done.2), custom_call_target="tpu_custom_call" | custom-call | flops 8000000 | bytes 8000000 | tf_op jit(solution)/shard_map/pallas_call | solution.py:543
  10.1 0.0 collective-permute-done.refs_3_
  10.1 0.0 collective-permute-done.1.refs_4_
  10.1 0.0 copy-done
  10.1 0.0 copy-done.1
  10.1 0.0 copy-done.3
  10.1 0.1 shard_map.111
  10.3 0.0 copy-start.4
  10.3 0.0 copy-start.5
  10.3 0.0 copy-start.6
  10.3 0.0 copy-start.7
  10.3 0.0 copy-start.8
  10.3 0.0 copy-start.9
  10.3 0.0 copy-start.10
  10.3 1.4 %collective-permute-start.2 = (bf16[20,2688]{1,0:T(8,128)(2,1)S(1)}, bf16[20,2688]{1,0:T(8,128)(2,1)S(1)}, u32[]{:S(2)}, u32[]{:S(2)}) collective-permute-start(bf16[20,2688]{1,0:T(8,128)(2,1)S(1)} %shard_map.111), channel_id=1, source_target_pairs={{0,1},{1,0},{2,3},{3,2},{16,17},{17,16},{18,19},{19,18},{4,5},{5,4... | collective-permute-start | bytes 322568 | tf_op jit(solution)/shard_map/ppermute | solution.py:617
  11.7 0.1 shard_map.112
  11.8 5.6 %collective-permute-start.3 = (bf16[20,2688]{1,0:T(8,128)(2,1)S(1)}, bf16[20,2688]{1,0:T(8,128)(2,1)S(1)}, u32[]{:S(2)}, u32[]{:S(2)}) collective-permute-start(bf16[20,2688]{1,0:T(8,128)(2,1)S(1)} %shard_map.112), channel_id=1, source_target_pairs={{1,2},{2,1},{3,16},{16,3},{17,18},{18,17},{5,6},{6,5},{7,20},{20,7... | collective-permute-start | bytes 322568 | tf_op jit(solution)/shard_map/ppermute | solution.py:617
  17.5 0.0 copy-done.4
  17.5 0.0 copy-done.5
  17.5 0.9 %shard_map.113 = (bf16[2048,256]{1,0:T(8,128)(2,1)S(1)}, bf16[9,192,512]{2,1,0:T(8,128)(2,1)S(1)}) custom-call(bf16[9,18432]{1,0:T(8,128)(2,1)S(1)} %copy-done.4, bf16[27,9216]{1,0:T(8,128)(2,1)S(1)} %copy-done.5), custom_call_target="tpu_custom_call" | custom-call | flops 8000000 | bytes 8000000 | tf_op jit(solution)/shard_map/pallas_call | solution.py:543
  18.4 0.0 collective-permute-done.2.refs_5_
  18.4 1.8 %collective-permute-done.3.refs_6_ = bf16[20,2688]{1,0:T(8,128)(2,1)S(1)} collective-permute-done((bf16[20,2688]{1,0:T(8,128)(2,1)S(1)}, bf16[20,2688]{1,0:T(8,128)(2,1)S(1)}, u32[]{:S(2)}, u32[]{:S(2)}) %collective-permute-start.3) | collective-permute-done | bytes 107552 | tf_op jit(solution)/shard_map/ppermute | solution.py:617
  20.2 0.0 copy-done.6
  20.2 0.0 copy-done.7
  20.2 0.0 copy-done.8
  20.2 0.0 copy-done.9
  20.2 0.0 copy-done.10
  20.2 11.0 %shard_map.114 = bf16[32,7680]{1,0:T(8,128)(2,1)} custom-call(bf16[16,7680]{1,0:T(8,128)(2,1)S(1)} %copy-done, bf16[16,3840]{1,0:T(8,128)(2,1)S(1)} %copy-done.3, bf16[32,3840]{1,0:T(8,128)(2,1)S(1)} %copy-done.1, bf16[2,15360]{1,0:T(2,128)(2,1)S(1)} %collective-permute-done.refs_3_, bf16[2,15360]{1,0:T(2,128)(2,1)S(1)} %collective-permute-done.1.refs_4_, ...), custom_call_target="tpu_custom_call" | custom-call | tf_op jit(solution)/shard_map/pallas_call | solution.py:543
Async XLA Ops:
  1.9 8.2 %collective-permute-start = (bf16[2,15360]{1,0:T(2,128)(2,1)}, bf16[2,15360]{1,0:T(2,128)(2,1)S(1)}, u32[]{:S(2)}, u32[]{:S(2)}) collective-permute-start(bf16[2,15360]{1,0:T(2,128)(2,1)} %get-tuple-element.9), channel_id=1, source_target_pairs={{4,8},{8,4},{5,9},{9,5},{6,10},{10,6},{7,11},{11,7},{20,24},{24,20... | collective-permute-start | bytes 184328 | tf_op jit(solution)/shard_map/ppermute | solution.py:590
  2.5 7.6 %copy-start = (bf16[16,7680]{1,0:T(8,128)(2,1)S(1)}, bf16[16,7680]{1,0:T(8,128)(2,1)}, u32[]{:S(2)}) copy-start(bf16[16,7680]{1,0:T(8,128)(2,1)} %refs_0_.5) | copy-start | bytes 737284
  2.5 7.6 %copy-start.1 = (bf16[32,3840]{1,0:T(8,128)(2,1)S(1)}, bf16[32,3840]{1,0:T(8,128)(2,1)}, u32[]{:S(2)}) copy-start(bf16[32,3840]{1,0:T(8,128)(2,1)} %refs_2_.5) | copy-start | bytes 737284
  2.6 7.5 %collective-permute-start.1 = (bf16[2,15360]{1,0:T(2,128)(2,1)}, bf16[2,15360]{1,0:T(2,128)(2,1)S(1)}, u32[]{:S(2)}, u32[]{:S(2)}) collective-permute-start(bf16[2,15360]{1,0:T(2,128)(2,1)} %get-tuple-element.10), channel_id=1, source_target_pairs={{0,4},{4,0},{8,12},{12,8},{1,5},{5,1},{9,13},{13,9},{2,6},{6,2},{1... | collective-permute-start | bytes 184328 | tf_op jit(solution)/shard_map/ppermute | solution.py:589
  7.1 1.7 %copy-start.2 = (bf16[27,36864]{1,0:T(8,128)(2,1)S(1)}, bf16[27,36864]{1,0:T(8,128)(2,1)}, u32[]{:S(2)}) copy-start(bf16[27,36864]{1,0:T(8,128)(2,1)} %flat_ref.1) | copy-start | bytes 5971972
  8.8 1.3 %copy-start.3 = (bf16[16,3840]{1,0:T(8,128)(2,1)S(1)}, bf16[16,3840]{1,0:T(8,128)(2,1)}, u32[]{:S(2)}) copy-start(bf16[16,3840]{1,0:T(8,128)(2,1)} %refs_1_.5) | copy-start | bytes 368644
  10.3 7.2 %copy-start.4 = (bf16[9,18432]{1,0:T(8,128)(2,1)S(1)}, bf16[9,18432]{1,0:T(8,128)(2,1)}, u32[]{:S(2)}) copy-start(bf16[9,18432]{1,0:T(8,128)(2,1)} %up_ref.1) | copy-start | bytes 995332
  10.3 7.2 %copy-start.5 = (bf16[27,9216]{1,0:T(8,128)(2,1)S(1)}, bf16[27,9216]{1,0:T(8,128)(2,1)}, u32[]{:S(2)}) copy-start(bf16[27,9216]{1,0:T(8,128)(2,1)} %four_ref.1) | copy-start | bytes 1492996
  10.3 9.9 %copy-start.6 = (f32[192]{0:T(256)S(1)}, f32[192]{0:T(256)}, u32[]{:S(2)}) copy-start(f32[192]{0:T(256)} %param.13) | copy-start | bytes 2308
  10.3 9.9 %copy-start.7 = (f32[192]{0:T(256)S(1)}, f32[192]{0:T(256)}, u32[]{:S(2)}) copy-start(f32[192]{0:T(256)} %param.14) | copy-start | bytes 2308
  10.3 9.9 %copy-start.8 = (f32[96]{0:T(128)S(1)}, f32[96]{0:T(128)}, u32[]{:S(2)}) copy-start(f32[96]{0:T(128)} %param.17) | copy-start | bytes 1156
  10.3 9.9 %copy-start.9 = (f32[96]{0:T(128)S(1)}, f32[96]{0:T(128)}, u32[]{:S(2)}) copy-start(f32[96]{0:T(128)} %param.19) | copy-start | bytes 1156
  10.3 9.9 %copy-start.10 = (f32[96]{0:T(128)S(1)}, f32[96]{0:T(128)}, u32[]{:S(2)}) copy-start(f32[96]{0:T(128)} %param.21) | copy-start | bytes 1156
  10.3 8.0 %collective-permute-start.2 = (bf16[20,2688]{1,0:T(8,128)(2,1)S(1)}, bf16[20,2688]{1,0:T(8,128)(2,1)S(1)}, u32[]{:S(2)}, u32[]{:S(2)}) collective-permute-start(bf16[20,2688]{1,0:T(8,128)(2,1)S(1)} %shard_map.111), channel_id=1, source_target_pairs={{0,1},{1,0},{2,3},{3,2},{16,17},{17,16},{18,19},{19,18},{4,5},{5,4... | collective-permute-start | bytes 322568 | tf_op jit(solution)/shard_map/ppermute | solution.py:617
  11.8 8.4 %collective-permute-start.3 = (bf16[20,2688]{1,0:T(8,128)(2,1)S(1)}, bf16[20,2688]{1,0:T(8,128)(2,1)S(1)}, u32[]{:S(2)}, u32[]{:S(2)}) collective-permute-start(bf16[20,2688]{1,0:T(8,128)(2,1)S(1)} %shard_map.112), channel_id=1, source_target_pairs={{1,2},{2,1},{3,16},{16,3},{17,18},{18,17},{5,6},{6,5},{7,20},{20,7... | collective-permute-start | bytes 322568 | tf_op jit(solution)/shard_map/ppermute | solution.py:617

commit v2 on v1

--- a/solution.py
+++ b/solution.py
@@ -74,17 +74,6 @@
         order += [((n + 0.5) / len(steps), place, step) for n, step in enumerate(steps)]
     for _, _, step in sorted(order, key=lambda entry: entry[:2]):
         step()
-
-
-def up_slots():
-    slots = {}
-    count = 0
-    for di in range(3):
-        for dj in range(3):
-            phases = [(a, b) for a in range(2) for b in range(2) if 0 <= di - a < 2 and 0 <= dj - b < 2]
-            slots[di, dj] = (count, phases)
-            count += len(phases)
-    return slots
 
 
 def main_kernel(
@@ -175,40 +164,41 @@
                 act_d[group][dy, slab * ROWS : (slab + 1) * ROWS, :] = pair_of(act[group], rows, slice(None))
 
     def gather_rows(group, place):
-        ext = (0, 1, 2, 17, 18, 19)[place]
+        dx, ext = place // 6, (0, 1, 2, 17, 18, 19)[place % 6]
         for half in range(2):
-            rows = pl.ds(half * WIDE * EXT + ext, 16, stride=EXT)
+            rows = pl.ds((half * WIDE + dx) * EXT + ext, 16, stride=EXT)
             halo_d[group][place, half * 16 : (half + 1) * 16, :] = pair_of(act[group], rows, slice(None))
 
     def coarse_steps(group):
         for jj in range(WIDE):
             yield lambda jj=jj: (load_column(group, jj), shift_column(group, jj))
-        for place in range(6):
+        for place in range(18):
             yield lambda place=place: gather_rows(group, place)
 
-    mid = 2 * MID * ROWS
-    center = [None, None]
-    edges = [[None] * 3, [None] * 3]
-
-    def conv_three(p, dy, dx, t):
-        parts = []
-        halos = []
-        for k in range(2):
-            group, half = p + (k + t) // 2, (k + t) % 2
-            at = (half * WIDE + dx) * ROWS
-            parts.append(act_d[group][dy, at : at + MID * ROWS, 0:C3])
-            for side in range(2):
-                halos.append(halo_d[group][3 * side + dy, half * 16 : (half + 1) * 16, 0:C3])
-        kernel = w3_ref[9 * t + 3 * dy + dx, :, 0:C3]
-        got = nt_dot(jnp.concatenate(parts + halos, axis=0), kernel)
-        center[p] = got[:mid] if center[p] is None else center[p] + got[:mid]
-        edges[p][dx] = got[mid:] if edges[p][dx] is None else edges[p][dx] + got[mid:]
-
-    def conv_three_steps(p):
+    mid = MID * ROWS
+    center = [[None, None], [None, None]]
+
+    def conv_three(p, k):
+        kernels = []
+        pieces = []
         for dy in range(3):
             for dx in range(3):
+                kernels.append(w3_ref[3 * dy + dx])
                 for t in range(3):
-                    yield lambda dy=dy, dx=dx, t=t: conv_three(p, dy, dx, t)
+                    parts = []
+                    group, half = p + (k + t) // 2, (k + t) % 2
+                    at = (half * WIDE + dx) * ROWS
+                    parts.append(act_d[group][dy, at : at + MID * ROWS, :])
+                    for side in range(2):
+                        place = 6 * dx + 3 * side + dy
+                        parts.append(halo_d[group][place, half * 16 : (half + 1) * 16, :])
+                    pieces.append(jnp.concatenate(parts, axis=0))
+        got = nt_dot(jnp.concatenate(pieces, axis=1), jnp.concatenate(kernels, axis=1))
+        center[p][k] = got
+
+    def conv_three_steps(p):
+        for k in range(2):
+            yield lambda k=k: conv_three(p, k)
 
     b3 = b3_ref[...]
     column = lax.broadcasted_iota(jnp.int32, (MID, 1), 0)
@@ -219,14 +209,15 @@
 
     def put_res(p, rows, value):
         res[p][0, rows, :] = value[:, 0:128]
-        res[p][1, rows, 0:64] = value[:, 128:192]
+        rest = jnp.zeros((value.shape[0], 64), F32)
+        res[p][1, rows, :] = jnp.concatenate([value[:, 128:192], rest], axis=1)
 
     def result_column(p, jm):
         at = (jm + 1) * EXT
         tiles = [raw[p + 1][q, at : at + ROWS, :] for q in range(3)]
         for k, skip in enumerate(split_pair(*tiles)):
             slab = k * MID + jm
-            value = center[p][slab * ROWS : (slab + 1) * ROWS] + b3
+            value = center[p][k][jm * ROWS : (jm + 1) * ROWS] + b3
             value = rounded(value + jnp.concatenate([skip[0], skip[1][:, 0:64]], axis=1))
             if jm == 0:
                 value = keep(jnp.logical_not(first_col), value)
@@ -239,9 +230,8 @@
         ext = 18 if side else 17
         tiles = [raw[p + 1][q, pl.ds(EXT + ext, MID, stride=EXT), :] for q in range(3)]
         for k, skip in enumerate(split_pair(*tiles)):
-            at = (2 * k + side) * 16
-            value = b3 + edges[p][0][at : at + MID] + edges[p][1][at + 1 : at + 1 + MID]
-            value = value + edges[p][2][at + 2 : at + 2 + MID]
+            at = mid + side * 16
+            value = center[p][k][at : at + MID] + b3
             value = rounded(value + jnp.concatenate([skip[0], skip[1][:, 0:64]], axis=1))
             value = keep(jnp.logical_and(cols_in, rows_in), value)
             put_res(p, pl.ds(k * MID * EXT + (17 if side else 0), MID, stride=EXT), value)
@@ -249,14 +239,14 @@
     def shift_result(p, jm):
         for k in range(2):
             slab = k * MID + jm
-            for di in range(3):
-                rows = slice(slab * EXT + di, slab * EXT + di + ROWS)
-                res_d[p][di, slab * ROWS : (slab + 1) * ROWS, :] = pair_of(res[p], rows, slice(None))
+            for r in range(2):
+                rows = slice(slab * EXT + r, slab * EXT + r + ROWS)
+                res_d[p][r, slab * ROWS : (slab + 1) * ROWS, :] = pair_of(res[p], rows, slice(None))
 
     def gather_result(p, place):
-        ext = (0, 1, 16, 17)[place]
+        r, c = divmod(place, 2)
         for k in range(2):
-            rows = pl.ds(k * MID * EXT + ext, 16, stride=EXT)
+            rows = pl.ds((k * MID + c) * EXT + ROWS + r, 16, stride=EXT)
             res_h[p][place, k * 16 : (k + 1) * 16, :] = pair_of(res[p], rows, slice(None))
 
     def result_steps(p):
@@ -268,40 +258,21 @@
             yield lambda place=place: gather_result(p, place)
 
     span = COLS + 1
-    slots = up_slots()
-    total = [{}, {}]
-    rim = [{}, {}]
-
-    def conv_up(p, di, dj):
-        start, phases = slots[di, dj]
-        low = min(dj - b for _, b in phases)
-        wide_cols = span + max(dj - b for _, b in phases) - low
-        sides = sorted({a for a, _ in phases})
-        parts = []
+    total = [[None, None], [None, None]]
+
+    def conv_up(p, k):
+        pieces = []
+        for r in range(2):
+            for c in range(2):
+                at = (k * MID + c) * ROWS
+                own = res_d[p][r, at : at + span * ROWS, :]
+                last = res_h[p][2 * r + c, k * 16 : (k + 1) * 16, :]
+                pieces.append(jnp.concatenate([own, last], axis=0))
+        total[p][k] = nt_dot(jnp.concatenate(pieces, axis=1), wu_ref[...])
+
+    def conv_up_steps(p):
         for k in range(2):
-            at = (k * MID + low) * ROWS
-            parts.append(res_d[p][di, at : at + wide_cols * ROWS, 0:C3])
-        for a in sides:
-            parts.append(res_h[p][(di - 1) if a else (2 + di), :, 0:C3])
-        kernel = wu_ref[start * 128 : (start + len(phases)) * 128, 0:C3]
-        got = nt_dot(jnp.concatenate(parts, axis=0), kernel)
-        for n, (a, b) in enumerate(phases):
-            lanes = slice(n * 128, (n + 1) * 128)
-            for k in range(2):
-                at = (k * wide_cols + dj - b - low) * ROWS
-                value = got[at : at + span * ROWS, lanes]
-                at = 2 * wide_cols * ROWS + sides.index(a) * 32 + k * 16 + dj - b
-                edge = got[at : at + span, lanes]
-                if (a, b, k) in total[p]:
-                    value = value + total[p][a, b, k]
-                    edge = edge + rim[p][a, b, k]
-                total[p][a, b, k] = value
-                rim[p][a, b, k] = edge
-
-    def conv_up_steps(p):
-        for di in range(3):
-            for dj in range(3):
-                yield lambda di=di, dj=dj: conv_up(p, di, dj)
+            yield lambda k=k: conv_up(p, k)
 
     bias_up = jnp.concatenate([bu_ref[...], jnp.zeros((1, 32), F32)], axis=1)
     g4 = jnp.concatenate([g4_ref[...], jnp.zeros((1, 32), F32)], axis=1)
@@ -311,29 +282,43 @@
         return silu(value * lax.rsqrt(square * (1.0 / C4) + EPSILON) * g4)
 
     def fine_rows(p, a, b, k):
-        value = act_four(rounded(rim[p][a, b, k] + bias_up))
+        at = span * ROWS
+        lanes = slice((2 * a + b) * 128, (2 * a + b + 1) * 128)
+        value = rounded(total[p][k][at : at + span, lanes] + bias_up)
+        ext = FROWS if a else FROWS + 1
+        rows = pl.ds((0 if b else FEXT) + ext, span, stride=2 * FEXT)
+        if a:
+            s4[p][k, rows, :] = value
+        value = act_four(value)
         index = lax.broadcasted_iota(jnp.int32, (span, 1), 0)
         if b:
             inside = jnp.logical_or(index > 0, jnp.logical_not(first_col))
         else:
             inside = jnp.logical_or(index < span - 1, jnp.logical_not(last_col))
-        value = keep(jnp.logical_and(inside, jnp.logical_not(first_row if a else last_row)), value)
-        start = (0 if b else FEXT) + (0 if a else FROWS + 1)
-        z4[p + 1][k, pl.ds(start, span, stride=2 * FEXT), :] = value
+        if not a:
+            inside = jnp.logical_and(inside, jnp.logical_not(last_row))
+        z4[p + 1][k, rows, :] = keep(inside, value)
+
+    top = lax.broadcasted_iota(jnp.int32, (ROWS, 1), 0) > 0
+    rows_in = jnp.logical_or(top, jnp.logical_not(first_row))
 
     def fine_column(p, b, j):
         fx = 2 * j if b else 2 * j + 1
         for k in range(2):
             for a in range(2):
-                value = rounded(total[p][a, b, k][j * ROWS : (j + 1) * ROWS] + bias_up)
+                lanes = slice((2 * a + b) * 128, (2 * a + b + 1) * 128)
+                value = rounded(total[p][k][j * ROWS : (j + 1) * ROWS, lanes] + bias_up)
+                rows = pl.ds(fx * FEXT + 1 - a, ROWS, stride=2)
                 if 1 <= fx <= 2 * COLS:
-                    s4[p][k, pl.ds((fx - 1) * FROWS + a, ROWS, stride=2), :] = value
+                    s4[p][k, rows, :] = value
                 value = act_four(value)
+                if a:
+                    value = keep(rows_in, value)
                 if fx == 0:
                     value = keep(jnp.logical_not(first_col), value)
                 if fx == FINE - 1:
                     value = keep(jnp.logical_not(last_col), value)
-                z4[p + 1][k, pl.ds(fx * FEXT + 1 + a, ROWS, stride=2), :] = value
+                z4[p + 1][k, rows, :] = value
         shift_fine(p + 1, fx)
 
     def shift_fine(group, fx):
@@ -378,29 +363,32 @@
         for fx in range(FINE):
             yield lambda fx=fx: cached_column(fx)
 
-    size = 2 * COLS * FROWS
-    done = [None, None]
-
-    def conv_four(p, dy, dx):
-        at = dx * FROWS
-        parts = [act4_d[group][dy, at : at + size, :] for group in (p, p + 1)]
-        got = nt_dot(jnp.concatenate(parts, axis=1), w4_ref[3 * dy + dx])
-        done[p] = got if done[p] is None else done[p] + got
-
-    def conv_four_steps(p):
+    size = COLS * FROWS
+    done = [[None, None], [None, None]]
+
+    def conv_four(p, half):
+        pieces = []
         for dy in range(3):
             for dx in range(3):
-                yield lambda dy=dy, dx=dx: conv_four(p, dy, dx)
+                at = (dx + half * COLS) * FROWS
+                pieces += [act4_d[group][dy, at : at + size, :] for group in (p, p + 1)]
+        kernel = jnp.concatenate([w4_ref[dy] for dy in range(3)], axis=1)
+        done[p][half] = nt_dot(jnp.concatenate(pieces, axis=1), kernel)
+
+    def conv_four_steps(p):
+        for half in range(2):
+            yield lambda half=half: conv_four(p, half)
 
     b4 = b4_ref[...]
     bias_four = jnp.concatenate([b4, b4], axis=1)
     first = lane_mask(FROWS, C4)
 
     def out_column(p, fx):
-        rows = slice(fx * FROWS, (fx + 1) * FROWS)
+        rows = slice((fx + 1) * FEXT + 1, (fx + 1) * FEXT + 1 + FROWS)
         other = pltpu.roll(s4[p][1, rows, :], C4, 1)
         skip = jnp.concatenate([jnp.where(first, s4[p][0, rows, :], other), other[:, 0:64]], axis=1)
-        value = (done[p][rows] + bias_four + skip).astype(BF16)
+        at = fx % COLS * FROWS
+        value = (done[p][fx // COLS][at : at + FROWS] + bias_four + skip).astype(BF16)
         out_ref[:, fx * 384 + p * 192 : fx * 384 + (p + 1) * 192] = value
 
     def out_steps(p):
@@ -409,16 +397,16 @@
 
     weave(coarse_steps(0), coarse_steps(1))
     weave(conv_three_steps(0), coarse_steps(2), cached_steps())
-    later = list(conv_three_steps(1))
-    weave(later[:13], result_steps(0))
+    weave(conv_three_steps(1), result_steps(0))
     weave(conv_up_steps(0))
-    weave(later[13:], fine_steps(0))
-    later = list(conv_four_steps(0))
-    weave(later[:4], result_steps(1))
+    weave(fine_steps(0), result_steps(1))
     weave(conv_up_steps(1))
-    weave(later[4:], fine_steps(1))
-    weave(conv_four_steps(1), out_steps(0))
-    weave(out_steps(1))
+    weave(conv_four_steps(0), fine_steps(1))
+    later = list(conv_four_steps(1))
+    ends = list(out_steps(1))
+    weave(later[:1], out_steps(0))
+    weave(later[1:], ends[:10])
+    weave(ends[10:])
 
 
 def split_pairs(flat_ref, parts, pairs, taps, stride):
@@ -438,7 +426,8 @@
     split_pairs(flat_ref, parts, range(C3 // 2), 27, 40)
     for tap in range(27):
         both = [parts[q, pl.ds(tap, C3, stride=40), :] for q in range(2)]
-        out_ref[tap] = jnp.concatenate(both, axis=1).astype(BF16)
+        t, place = divmod(tap, 9)
+        out_ref[place, :, t * 256 : (t + 1) * 256] = jnp.concatenate(both, axis=1).astype(BF16)
 
 
 def prep_four_kernel(up_ref, four_ref, up_out, four_out, parts_u, parts_f):
@@ -449,19 +438,22 @@
             taps[tap, q] = parts_u[q, pl.ds(tap, C4, stride=24), :]
     spans = {(0, 0): (0,), (0, 1): (1, 2), (1, 0): (0, 1), (1, 1): (2,)}
     rest = jnp.zeros((32, 256), BF16)
-    for (di, dj), (start, phases) in up_slots().items():
-        for n, (a, b) in enumerate(phases):
-            tiles = []
-            for q in range(2):
-                total = None
-                for dy in spans[a, di - a]:
-                    for dx in spans[b, dj - b]:
-                        one = taps[3 * dy + dx, q]
-                        total = one if total is None else total + one
-                tiles.append(total)
-            at = (start + n) * 128
-            up_out[at : at + C4, :] = jnp.concatenate(tiles, axis=1).astype(BF16)
-            up_out[at + C4 : at + 128, :] = rest
+    for a in range(2):
+        for b in range(2):
+            at = (2 * a + b) * 128
+            for r in range(2):
+                for c in range(2):
+                    tiles = []
+                    for q in range(2):
+                        total = None
+                        for dy in spans[a, r]:
+                            for dx in spans[b, c]:
+                                one = taps[3 * dy + dx, q]
+                                total = one if total is None else total + one
+                        tiles.append(total)
+                    lanes = slice((2 * r + c) * 256, (2 * r + c + 1) * 256)
+                    up_out[at : at + C4, lanes] = jnp.concatenate(tiles, axis=1).astype(BF16)
+                    up_out[at + C4 : at + 128, lanes] = rest
     lane = lax.broadcasted_iota(jnp.int32, (27, 128), 1)
     empty = jnp.zeros((27, 128), F32)
     for four in range(C4 // 4):
@@ -474,12 +466,14 @@
             parts_f[at : at + 27, :] = jnp.where(lane < C4, value, empty)
     none = jnp.zeros((C4, 128), BF16)
     for place in range(9):
-        four_out[place, 0:C4, 384:512] = none
-        four_out[place, C4 : 2 * C4, 0:128] = none
+        dy, dx = divmod(place, 3)
+        at = dx * 512
+        four_out[dy, 0:C4, at + 384 : at + 512] = none
+        four_out[dy, C4 : 2 * C4, at : at + 128] = none
         for t in range(3):
             kernel = parts_f[pl.ds(9 * t + place, C4, stride=40), :].astype(BF16)
-            four_out[place, 0:C4, t * 128 : (t + 1) * 128] = kernel
-            four_out[place, C4 : 2 * C4, (t + 1) * 128 : (t + 2) * 128] = kernel
+            four_out[dy, 0:C4, at + t * 128 : at + (t + 1) * 128] = kernel
+            four_out[dy, C4 : 2 * C4, at + (t + 1) * 128 : at + (t + 2) * 128] = kernel
 
 
 def row_strips(refs, low_flag, out_ref):
@@ -592,14 +586,14 @@
     w3 = call(
         prep_three_kernel,
         (weight_three,),
-        [(27, C3, 256)],
+        [(9, C3, 3 * 256)],
         [pltpu.VMEM((2, 40 * C3, 128), F32)],
         16, 8_000_000,
     )
     wu, w4 = call(
         prep_four_kernel,
         (weight_up, weight_four),
-        [(16 * 128, 256), (9, 2 * C4, 512)],
+        [(4 * 128, 4 * 256), (3, 2 * C4, 3 * 512)],
         [
             pltpu.VMEM((2, 24 * C4, 128), F32),
             pltpu.VMEM((40 * C4, 128), F32),
@@ -628,14 +622,14 @@
         gain_four.reshape(1, C4), w4, bias_four.reshape(1, C4),
     )
     scratch = [pltpu.VMEM((3, 16 * EXT, 128), F32)] * 3
-    scratch += [pltpu.VMEM((2, (2 * WIDE + 2) * EXT, 128), F32)] * 3
+    scratch += [pltpu.VMEM((2, (2 * WIDE + 4) * EXT, 128), F32)] * 3
     scratch += [pltpu.VMEM((3, 2 * WIDE * ROWS, 256), BF16)] * 3
-    scratch += [pltpu.VMEM((6, 2 * 16, 256), BF16)] * 3
-    scratch += [pltpu.VMEM((2, (2 * MID + 4) * EXT, 128), F32)] * 2
-    scratch += [pltpu.VMEM((3, 2 * MID * ROWS, 256), BF16)] * 2
+    scratch += [pltpu.VMEM((18, 2 * 16, 256), BF16)] * 3
+    scratch += [pltpu.VMEM((2, (2 * MID + 5) * EXT, 128), F32)] * 2
+    scratch += [pltpu.VMEM((2, 2 * MID * ROWS, 256), BF16)] * 2
     scratch += [pltpu.VMEM((4, 2 * 16, 256), BF16)] * 2
     scratch += [pltpu.VMEM((2, FINE * FEXT, 128), F32)] * 3
-    scratch += [pltpu.VMEM((2, 2 * COLS * FROWS, 128), F32)] * 2
+    scratch += [pltpu.VMEM((2, FINE * FEXT, 128), F32)] * 2
     scratch += [pltpu.VMEM((3, FINE * FROWS, 256), BF16)] * 3
     return call(kernel, operands, [(FROWS, 2 * COLS * FRAMES * C4)], scratch, 32)
 

time: 31.4 us -> 29.7 us (0.946)
  Pallas kernels: 15.3 us -> 13.5 us
    pallas_call x6, Pallas kernels: 15.3 us -> 13.5 us  [call(): pl.pallas_call(kernel, out_shape=shapes, in_specs=[vmem] * (len(operands)...]
  transfers between devices with their start and end apart: 4 -> 4, of which waited for: 1 -> 1; matrix products, arithmetic and copies ran while one was open for 0% -> 0% of each run, Pallas kernels for 7% -> 8%
where the time goes in v2:
time: 29.7 us; the launch traced here: 29.5 us
  Pallas kernels  13.5 us (45%)
  starting transfers between devices  12.2 us (41%)
  waiting for transfers between devices  1.85 us (6%)
  local copies, waits for them, and re-layouts  1.72 us (6%)
    pallas_call x6, Pallas kernels, call(): pl.pallas_call(kernel, out_shape=shapes, in_specs=[vmem] * (len(operands)...  13.5 us
    ppermute x2, starting transfers between devices, swap_columns(): lax.ppermute(strip, ('section', 'col'), swap_pairs(col_count, parity))  7 us
    ppermute x1, starting transfers between devices, shards(): even_row = lax.ppermute(even_strip, 'row', swap_pairs(row_count, 0))  4.56 us
    ppermute x2, waiting for transfers between devices, swap_columns(): lax.ppermute(strip, ('section', 'col'), swap_pairs(col_count, parity))  1.85 us
    unnamed x22, local copies, waits for them, and re-layouts  1.72 us
    ppermute x1, starting transfers between devices, shards(): odd_row = lax.ppermute(odd_strip, 'row', swap_pairs(row_count, 1))  0.66 us
  transfers between devices with their start and end apart: 4, of which 1 were waited for; matrix products, arithmetic and copies ran while one was open for 0% of the time, Pallas kernels for 8%

profile of v2, /device:TPU:1, one launch (start us, length us, event | category | flops | bytes accessed | tf_op | source)
XLA Modules:
  0.0 29.5 jit_solution(3313179234107276316)
XLA Ops:
  0.0 1.8 %shard_map.109 = (bf16[2,15360]{1,0:T(2,128)(2,1)}, bf16[2,15360]{1,0:T(2,128)(2,1)}) custom-call(bf16[16,7680]{1,0:T(8,128)(2,1)} %refs_0_.5, bf16[16,3840]{1,0:T(8,128)(2,1)} %refs_1_.5, bf16[32,3840]{1,0:T(8,128)(2,1)} %refs_2_.5), custom_call_target="tpu_custom_call" | custom-call | tf_op jit(solution)/shard_map/pallas_call | solution.py:537
  1.9 0.7 %collective-permute-start = (bf16[2,15360]{1,0:T(2,128)(2,1)}, bf16[2,15360]{1,0:T(2,128)(2,1)S(1)}, u32[]{:S(2)}, u32[]{:S(2)}) collective-permute-start(bf16[2,15360]{1,0:T(2,128)(2,1)} %get-tuple-element.9), channel_id=1, source_target_pairs={{4,8},{8,4},{5,9},{9,5},{6,10},{10,6},{7,11},{11,7},{20,24},{24,20... | collective-permute-start | bytes 184328 | tf_op jit(solution)/shard_map/ppermute | solution.py:584
  2.5 0.0 copy-start
  2.5 0.0 copy-start.1
  2.6 4.6 %collective-permute-start.1 = (bf16[2,15360]{1,0:T(2,128)(2,1)}, bf16[2,15360]{1,0:T(2,128)(2,1)S(1)}, u32[]{:S(2)}, u32[]{:S(2)}) collective-permute-start(bf16[2,15360]{1,0:T(2,128)(2,1)} %get-tuple-element.10), channel_id=1, source_target_pairs={{0,4},{4,0},{8,12},{12,8},{1,5},{5,1},{9,13},{13,9},{2,6},{6,2},{1... | collective-permute-start | bytes 184328 | tf_op jit(solution)/shard_map/ppermute | solution.py:583
  7.1 0.0 copy-start.2
  7.1 1.7 %copy-done.2 = bf16[27,36864]{1,0:T(8,128)(2,1)S(1)} copy-done((bf16[27,36864]{1,0:T(8,128)(2,1)S(1)}, bf16[27,36864]{1,0:T(8,128)(2,1)}, u32[]{:S(2)}) %copy-start.2) | copy-done | bytes 1990680
  8.8 0.0 copy-start.3
  8.8 1.3 %shard_map.110.refs_5_.refs_9_ = bf16[9,192,768]{2,1,0:T(8,128)(2,1)S(1)} custom-call(bf16[27,36864]{1,0:T(8,128)(2,1)S(1)} %copy-done.2), custom_call_target="tpu_custom_call" | custom-call | flops 8000000 | bytes 8000000 | tf_op jit(solution)/shard_map/pallas_call | solution.py:537
  10.1 0.0 collective-permute-done.refs_3_
  10.1 0.0 collective-permute-done.1.refs_4_
  10.1 0.0 copy-done
  10.1 0.0 copy-done.1
  10.1 0.0 copy-done.3
  10.1 0.1 shard_map.111
  10.3 0.0 copy-start.4
  10.3 0.0 copy-start.5
  10.3 0.0 copy-start.6
  10.3 0.0 copy-start.7
  10.3 0.0 copy-start.8
  10.3 0.0 copy-start.9
  10.3 0.0 copy-start.10
  10.3 1.4 %collective-permute-start.2 = (bf16[20,2688]{1,0:T(8,128)(2,1)S(1)}, bf16[20,2688]{1,0:T(8,128)(2,1)S(1)}, u32[]{:S(2)}, u32[]{:S(2)}) collective-permute-start(bf16[20,2688]{1,0:T(8,128)(2,1)S(1)} %shard_map.111), channel_id=1, source_target_pairs={{0,1},{1,0},{2,3},{3,2},{16,17},{17,16},{18,19},{19,18},{4,5},{5,4... | collective-permute-start | bytes 322568 | tf_op jit(solution)/shard_map/ppermute | solution.py:611
  11.7 0.1 shard_map.112
  11.8 5.6 %collective-permute-start.3 = (bf16[20,2688]{1,0:T(8,128)(2,1)S(1)}, bf16[20,2688]{1,0:T(8,128)(2,1)S(1)}, u32[]{:S(2)}, u32[]{:S(2)}) collective-permute-start(bf16[20,2688]{1,0:T(8,128)(2,1)S(1)} %shard_map.112), channel_id=1, source_target_pairs={{1,2},{2,1},{3,16},{16,3},{17,18},{18,17},{5,6},{6,5},{7,20},{20,7... | collective-permute-start | bytes 322568 | tf_op jit(solution)/shard_map/ppermute | solution.py:611
  17.5 0.0 copy-done.4
  17.5 0.0 copy-done.5
  17.5 0.8 %shard_map.113 = (bf16[512,1024]{1,0:T(8,128)(2,1)S(1)}, bf16[3,192,1536]{2,1,0:T(8,128)(2,1)S(1)}) custom-call(bf16[9,18432]{1,0:T(8,128)(2,1)S(1)} %copy-done.4, bf16[27,9216]{1,0:T(8,128)(2,1)S(1)} %copy-done.5), custom_call_target="tpu_custom_call" | custom-call | flops 8000000 | bytes 8000000 | tf_op jit(solution)/shard_map/pallas_call | solution.py:537
  18.3 0.0 collective-permute-done.2.refs_5_
  18.3 1.8 %collective-permute-done.3.refs_6_ = bf16[20,2688]{1,0:T(8,128)(2,1)S(1)} collective-permute-done((bf16[20,2688]{1,0:T(8,128)(2,1)S(1)}, bf16[20,2688]{1,0:T(8,128)(2,1)S(1)}, u32[]{:S(2)}, u32[]{:S(2)}) %collective-permute-start.3) | collective-permute-done | bytes 107552 | tf_op jit(solution)/shard_map/ppermute | solution.py:611
  20.2 0.0 copy-done.6
  20.2 0.0 copy-done.7
  20.2 0.0 copy-done.8
  20.2 0.0 copy-done.9
  20.2 0.0 copy-done.10
  20.2 9.3 %shard_map.114 = bf16[32,7680]{1,0:T(8,128)(2,1)} custom-call(bf16[16,7680]{1,0:T(8,128)(2,1)S(1)} %copy-done, bf16[16,3840]{1,0:T(8,128)(2,1)S(1)} %copy-done.3, bf16[32,3840]{1,0:T(8,128)(2,1)S(1)} %copy-done.1, bf16[2,15360]{1,0:T(2,128)(2,1)S(1)} %collective-permute-done.refs_3_, bf16[2,15360]{1,0:T(2,128)(2,1)S(1)} %collective-permute-done.1.refs_4_, ...), custom_call_target="tpu_custom_call" | custom-call | tf_op jit(solution)/shard_map/pallas_call | solution.py:537
Async XLA Ops:
  1.9 8.2 %collective-permute-start = (bf16[2,15360]{1,0:T(2,128)(2,1)}, bf16[2,15360]{1,0:T(2,128)(2,1)S(1)}, u32[]{:S(2)}, u32[]{:S(2)}) collective-permute-start(bf16[2,15360]{1,0:T(2,128)(2,1)} %get-tuple-element.9), channel_id=1, source_target_pairs={{4,8},{8,4},{5,9},{9,5},{6,10},{10,6},{7,11},{11,7},{20,24},{24,20... | collective-permute-start | bytes 184328 | tf_op jit(solution)/shard_map/ppermute | solution.py:584
  2.5 7.6 %copy-start = (bf16[16,7680]{1,0:T(8,128)(2,1)S(1)}, bf16[16,7680]{1,0:T(8,128)(2,1)}, u32[]{:S(2)}) copy-start(bf16[16,7680]{1,0:T(8,128)(2,1)} %refs_0_.5) | copy-start | bytes 737284
  2.5 7.6 %copy-start.1 = (bf16[32,3840]{1,0:T(8,128)(2,1)S(1)}, bf16[32,3840]{1,0:T(8,128)(2,1)}, u32[]{:S(2)}) copy-start(bf16[32,3840]{1,0:T(8,128)(2,1)} %refs_2_.5) | copy-start | bytes 737284
  2.6 7.5 %collective-permute-start.1 = (bf16[2,15360]{1,0:T(2,128)(2,1)}, bf16[2,15360]{1,0:T(2,128)(2,1)S(1)}, u32[]{:S(2)}, u32[]{:S(2)}) collective-permute-start(bf16[2,15360]{1,0:T(2,128)(2,1)} %get-tuple-element.10), channel_id=1, source_target_pairs={{0,4},{4,0},{8,12},{12,8},{1,5},{5,1},{9,13},{13,9},{2,6},{6,2},{1... | collective-permute-start | bytes 184328 | tf_op jit(solution)/shard_map/ppermute | solution.py:583
  7.1 1.7 %copy-start.2 = (bf16[27,36864]{1,0:T(8,128)(2,1)S(1)}, bf16[27,36864]{1,0:T(8,128)(2,1)}, u32[]{:S(2)}) copy-start(bf16[27,36864]{1,0:T(8,128)(2,1)} %flat_ref.1) | copy-start | bytes 5971972
  8.8 1.3 %copy-start.3 = (bf16[16,3840]{1,0:T(8,128)(2,1)S(1)}, bf16[16,3840]{1,0:T(8,128)(2,1)}, u32[]{:S(2)}) copy-start(bf16[16,3840]{1,0:T(8,128)(2,1)} %refs_1_.5) | copy-start | bytes 368644
  10.3 7.2 %copy-start.4 = (bf16[9,18432]{1,0:T(8,128)(2,1)S(1)}, bf16[9,18432]{1,0:T(8,128)(2,1)}, u32[]{:S(2)}) copy-start(bf16[9,18432]{1,0:T(8,128)(2,1)} %up_ref.1) | copy-start | bytes 995332
  10.3 7.2 %copy-start.5 = (bf16[27,9216]{1,0:T(8,128)(2,1)S(1)}, bf16[27,9216]{1,0:T(8,128)(2,1)}, u32[]{:S(2)}) copy-start(bf16[27,9216]{1,0:T(8,128)(2,1)} %four_ref.1) | copy-start | bytes 1492996
  10.3 9.9 %copy-start.6 = (f32[192]{0:T(256)S(1)}, f32[192]{0:T(256)}, u32[]{:S(2)}) copy-start(f32[192]{0:T(256)} %param.13) | copy-start | bytes 2308
  10.3 9.9 %copy-start.7 = (f32[192]{0:T(256)S(1)}, f32[192]{0:T(256)}, u32[]{:S(2)}) copy-start(f32[192]{0:T(256)} %param.14) | copy-start | bytes 2308
  10.3 9.9 %copy-start.8 = (f32[96]{0:T(128)S(1)}, f32[96]{0:T(128)}, u32[]{:S(2)}) copy-start(f32[96]{0:T(128)} %param.17) | copy-start | bytes 1156
  10.3 9.9 %copy-start.9 = (f32[96]{0:T(128)S(1)}, f32[96]{0:T(128)}, u32[]{:S(2)}) copy-start(f32[96]{0:T(128)} %param.19) | copy-start | bytes 1156
  10.3 9.9 %copy-start.10 = (f32[96]{0:T(128)S(1)}, f32[96]{0:T(128)}, u32[]{:S(2)}) copy-start(f32[96]{0:T(128)} %param.21) | copy-start | bytes 1156
  10.3 8.0 %collective-permute-start.2 = (bf16[20,2688]{1,0:T(8,128)(2,1)S(1)}, bf16[20,2688]{1,0:T(8,128)(2,1)S(1)}, u32[]{:S(2)}, u32[]{:S(2)}) collective-permute-start(bf16[20,2688]{1,0:T(8,128)(2,1)S(1)} %shard_map.111), channel_id=1, source_target_pairs={{0,1},{1,0},{2,3},{3,2},{16,17},{17,16},{18,19},{19,18},{4,5},{5,4... | collective-permute-start | bytes 322568 | tf_op jit(solution)/shard_map/ppermute | solution.py:611
  11.8 8.4 %collective-permute-start.3 = (bf16[20,2688]{1,0:T(8,128)(2,1)S(1)}, bf16[20,2688]{1,0:T(8,128)(2,1)S(1)}, u32[]{:S(2)}, u32[]{:S(2)}) collective-permute-start(bf16[20,2688]{1,0:T(8,128)(2,1)S(1)} %shard_map.112), channel_id=1, source_target_pairs={{1,2},{2,1},{3,16},{16,3},{17,18},{18,17},{5,6},{6,5},{7,20},{20,7... | collective-permute-start | bytes 322568 | tf_op jit(solution)/shard_map/ppermute | solution.py:611

commit v3 on v2

--- a/solution.py
+++ b/solution.py
@@ -1,3 +1,6 @@
+import functools
+import types
+
 import jax
 import jax.numpy as jnp
 from jax import lax
@@ -76,17 +79,25 @@
         step()
 
 
-def main_kernel(
-    x_ref, p_ref, q_ref, odd_row, even_row, even_col, odd_col,
-    g3_ref, b3_ref, w3_ref, wu_ref, bu_ref, g4_ref, w4_ref, b4_ref,
-    out_ref,
-    raw0, raw1, raw2, act0, act1, act2, actd0, actd1, actd2, halo0, halo1, halo2,
-    res0, res1, resd0, resd1, resh0, resh1, z0, z1, z2, s0, s1, fine0, fine1, fine2,
-    *, row_count, col_count, col_size,
-):
-    raw, act, act_d, halo_d = (raw0, raw1, raw2), (act0, act1, act2), (actd0, actd1, actd2), (halo0, halo1, halo2)
-    res, res_d, res_h = (res0, res1), (resd0, resd1), (resh0, resh1)
-    z4, s4, act4_d = (z0, z1, z2), (s0, s1), (fine0, fine1, fine2)
+FIRST = ("raw1", "act0", "act1", "actd0", "actd1")
+SHARED = (*FIRST, "raw2", "act2", "actd2", "res0", "res1", "resd0", "resd1")
+INNER = (2, COLS - 2)
+RIMS = ((0, 2), (COLS, 2))
+
+
+def stages(refs, row_count, col_count, col_size):
+    x_ref, p_ref, q_ref = refs.get("x"), refs.get("p"), refs.get("q")
+    odd_row, even_row = refs.get("odd_row"), refs.get("even_row")
+    even_col, odd_col = refs.get("even_col"), refs.get("odd_col")
+    w3_ref, wu_ref, w4_ref = refs.get("w3"), refs.get("wu"), refs.get("w4")
+    out_ref = refs.get("out")
+
+    def several(name, count):
+        return [refs.get(name + str(n)) for n in range(count)]
+
+    raw, act, act_d, halo_d = several("raw", 3), several("act", 3), several("actd", 3), several("halo", 3)
+    res, res_d, res_h = several("res", 2), several("resd", 2), several("resh", 2)
+    z4, s4, act4_d = several("z", 3), several("s", 2), several("fine", 3)
     row = lax.axis_index("row")
     col = lax.axis_index("section") * col_size + lax.axis_index("col")
     row_odd = lax.rem(row, 2) == 1
@@ -121,7 +132,7 @@
     def pair_of(ref, *index):
         return jnp.concatenate([ref[(0,) + index], ref[(1,) + index]], axis=1).astype(BF16)
 
-    g3 = g3_ref[...]
+    g3 = refs["g3"][...]
     gains = (
         g3[:, 0:128],
         jnp.concatenate([g3[:, 128:192], g3[:, 0:64]], axis=1),
@@ -169,16 +180,18 @@
             rows = pl.ds((half * WIDE + dx) * EXT + ext, 16, stride=EXT)
             halo_d[group][place, half * 16 : (half + 1) * 16, :] = pair_of(act[group], rows, slice(None))
 
-    def coarse_steps(group):
-        for jj in range(WIDE):
+    def coarse_steps(group, columns):
+        for jj in columns:
             yield lambda jj=jj: (load_column(group, jj), shift_column(group, jj))
+
+    def row_steps(group):
         for place in range(18):
             yield lambda place=place: gather_rows(group, place)
 
-    mid = MID * ROWS
-    center = [[None, None], [None, None]]
-
-    def conv_three(p, k):
+    center = {}
+    edges = {}
+
+    def conv_three(frames, runs):
         kernels = []
         pieces = []
         for dy in range(3):
@@ -186,26 +199,31 @@
                 kernels.append(w3_ref[3 * dy + dx])
                 for t in range(3):
                     parts = []
-                    group, half = p + (k + t) // 2, (k + t) % 2
-                    at = (half * WIDE + dx) * ROWS
-                    parts.append(act_d[group][dy, at : at + MID * ROWS, :])
-                    for side in range(2):
-                        place = 6 * dx + 3 * side + dy
-                        parts.append(halo_d[group][place, half * 16 : (half + 1) * 16, :])
+                    for p, k in frames:
+                        group, half = p + (k + t) // 2, (k + t) % 2
+                        for start, count in runs:
+                            at = (half * WIDE + start + dx) * ROWS
+                            parts.append(act_d[group][dy, at : at + count * ROWS, :])
+                        for side in range(2):
+                            place = 6 * dx + 3 * side + dy
+                            parts.append(halo_d[group][place, half * 16 : (half + 1) * 16, :])
                     pieces.append(jnp.concatenate(parts, axis=0))
         got = nt_dot(jnp.concatenate(pieces, axis=1), jnp.concatenate(kernels, axis=1))
-        center[p][k] = got
-
-    def conv_three_steps(p):
-        for k in range(2):
-            yield lambda k=k: conv_three(p, k)
-
-    b3 = b3_ref[...]
-    column = lax.broadcasted_iota(jnp.int32, (MID, 1), 0)
-    cols_in = jnp.logical_and(
-        jnp.logical_or(column > 0, jnp.logical_not(first_col)),
-        jnp.logical_or(column < MID - 1, jnp.logical_not(last_col)),
-    )
+        at = 0
+        for p, k in frames:
+            for start, count in runs:
+                for jm in range(start, start + count):
+                    center[p, k, jm] = got[at : at + ROWS]
+                    at += ROWS
+            for side in range(2):
+                edges[p, k, side] = got[at : at + 16]
+                at += 16
+
+    def conv_three_steps(runs, *batches):
+        for frames in batches:
+            yield lambda frames=frames: conv_three(frames, runs)
+
+    b3 = refs["b3"][...] if "b3" in refs else None
 
     def put_res(p, rows, value):
         res[p][0, rows, :] = value[:, 0:128]
@@ -217,7 +235,7 @@
         tiles = [raw[p + 1][q, at : at + ROWS, :] for q in range(3)]
         for k, skip in enumerate(split_pair(*tiles)):
             slab = k * MID + jm
-            value = center[p][k][jm * ROWS : (jm + 1) * ROWS] + b3
+            value = center[p, k, jm] + b3
             value = rounded(value + jnp.concatenate([skip[0], skip[1][:, 0:64]], axis=1))
             if jm == 0:
                 value = keep(jnp.logical_not(first_col), value)
@@ -225,16 +243,20 @@
                 value = keep(jnp.logical_not(last_col), value)
             put_res(p, pl.ds(slab * EXT + 1, ROWS), value)
 
-    def result_rows(p, side):
-        rows_in = jnp.logical_not(last_row if side else first_row)
-        ext = 18 if side else 17
-        tiles = [raw[p + 1][q, pl.ds(EXT + ext, MID, stride=EXT), :] for q in range(3)]
+    def result_rows(p, side, start, count):
+        inside = jnp.logical_not(last_row if side else first_row)
+        column = lax.broadcasted_iota(jnp.int32, (count, 1), 0) + start
+        if start == 0:
+            inside = jnp.logical_and(inside, jnp.logical_or(column > 0, jnp.logical_not(first_col)))
+        if start + count == MID:
+            inside = jnp.logical_and(inside, jnp.logical_or(column < MID - 1, jnp.logical_not(last_col)))
+        rows = pl.ds((start + 1) * EXT + (18 if side else 17), count, stride=EXT)
+        tiles = [raw[p + 1][q, rows, :] for q in range(3)]
         for k, skip in enumerate(split_pair(*tiles)):
-            at = mid + side * 16
-            value = center[p][k][at : at + MID] + b3
+            value = edges[p, k, side][start : start + count] + b3
             value = rounded(value + jnp.concatenate([skip[0], skip[1][:, 0:64]], axis=1))
-            value = keep(jnp.logical_and(cols_in, rows_in), value)
-            put_res(p, pl.ds(k * MID * EXT + (17 if side else 0), MID, stride=EXT), value)
+            at = (k * MID + start) * EXT + (17 if side else 0)
+            put_res(p, pl.ds(at, count, stride=EXT), keep(inside, value))
 
     def shift_result(p, jm):
         for k in range(2):
@@ -249,11 +271,14 @@
             rows = pl.ds((k * MID + c) * EXT + ROWS + r, 16, stride=EXT)
             res_h[p][place, k * 16 : (k + 1) * 16, :] = pair_of(res[p], rows, slice(None))
 
-    def result_steps(p):
-        for side in range(2):
-            yield lambda side=side: result_rows(p, side)
-        for jm in range(MID):
-            yield lambda jm=jm: (result_column(p, jm), shift_result(p, jm))
+    def result_steps(p, runs):
+        for start, count in runs:
+            for side in range(2):
+                yield lambda side=side, start=start, count=count: result_rows(p, side, start, count)
+            for jm in range(start, start + count):
+                yield lambda jm=jm: (result_column(p, jm), shift_result(p, jm))
+
+    def gather_steps(p):
         for place in range(4):
             yield lambda place=place: gather_result(p, place)
 
@@ -274,8 +299,11 @@
         for k in range(2):
             yield lambda k=k: conv_up(p, k)
 
-    bias_up = jnp.concatenate([bu_ref[...], jnp.zeros((1, 32), F32)], axis=1)
-    g4 = jnp.concatenate([g4_ref[...], jnp.zeros((1, 32), F32)], axis=1)
+    def padded(name):
+        return jnp.concatenate([refs[name][...], jnp.zeros((1, 32), F32)], axis=1)
+
+    bias_up = padded("bu") if "bu" in refs else None
+    g4 = padded("g4") if "g4" in refs else None
 
     def act_four(value):
         square = jnp.sum(value * value, axis=1, keepdims=True)
@@ -379,8 +407,7 @@
         for half in range(2):
             yield lambda half=half: conv_four(p, half)
 
-    b4 = b4_ref[...]
-    bias_four = jnp.concatenate([b4, b4], axis=1)
+    bias_four = jnp.concatenate([refs["b4"][...]] * 2, axis=1) if "b4" in refs else None
     first = lane_mask(FROWS, C4)
 
     def out_column(p, fx):
@@ -395,16 +422,54 @@
         for fx in range(2 * COLS):
             yield lambda fx=fx: out_column(p, fx)
 
-    weave(coarse_steps(0), coarse_steps(1))
-    weave(conv_three_steps(0), coarse_steps(2), cached_steps())
-    weave(conv_three_steps(1), result_steps(0))
-    weave(conv_up_steps(0))
-    weave(fine_steps(0), result_steps(1))
-    weave(conv_up_steps(1))
-    weave(conv_four_steps(0), fine_steps(1))
-    later = list(conv_four_steps(1))
-    ends = list(out_steps(1))
-    weave(later[:1], out_steps(0))
+    return types.SimpleNamespace(**locals())
+
+
+OWN = range(2, WIDE - 2)
+
+
+def first_inner_kernel(names, sizes, *all_refs):
+    refs = dict(zip(names, all_refs))
+    col = lax.axis_index("section") * sizes[2] + lax.axis_index("col")
+
+    @pl.when(col == sizes[1] // 2)
+    def _():
+        do = stages(refs, *sizes)
+        weave(do.coarse_steps(0, OWN), do.coarse_steps(1, OWN))
+
+
+def inner_kernel(names, sizes, *all_refs):
+    refs = dict(zip(names, all_refs))
+    col = lax.axis_index("section") * sizes[2] + lax.axis_index("col")
+
+    @pl.when(col != sizes[1] // 2)
+    def _():
+        do = stages(refs, *sizes)
+        weave(do.coarse_steps(0, OWN), do.coarse_steps(1, OWN))
+
+    do = stages(refs, *sizes)
+    weave(do.row_steps(0), do.row_steps(1))
+    weave(do.conv_three_steps([INNER], [(0, 0), (0, 1)]), do.coarse_steps(2, OWN))
+    weave(do.row_steps(2))
+    weave(do.conv_three_steps([INNER], [(1, 0), (1, 1)]), do.result_steps(0, [INNER]))
+    weave(do.result_steps(1, [INNER]))
+
+
+def main_kernel(names, sizes, *all_refs):
+    do = stages(dict(zip(names, all_refs)), *sizes)
+    sides = (0, 1, WIDE - 2, WIDE - 1)
+    weave(*[do.coarse_steps(group, sides) for group in range(3)])
+    weave(*[do.row_steps(group) for group in range(3)])
+    weave(do.conv_three_steps(RIMS, [(0, 0), (0, 1)], [(1, 0), (1, 1)]), do.cached_steps())
+    weave(do.result_steps(0, RIMS))
+    weave(do.gather_steps(0))
+    weave(do.conv_up_steps(0), do.result_steps(1, RIMS))
+    weave(do.gather_steps(1))
+    weave(do.conv_up_steps(1), do.fine_steps(0))
+    weave(do.conv_four_steps(0), do.fine_steps(1))
+    later = list(do.conv_four_steps(1))
+    ends = list(do.out_steps(1))
+    weave(later[:1], do.out_steps(0))
     weave(later[1:], ends[:10])
     weave(ends[10:])
 
@@ -530,10 +595,13 @@
         start += width
 
 
-def call(kernel, operands, outputs, scratch, megabytes, moved=0, unread=0, space=pl.ANY):
+def call(kernel, operands, outputs, scratch, megabytes, moved=0, unread=0, space=pl.ANY, aliases=None):
     cost = pl.CostEstimate(flops=moved, bytes_accessed=moved, transcendentals=0) if moved else None
     vmem = pl.BlockSpec(memory_space=pltpu.VMEM)
-    shapes = [jax.ShapeDtypeStruct(shape, BF16) for shape in outputs]
+    shapes = [
+        shape if isinstance(shape, jax.ShapeDtypeStruct) else jax.ShapeDtypeStruct(shape, BF16)
+        for shape in outputs
+    ]
     got = pl.pallas_call(
         kernel,
         out_shape=shapes,
@@ -541,6 +609,7 @@
         out_specs=[vmem] * len(outputs),
         scratch_shapes=scratch,
         cost_estimate=cost,
+        input_output_aliases=aliases or {},
         compiler_params=pltpu.CompilerParams(vmem_limit_bytes=megabytes * 1024 * 1024),
     )(*operands)
     return got[0] if len(outputs) == 1 else got
@@ -590,6 +659,43 @@
         [pltpu.VMEM((2, 40 * C3, 128), F32)],
         16, 8_000_000,
     )
+    col_strip = (ROWS + 4, QAT + 2 * COLQ)
+
+    def swap_columns(parity, after):
+        def col_kernel(*refs):
+            col_strips_kernel(*refs, col_size=col_size, parity=1 - parity)
+
+        strip = call(col_kernel, (*tile, odd_row, even_row, after), [col_strip], [], 4, unread=1)
+        return lax.ppermute(strip, ("section", "col"), swap_pairs(col_count, parity))
+
+    sizes = (row_count, col_count, col_size)
+    rows = (section_input, cache_three, odd_row, even_row)
+    params = (gain_three.reshape(1, C3), bias_three.reshape(1, C3), w3)
+    names = ("x", "p", "odd_row", "even_row", "g3", "b3", "w3")
+
+    def block(shape, dtype=F32):
+        return jax.ShapeDtypeStruct(shape, dtype)
+
+    raw = block((3, 16 * EXT, 128))
+    act = block((2, (2 * WIDE + 4) * EXT, 128))
+    act_d = block((3, 2 * WIDE * ROWS, 256), BF16)
+    res = block((2, (2 * MID + 5) * EXT, 128))
+    res_d = block((2, 2 * MID * ROWS, 256), BF16)
+    first = [raw, act, act, act_d, act_d]
+    rest = [raw, act, act_d, res, res, res_d, res_d]
+    halo = pltpu.VMEM((18, 2 * 16, 256), BF16)
+    inner_scratch = [pltpu.VMEM(raw.shape, F32), halo, halo, halo]
+    scratch_names = ("raw0", "halo0", "halo1", "halo2")
+
+    even_col = swap_columns(0, w3)
+    *held, token = call(
+        functools.partial(first_inner_kernel, (*names[:-2], *FIRST, "token", "raw0"), sizes),
+        (*rows, *params[:1]),
+        [*first, (16, 128)],
+        inner_scratch[:1],
+        8, 2_000_000,
+    )
+    odd_col = swap_columns(1, token)
     wu, w4 = call(
         prep_four_kernel,
         (weight_up, weight_four),
@@ -601,37 +707,42 @@
         16, 8_000_000,
     )
 
-    col_strip = (ROWS + 4, QAT + 2 * COLQ)
-
-    def swap_columns(parity):
-        def col_kernel(*refs):
-            col_strips_kernel(*refs, col_size=col_size, parity=1 - parity)
-
-        strip = call(col_kernel, (*tile, odd_row, even_row, w3), [col_strip], [], 4, unread=1)
-        return lax.ppermute(strip, ("section", "col"), swap_pairs(col_count, parity))
-
-    even_col = swap_columns(0)
-    odd_col = swap_columns(1)
-
-    def kernel(*refs):
-        main_kernel(*refs, row_count=row_count, col_count=col_count, col_size=col_size)
+    held = call(
+        functools.partial(
+            inner_kernel, (*names, *["_" + name for name in FIRST], *SHARED, *scratch_names), sizes
+        ),
+        (*rows, *params, *held),
+        [*first, *rest],
+        inner_scratch,
+        16, 8_000_000,
+        aliases={len(names) + n: n for n in range(len(first))},
+    )
 
     operands = (
         *tile, odd_row, even_row, even_col, odd_col,
-        gain_three.reshape(1, C3), bias_three.reshape(1, C3), w3, wu, bias_up.reshape(1, C4),
-        gain_four.reshape(1, C4), w4, bias_four.reshape(1, C4),
-    )
-    scratch = [pltpu.VMEM((3, 16 * EXT, 128), F32)] * 3
-    scratch += [pltpu.VMEM((2, (2 * WIDE + 4) * EXT, 128), F32)] * 3
-    scratch += [pltpu.VMEM((3, 2 * WIDE * ROWS, 256), BF16)] * 3
-    scratch += [pltpu.VMEM((18, 2 * 16, 256), BF16)] * 3
-    scratch += [pltpu.VMEM((2, (2 * MID + 5) * EXT, 128), F32)] * 2
-    scratch += [pltpu.VMEM((2, 2 * MID * ROWS, 256), BF16)] * 2
+        *params, wu, bias_up.reshape(1, C4), gain_four.reshape(1, C4), w4, bias_four.reshape(1, C4),
+    )
+    names = (
+        "x", "p", "q", "odd_row", "even_row", "even_col", "odd_col",
+        "g3", "b3", "w3", "wu", "bu", "g4", "w4", "b4",
+    )
+    scratch = list(inner_scratch)
     scratch += [pltpu.VMEM((4, 2 * 16, 256), BF16)] * 2
     scratch += [pltpu.VMEM((2, FINE * FEXT, 128), F32)] * 3
     scratch += [pltpu.VMEM((2, FINE * FEXT, 128), F32)] * 2
     scratch += [pltpu.VMEM((3, FINE * FROWS, 256), BF16)] * 3
-    return call(kernel, operands, [(FROWS, 2 * COLS * FRAMES * C4)], scratch, 32)
+    scratch_names += ("resh0", "resh1", "z0", "z1", "z2", "s0", "s1", "fine0", "fine1", "fine2")
+    got = call(
+        functools.partial(
+            main_kernel, (*names, *["_" + name for name in SHARED], "out", *SHARED, *scratch_names), sizes
+        ),
+        (*operands, *held),
+        [(FROWS, 2 * COLS * FRAMES * C4), *first, *rest],
+        scratch,
+        24,
+        aliases={len(names) + n: n + 1 for n in range(len(SHARED))},
+    )
+    return got[0]
 
 
 def solution(mesh):

time: 29.7 us -> 28.7 us (0.966)
  Pallas kernels: 13.5 us -> 15.5 us
  waiting for transfers between devices: 1.85 us -> 0.05 us
  starting transfers between devices: 12.2 us -> 11 us
    pallas_call x6 -> x8, Pallas kernels: 13.5 us -> 15.5 us  [call(): pl.pallas_call(kernel, out_shape=shapes, in_specs=[vmem] * (len(operands)...]
    ppermute x2, waiting for transfers between devices: 1.85 us -> 0.05 us  [swap_columns(): lax.ppermute(strip, ('section', 'col'), swap_pairs(col_count, parity))]
    ppermute x2, starting transfers between devices: 7 us -> 5.82 us  [swap_columns(): lax.ppermute(strip, ('section', 'col'), swap_pairs(col_count, parity))]
  transfers between devices with their start and end apart: 4 -> 4, of which waited for: 1 -> 0; matrix products, arithmetic and copies ran while one was open for 0% -> 0% of each run, Pallas kernels for 8% -> 21%
where the time goes in v3:
time: 28.7 us; the launch traced here: 28.5 us
  Pallas kernels  15.5 us (54%)
  starting transfers between devices  11 us (38%)
  local copies, waits for them, and re-layouts  1.73 us (6%)
    pallas_call x8, Pallas kernels, call(): pl.pallas_call(kernel, out_shape=shapes, in_specs=[vmem] * (len(operands)...  15.5 us
    ppermute x2, starting transfers between devices, swap_columns(): lax.ppermute(strip, ('section', 'col'), swap_pairs(col_count, parity))  5.82 us
    ppermute x1, starting transfers between devices, shards(): even_row = lax.ppermute(even_strip, 'row', swap_pairs(row_count, 0))  4.56 us
    unnamed x22, local copies, waits for them, and re-layouts  1.73 us
    ppermute x1, starting transfers between devices, shards(): odd_row = lax.ppermute(odd_strip, 'row', swap_pairs(row_count, 1))  0.66 us
  transfers between devices with their start and end apart: 4, of which 0 were waited for; matrix products, arithmetic and copies ran while one was open for 0% of the time, Pallas kernels for 21%

profile of v3, /device:TPU:1, one launch (start us, length us, event | category | flops | bytes accessed | tf_op | source)
XLA Modules:
  0.0 28.5 jit_solution(5380546113544303811)
XLA Ops:
  0.0 1.9 %shard_map.109 = (bf16[2,15360]{1,0:T(2,128)(2,1)}, bf16[2,15360]{1,0:T(2,128)(2,1)}) custom-call(bf16[16,7680]{1,0:T(8,128)(2,1)} %all_refs_0_.5, bf16[16,3840]{1,0:T(8,128)(2,1)} %all_refs_1_.5, bf16[32,3840]{1,0:T(8,128)(2,1)} %all_refs_2_.1), custom_call_target="tpu_custom_call" | custom-call | tf_op jit(solution)/shard_map/pallas_call | solution.py:605
  1.9 0.7 %collective-permute-start = (bf16[2,15360]{1,0:T(2,128)(2,1)}, bf16[2,15360]{1,0:T(2,128)(2,1)S(1)}, u32[]{:S(2)}, u32[]{:S(2)}) collective-permute-start(bf16[2,15360]{1,0:T(2,128)(2,1)} %get-tuple-element.28), channel_id=1, source_target_pairs={{4,8},{8,4},{5,9},{9,5},{6,10},{10,6},{7,11},{11,7},{20,24},{24,20... | collective-permute-start | bytes 184328 | tf_op jit(solution)/shard_map/ppermute | solution.py:653
  2.5 0.0 copy-start
  2.5 0.0 copy-start.1
  2.6 0.0 copy-start.2
  2.6 4.6 %collective-permute-start.1 = (bf16[2,15360]{1,0:T(2,128)(2,1)}, bf16[2,15360]{1,0:T(2,128)(2,1)S(1)}, u32[]{:S(2)}, u32[]{:S(2)}) collective-permute-start(bf16[2,15360]{1,0:T(2,128)(2,1)} %get-tuple-element.29), channel_id=1, source_target_pairs={{0,4},{4,0},{8,12},{12,8},{1,5},{5,1},{9,13},{13,9},{2,6},{6,2},{1... | collective-permute-start | bytes 184328 | tf_op jit(solution)/shard_map/ppermute | solution.py:652
  7.1 0.0 copy-start.3
  7.1 1.7 %copy-done.3 = bf16[27,36864]{1,0:T(8,128)(2,1)S(1)} copy-done((bf16[27,36864]{1,0:T(8,128)(2,1)S(1)}, bf16[27,36864]{1,0:T(8,128)(2,1)}, u32[]{:S(2)}) %copy-start.3) | copy-done | bytes 1990680
  8.8 1.3 %shard_map.110.refs_5_.all_refs_6_.all_refs_9_ = bf16[9,192,768]{2,1,0:T(8,128)(2,1)S(1)} custom-call(bf16[27,36864]{1,0:T(8,128)(2,1)S(1)} %copy-done.3), custom_call_target="tpu_custom_call" | custom-call | flops 8000000 | bytes 8000000 | tf_op jit(solution)/shard_map/pallas_call | solution.py:605
  10.1 0.0 copy-start.6
  10.1 0.0 copy-start.4
  10.1 0.0 copy-start.5
  10.1 0.0 copy-start.7
  10.1 0.0 collective-permute-done.refs_3_.all_refs_2_.all_refs_3_
  10.1 0.0 collective-permute-done.1.refs_4_.all_refs_3_.all_refs_4_
  10.1 0.0 copy-done
  10.2 0.0 copy-done.1
  10.2 0.0 copy-done.2
  10.2 0.1 shard_map.111
  10.3 1.3 %collective-permute-start.2 = (bf16[20,2688]{1,0:T(8,128)(2,1)S(1)}, bf16[20,2688]{1,0:T(8,128)(2,1)S(1)}, u32[]{:S(2)}, u32[]{:S(2)}) collective-permute-start(bf16[20,2688]{1,0:T(8,128)(2,1)S(1)} %shard_map.111), channel_id=1, source_target_pairs={{0,1},{1,0},{2,3},{3,2},{16,17},{17,16},{18,19},{19,18},{4,5},{5,4... | collective-permute-start | bytes 322568 | tf_op jit(solution)/shard_map/ppermute | solution.py:669
  11.6 0.0 copy-done.6
  11.6 1.1 %shard_map.112 = (f32[3,384,128]{2,1,0:T(8,128)S(1)}, f32[2,768,128]{2,1,0:T(8,128)S(1)}, f32[2,768,128]{2,1,0:T(8,128)S(1)}, bf16[3,448,256]{2,1,0:T(8,128)(2,1...) custom-call(bf16[16,7680]{1,0:T(8,128)(2,1)S(1)} %copy-done, bf16[16,3840]{1,0:T(8,128)(2,1)S(1)} %copy-done.1, ...), custom_call_target="tpu_custom_call" | custom-call | flops 2000000 | bytes 2000000 | tf_op jit(solution)/shard_map/pallas_call | solution.py:605
  12.7 0.1 shard_map.113
  12.9 4.5 %collective-permute-start.3 = (bf16[20,2688]{1,0:T(8,128)(2,1)S(1)}, bf16[20,2688]{1,0:T(8,128)(2,1)S(1)}, u32[]{:S(2)}, u32[]{:S(2)}) collective-permute-start(bf16[20,2688]{1,0:T(8,128)(2,1)S(1)} %shard_map.113), channel_id=1, source_target_pairs={{1,2},{2,1},{3,16},{16,3},{17,18},{18,17},{5,6},{6,5},{7,20},{20,7... | collective-permute-start | bytes 322568 | tf_op jit(solution)/shard_map/ppermute | solution.py:669
  17.4 0.0 copy-done.4
  17.4 0.0 copy-done.5
  17.4 0.8 %shard_map.114 = (bf16[512,1024]{1,0:T(8,128)(2,1)S(1)}, bf16[3,192,1536]{2,1,0:T(8,128)(2,1)S(1)}) custom-call(bf16[9,18432]{1,0:T(8,128)(2,1)S(1)} %copy-done.4, bf16[27,9216]{1,0:T(8,128)(2,1)S(1)} %copy-done.5), custom_call_target="tpu_custom_call" | custom-call | flops 8000000 | bytes 8000000 | tf_op jit(solution)/shard_map/pallas_call | solution.py:605
  18.2 0.0 copy-done.7
  18.3 0.0 copy-start.8
  18.3 0.0 copy-start.9
  18.3 0.0 copy-start.10
  18.3 2.7 %shard_map.115 = (f32[3,384,128]{2,1,0:T(8,128)S(1)}, f32[2,768,128]{2,1,0:T(8,128)S(1)}, f32[2,768,128]{2,1,0:T(8,128)S(1)}, bf16[3,448,256]{2,1,0:T(8,128)(2,1...) custom-call(bf16[16,7680]{1,0:T(8,128)(2,1)S(1)} %copy-done, ...), custom_call_target="tpu_custom_call", output_to_operand_aliasing={{0}: (7, {}), {1}: (8, {}), {2}: (9, {}), {3}: (10, {}), {4... | custom-call | flops 8000000 | bytes 8000000 | tf_op jit(solution)/shard_map/pallas_call | solution.py:605
  21.0 0.0 collective-permute-done.2.all_refs_5_
  21.0 0.0 collective-permute-done.3.all_refs_6_
  21.0 0.0 copy-done.8
  21.0 0.0 copy-done.9
  21.0 0.0 copy-done.10
  21.0 7.5 %shard_map.116 = (bf16[32,7680]{1,0:T(8,128)(2,1)}, f32[3,384,128]{2,1,0:T(8,128)S(1)}, f32[2,768,128]{2,1,0:T(8,128)S(1)}, f32[2,768,128]{2,1,0:T(8,128)S(1)}, ...) custom-call(bf16[16,7680]{1,0:T(8,128)(2,1)S(1)} %copy-done, ...), custom_call_target="tpu_custom_call", output_to_operand_aliasing={{1}: (15, {}), {2}: (16, {}), {3}: (17, {}), {4}: (18, {}),... | custom-call | tf_op jit(solution)/shard_map/pallas_call | solution.py:605
Async XLA Ops:
  1.9 8.3 %collective-permute-start = (bf16[2,15360]{1,0:T(2,128)(2,1)}, bf16[2,15360]{1,0:T(2,128)(2,1)S(1)}, u32[]{:S(2)}, u32[]{:S(2)}) collective-permute-start(bf16[2,15360]{1,0:T(2,128)(2,1)} %get-tuple-element.28), channel_id=1, source_target_pairs={{4,8},{8,4},{5,9},{9,5},{6,10},{10,6},{7,11},{11,7},{20,24},{24,20... | collective-permute-start | bytes 184328 | tf_op jit(solution)/shard_map/ppermute | solution.py:653
  2.5 7.6 %copy-start = (bf16[16,7680]{1,0:T(8,128)(2,1)S(1)}, bf16[16,7680]{1,0:T(8,128)(2,1)}, u32[]{:S(2)}) copy-start(bf16[16,7680]{1,0:T(8,128)(2,1)} %all_refs_0_.5) | copy-start | bytes 737284
  2.5 7.6 %copy-start.1 = (bf16[16,3840]{1,0:T(8,128)(2,1)S(1)}, bf16[16,3840]{1,0:T(8,128)(2,1)}, u32[]{:S(2)}) copy-start(bf16[16,3840]{1,0:T(8,128)(2,1)} %all_refs_1_.5) | copy-start | bytes 368644
  2.6 7.6 %copy-start.2 = (bf16[32,3840]{1,0:T(8,128)(2,1)S(1)}, bf16[32,3840]{1,0:T(8,128)(2,1)}, u32[]{:S(2)}) copy-start(bf16[32,3840]{1,0:T(8,128)(2,1)} %all_refs_2_.1) | copy-start | bytes 737284
  2.6 7.6 %collective-permute-start.1 = (bf16[2,15360]{1,0:T(2,128)(2,1)}, bf16[2,15360]{1,0:T(2,128)(2,1)S(1)}, u32[]{:S(2)}, u32[]{:S(2)}) collective-permute-start(bf16[2,15360]{1,0:T(2,128)(2,1)} %get-tuple-element.29), channel_id=1, source_target_pairs={{0,4},{4,0},{8,12},{12,8},{1,5},{5,1},{9,13},{13,9},{2,6},{6,2},{1... | collective-permute-start | bytes 184328 | tf_op jit(solution)/shard_map/ppermute | solution.py:652
  7.1 1.7 %copy-start.3 = (bf16[27,36864]{1,0:T(8,128)(2,1)S(1)}, bf16[27,36864]{1,0:T(8,128)(2,1)}, u32[]{:S(2)}) copy-start(bf16[27,36864]{1,0:T(8,128)(2,1)} %flat_ref.1) | copy-start | bytes 5971972
  10.1 1.6 %copy-start.6 = (f32[192]{0:T(256)S(1)}, f32[192]{0:T(256)}, u32[]{:S(2)}) copy-start(f32[192]{0:T(256)} %param.13) | copy-start | bytes 2308
  10.1 7.3 %copy-start.4 = (bf16[9,18432]{1,0:T(8,128)(2,1)S(1)}, bf16[9,18432]{1,0:T(8,128)(2,1)}, u32[]{:S(2)}) copy-start(bf16[9,18432]{1,0:T(8,128)(2,1)} %up_ref.1) | copy-start | bytes 995332
  10.1 7.3 %copy-start.5 = (bf16[27,9216]{1,0:T(8,128)(2,1)S(1)}, bf16[27,9216]{1,0:T(8,128)(2,1)}, u32[]{:S(2)}) copy-start(bf16[27,9216]{1,0:T(8,128)(2,1)} %four_ref.1) | copy-start | bytes 1492996
  10.1 8.1 %copy-start.7 = (f32[192]{0:T(256)S(1)}, f32[192]{0:T(256)}, u32[]{:S(2)}) copy-start(f32[192]{0:T(256)} %param.14) | copy-start | bytes 2308
  10.3 10.6 %collective-permute-start.2 = (bf16[20,2688]{1,0:T(8,128)(2,1)S(1)}, bf16[20,2688]{1,0:T(8,128)(2,1)S(1)}, u32[]{:S(2)}, u32[]{:S(2)}) collective-permute-start(bf16[20,2688]{1,0:T(8,128)(2,1)S(1)} %shard_map.111), channel_id=1, source_target_pairs={{0,1},{1,0},{2,3},{3,2},{16,17},{17,16},{18,19},{19,18},{4,5},{5,4... | collective-permute-start | bytes 322568 | tf_op jit(solution)/shard_map/ppermute | solution.py:669
  12.9 8.2 %collective-permute-start.3 = (bf16[20,2688]{1,0:T(8,128)(2,1)S(1)}, bf16[20,2688]{1,0:T(8,128)(2,1)S(1)}, u32[]{:S(2)}, u32[]{:S(2)}) collective-permute-start(bf16[20,2688]{1,0:T(8,128)(2,1)S(1)} %shard_map.113), channel_id=1, source_target_pairs={{1,2},{2,1},{3,16},{16,3},{17,18},{18,17},{5,6},{6,5},{7,20},{20,7... | collective-permute-start | bytes 322568 | tf_op jit(solution)/shard_map/ppermute | solution.py:669
  18.3 2.8 %copy-start.8 = (f32[96]{0:T(128)S(1)}, f32[96]{0:T(128)}, u32[]{:S(2)}) copy-start(f32[96]{0:T(128)} %param.17) | copy-start | bytes 1156
  18.3 2.8 %copy-start.9 = (f32[96]{0:T(128)S(1)}, f32[96]{0:T(128)}, u32[]{:S(2)}) copy-start(f32[96]{0:T(128)} %param.19) | copy-start | bytes 1156
  18.3 2.8 %copy-start.10 = (f32[96]{0:T(128)S(1)}, f32[96]{0:T(128)}, u32[]{:S(2)}) copy-start(f32[96]{0:T(128)} %param.21) | copy-start | bytes 1156

commit v4 on v3

--- a/solution.py
+++ b/solution.py
@@ -83,6 +83,7 @@
 SHARED = (*FIRST, "raw2", "act2", "actd2", "res0", "res1", "resd0", "resd1")
 INNER = (2, COLS - 2)
 RIMS = ((0, 2), (COLS, 2))
+RIM_SLOTS = (0, 1, 2, 3, WIDE - 4, WIDE - 3, WIDE - 2, WIDE - 1)
 
 
 def stages(refs, row_count, col_count, col_size):
@@ -96,6 +97,7 @@
         return [refs.get(name + str(n)) for n in range(count)]
 
     raw, act, act_d, halo_d = several("raw", 3), several("act", 3), several("actd", 3), several("halo", 3)
+    rims = several("rim", 3)
     res, res_d, res_h = several("res", 2), several("resd", 2), several("resh", 2)
     z4, s4, act4_d = several("z", 3), several("s", 2), several("fine", 3)
     row = lax.axis_index("row")
@@ -139,7 +141,13 @@
         g3[:, 64:192],
     )
 
-    def load_column(group, jj):
+    def place_of(jj, rim):
+        if rim:
+            return rims, len(RIM_SLOTS), RIM_SLOTS.index(jj)
+        return act, WIDE, jj
+
+    def load_column(group, jj, rim):
+        held, slots, slot = place_of(jj, rim)
         base = jj * EXT
         for q in range(3):
             if 2 <= jj < WIDE - 2:
@@ -161,32 +169,51 @@
         if group:
             tiles = norm_pair(*tiles, gains)
         for half, pair in enumerate(split_pair(*tiles)):
-            at = (half * WIDE + jj) * EXT
+            at = (half * slots + slot) * EXT
             for q in range(2):
-                act[group][q, at : at + 2, :] = pair[q][16:18]
-                act[group][q, at + 2 : at + 18, :] = pair[q][0:16]
-                act[group][q, at + 18 : at + 20, :] = pair[q][18:20]
-
-    def shift_column(group, jj):
+                held[group][q, at : at + 2, :] = pair[q][16:18]
+                held[group][q, at + 2 : at + 18, :] = pair[q][0:16]
+                held[group][q, at + 18 : at + 20, :] = pair[q][18:20]
+
+    def copy_column(group, jj):
+        slot = RIM_SLOTS.index(jj)
+        for half in range(2):
+            source, target = (half * WIDE + jj) * EXT, (half * len(RIM_SLOTS) + slot) * EXT
+            for q in range(2):
+                rims[group][q, target : target + EXT, :] = act[group][q, source : source + EXT, :]
+
+    def shift_column(group, jj, rim):
+        held, slots, slot = place_of(jj, rim)
         for half in range(2):
             slab = half * WIDE + jj
             for dy in range(3):
-                rows = slice(slab * EXT + 1 + dy, slab * EXT + 1 + dy + ROWS)
-                act_d[group][dy, slab * ROWS : (slab + 1) * ROWS, :] = pair_of(act[group], rows, slice(None))
-
-    def gather_rows(group, place):
-        dx, ext = place // 6, (0, 1, 2, 17, 18, 19)[place % 6]
+                at = (half * slots + slot) * EXT + 1 + dy
+                both = pair_of(held[group], slice(at, at + ROWS), slice(None))
+                act_d[group][dy, slab * ROWS : (slab + 1) * ROWS, :] = both
+
+    def gather_rows(group, dx, dy, rim):
+        held, slots, start = (rims, len(RIM_SLOTS), 0) if rim else (act, WIDE, INNER[0])
         for half in range(2):
-            rows = pl.ds((half * WIDE + dx) * EXT + ext, 16, stride=EXT)
-            halo_d[group][place, half * 16 : (half + 1) * 16, :] = pair_of(act[group], rows, slice(None))
-
-    def coarse_steps(group, columns):
+            at = (half * slots + start + dx) * EXT + dy
+            tiles = []
+            for q in range(2):
+                sides = [held[group][q, pl.ds(at + skip, 8, stride=EXT), :] for skip in (0, 17)]
+                tiles.append(jnp.concatenate(sides, axis=0))
+            both = jnp.concatenate(tiles, axis=1).astype(BF16)
+            halo_d[group][3 * dx + dy, half * 16 : (half + 1) * 16, :] = both
+
+    def coarse_steps(group, columns, rim=False):
         for jj in columns:
-            yield lambda jj=jj: (load_column(group, jj), shift_column(group, jj))
-
-    def row_steps(group):
-        for place in range(18):
-            yield lambda place=place: gather_rows(group, place)
+            yield lambda jj=jj: (load_column(group, jj, rim), shift_column(group, jj, rim))
+
+    def copy_steps(group):
+        for jj in RIM_SLOTS[2:6]:
+            yield lambda jj=jj: copy_column(group, jj)
+
+    def row_steps(group, rim=False):
+        for dx in range(3):
+            for dy in range(3):
+                yield lambda dx=dx, dy=dy: gather_rows(group, dx, dy, rim)
 
     center = {}
     edges = {}
@@ -204,9 +231,7 @@
                         for start, count in runs:
                             at = (half * WIDE + start + dx) * ROWS
                             parts.append(act_d[group][dy, at : at + count * ROWS, :])
-                        for side in range(2):
-                            place = 6 * dx + 3 * side + dy
-                            parts.append(halo_d[group][place, half * 16 : (half + 1) * 16, :])
+                        parts.append(halo_d[group][3 * dx + dy, half * 16 : (half + 1) * 16, :])
                     pieces.append(jnp.concatenate(parts, axis=0))
         got = nt_dot(jnp.concatenate(pieces, axis=1), jnp.concatenate(kernels, axis=1))
         at = 0
@@ -215,9 +240,8 @@
                 for jm in range(start, start + count):
                     center[p, k, jm] = got[at : at + ROWS]
                     at += ROWS
-            for side in range(2):
-                edges[p, k, side] = got[at : at + 16]
-                at += 16
+            edges[p, k] = got[at : at + 16]
+            at += 16
 
     def conv_three_steps(runs, *batches):
         for frames in batches:
@@ -253,7 +277,8 @@
         rows = pl.ds((start + 1) * EXT + (18 if side else 17), count, stride=EXT)
         tiles = [raw[p + 1][q, rows, :] for q in range(3)]
         for k, skip in enumerate(split_pair(*tiles)):
-            value = edges[p, k, side][start : start + count] + b3
+            at = 8 * side + (4 if start == COLS else 0)
+            value = edges[p, k][at : at + count] + b3
             value = rounded(value + jnp.concatenate([skip[0], skip[1][:, 0:64]], axis=1))
             at = (k * MID + start) * EXT + (17 if side else 0)
             put_res(p, pl.ds(at, count, stride=EXT), keep(inside, value))
@@ -458,14 +483,17 @@
 def main_kernel(names, sizes, *all_refs):
     do = stages(dict(zip(names, all_refs)), *sizes)
     sides = (0, 1, WIDE - 2, WIDE - 1)
-    weave(*[do.coarse_steps(group, sides) for group in range(3)])
-    weave(*[do.row_steps(group) for group in range(3)])
+    weave(*[do.copy_steps(group) for group in range(3)])
+    weave(*[do.coarse_steps(group, sides, True) for group in range(3)])
+    weave(*[do.row_steps(group, True) for group in range(3)])
     weave(do.conv_three_steps(RIMS, [(0, 0), (0, 1)], [(1, 0), (1, 1)]), do.cached_steps())
     weave(do.result_steps(0, RIMS))
     weave(do.gather_steps(0))
-    weave(do.conv_up_steps(0), do.result_steps(1, RIMS))
+    weave(do.result_steps(1, RIMS))
     weave(do.gather_steps(1))
-    weave(do.conv_up_steps(1), do.fine_steps(0))
+    weave(do.conv_up_steps(0))
+    weave(do.conv_up_steps(1))
+    weave(do.fine_steps(0))
     weave(do.conv_four_steps(0), do.fine_steps(1))
     later = list(do.conv_four_steps(1))
     ends = list(do.out_steps(1))
@@ -683,7 +711,7 @@
     res_d = block((2, 2 * MID * ROWS, 256), BF16)
     first = [raw, act, act, act_d, act_d]
     rest = [raw, act, act_d, res, res, res_d, res_d]
-    halo = pltpu.VMEM((18, 2 * 16, 256), BF16)
+    halo = pltpu.VMEM((9, 2 * 16, 256), BF16)
     inner_scratch = [pltpu.VMEM(raw.shape, F32), halo, halo, halo]
     scratch_names = ("raw0", "halo0", "halo1", "halo2")
 
@@ -727,11 +755,12 @@
         "g3", "b3", "w3", "wu", "bu", "g4", "w4", "b4",
     )
     scratch = list(inner_scratch)
+    scratch += [pltpu.VMEM((2, (2 * len(RIM_SLOTS) + 2) * EXT, 128), F32)] * 3
     scratch += [pltpu.VMEM((4, 2 * 16, 256), BF16)] * 2
     scratch += [pltpu.VMEM((2, FINE * FEXT, 128), F32)] * 3
     scratch += [pltpu.VMEM((2, FINE * FEXT, 128), F32)] * 2
     scratch += [pltpu.VMEM((3, FINE * FROWS, 256), BF16)] * 3
-    scratch_names += ("resh0", "resh1", "z0", "z1", "z2", "s0", "s1", "fine0", "fine1", "fine2")
+    scratch_names += ("rim0", "rim1", "rim2", "resh0", "resh1", "z0", "z1", "z2", "s0", "s1", "fine0", "fine1", "fine2")
     got = call(
         functools.partial(
             main_kernel, (*names, *["_" + name for name in SHARED], "out", *SHARED, *scratch_names), sizes

time: 28.7 us -> 28.7 us (level)
  Pallas kernels: 15.5 us -> 15.2 us
  transfers between devices with their start and end apart: 4 -> 4, of which waited for: 0 -> 1; matrix products, arithmetic and copies ran while one was open for 0% -> 0% of each run, Pallas kernels for 21% -> 20%
where the time goes in v4:
time: 28.7 us; the launch traced here: 28.5 us
  Pallas kernels  15.2 us (53%)
  starting transfers between devices  11 us (38%)
  local copies, waits for them, and re-layouts  1.73 us (6%)
  waiting for transfers between devices  0.3 us (1%)
    pallas_call x8, Pallas kernels, call(): pl.pallas_call(kernel, out_shape=shapes, in_specs=[vmem] * (len(operands)...  15.2 us
    ppermute x2, starting transfers between devices, swap_columns(): lax.ppermute(strip, ('section', 'col'), swap_pairs(col_count, parity))  5.82 us
    ppermute x1, starting transfers between devices, shards(): even_row = lax.ppermute(even_strip, 'row', swap_pairs(row_count, 0))  4.56 us
    unnamed x22, local copies, waits for them, and re-layouts  1.73 us
    ppermute x1, starting transfers between devices, shards(): odd_row = lax.ppermute(odd_strip, 'row', swap_pairs(row_count, 1))  0.66 us
  transfers between devices with their start and end apart: 4, of which 1 were waited for; matrix products, arithmetic and copies ran while one was open for 0% of the time, Pallas kernels for 20%

profile of v4, /device:TPU:1, one launch (start us, length us, event | category | flops | bytes accessed | tf_op | source)
XLA Modules:
  0.0 28.5 jit_solution(10241087815626361829)
XLA Ops:
  0.0 1.9 %shard_map.109 = (bf16[2,15360]{1,0:T(2,128)(2,1)}, bf16[2,15360]{1,0:T(2,128)(2,1)}) custom-call(bf16[16,7680]{1,0:T(8,128)(2,1)} %all_refs_0_.5, bf16[16,3840]{1,0:T(8,128)(2,1)} %all_refs_1_.5, bf16[32,3840]{1,0:T(8,128)(2,1)} %all_refs_2_.1), custom_call_target="tpu_custom_call" | custom-call | tf_op jit(solution)/shard_map/pallas_call | solution.py:633
  1.9 0.7 %collective-permute-start = (bf16[2,15360]{1,0:T(2,128)(2,1)}, bf16[2,15360]{1,0:T(2,128)(2,1)S(1)}, u32[]{:S(2)}, u32[]{:S(2)}) collective-permute-start(bf16[2,15360]{1,0:T(2,128)(2,1)} %get-tuple-element.28), channel_id=1, source_target_pairs={{4,8},{8,4},{5,9},{9,5},{6,10},{10,6},{7,11},{11,7},{20,24},{24,20... | collective-permute-start | bytes 184328 | tf_op jit(solution)/shard_map/ppermute | solution.py:681
  2.5 0.0 copy-start
  2.5 0.0 copy-start.1
  2.6 0.0 copy-start.2
  2.6 4.6 %collective-permute-start.1 = (bf16[2,15360]{1,0:T(2,128)(2,1)}, bf16[2,15360]{1,0:T(2,128)(2,1)S(1)}, u32[]{:S(2)}, u32[]{:S(2)}) collective-permute-start(bf16[2,15360]{1,0:T(2,128)(2,1)} %get-tuple-element.29), channel_id=1, source_target_pairs={{0,4},{4,0},{8,12},{12,8},{1,5},{5,1},{9,13},{13,9},{2,6},{6,2},{1... | collective-permute-start | bytes 184328 | tf_op jit(solution)/shard_map/ppermute | solution.py:680
  7.1 0.0 copy-start.3
  7.1 1.7 %copy-done.3 = bf16[27,36864]{1,0:T(8,128)(2,1)S(1)} copy-done((bf16[27,36864]{1,0:T(8,128)(2,1)S(1)}, bf16[27,36864]{1,0:T(8,128)(2,1)}, u32[]{:S(2)}) %copy-start.3) | copy-done | bytes 1990680
  8.8 1.3 %shard_map.110.refs_5_.all_refs_6_.all_refs_9_ = bf16[9,192,768]{2,1,0:T(8,128)(2,1)S(1)} custom-call(bf16[27,36864]{1,0:T(8,128)(2,1)S(1)} %copy-done.3), custom_call_target="tpu_custom_call" | custom-call | flops 8000000 | bytes 8000000 | tf_op jit(solution)/shard_map/pallas_call | solution.py:633
  10.1 0.0 copy-start.6
  10.1 0.0 copy-start.4
  10.1 0.0 copy-start.5
  10.1 0.0 copy-start.7
  10.1 0.0 collective-permute-done.refs_3_.all_refs_2_.all_refs_3_
  10.1 0.0 collective-permute-done.1.refs_4_.all_refs_3_.all_refs_4_
  10.1 0.0 copy-done
  10.2 0.0 copy-done.1
  10.2 0.0 copy-done.2
  10.2 0.1 shard_map.111
  10.3 1.3 %collective-permute-start.2 = (bf16[20,2688]{1,0:T(8,128)(2,1)S(1)}, bf16[20,2688]{1,0:T(8,128)(2,1)S(1)}, u32[]{:S(2)}, u32[]{:S(2)}) collective-permute-start(bf16[20,2688]{1,0:T(8,128)(2,1)S(1)} %shard_map.111), channel_id=1, source_target_pairs={{0,1},{1,0},{2,3},{3,2},{16,17},{17,16},{18,19},{19,18},{4,5},{5,4... | collective-permute-start | bytes 322568 | tf_op jit(solution)/shard_map/ppermute | solution.py:697
  11.6 0.0 copy-done.6
  11.6 1.1 %shard_map.112 = (f32[3,384,128]{2,1,0:T(8,128)S(1)}, f32[2,768,128]{2,1,0:T(8,128)S(1)}, f32[2,768,128]{2,1,0:T(8,128)S(1)}, bf16[3,448,256]{2,1,0:T(8,128)(2,1...) custom-call(bf16[16,7680]{1,0:T(8,128)(2,1)S(1)} %copy-done, bf16[16,3840]{1,0:T(8,128)(2,1)S(1)} %copy-done.1, ...), custom_call_target="tpu_custom_call" | custom-call | flops 2000000 | bytes 2000000 | tf_op jit(solution)/shard_map/pallas_call | solution.py:633
  12.7 0.1 shard_map.113
  12.9 4.5 %collective-permute-start.3 = (bf16[20,2688]{1,0:T(8,128)(2,1)S(1)}, bf16[20,2688]{1,0:T(8,128)(2,1)S(1)}, u32[]{:S(2)}, u32[]{:S(2)}) collective-permute-start(bf16[20,2688]{1,0:T(8,128)(2,1)S(1)} %shard_map.113), channel_id=1, source_target_pairs={{1,2},{2,1},{3,16},{16,3},{17,18},{18,17},{5,6},{6,5},{7,20},{20,7... | collective-permute-start | bytes 322568 | tf_op jit(solution)/shard_map/ppermute | solution.py:697
  17.4 0.0 copy-done.4
  17.4 0.0 copy-done.5
  17.4 0.8 %shard_map.114 = (bf16[512,1024]{1,0:T(8,128)(2,1)S(1)}, bf16[3,192,1536]{2,1,0:T(8,128)(2,1)S(1)}) custom-call(bf16[9,18432]{1,0:T(8,128)(2,1)S(1)} %copy-done.4, bf16[27,9216]{1,0:T(8,128)(2,1)S(1)} %copy-done.5), custom_call_target="tpu_custom_call" | custom-call | flops 8000000 | bytes 8000000 | tf_op jit(solution)/shard_map/pallas_call | solution.py:633
  18.2 0.0 copy-done.7
  18.3 0.0 copy-start.8
  18.3 0.0 copy-start.9
  18.3 0.0 copy-start.10
  18.3 2.4 %shard_map.115 = (f32[3,384,128]{2,1,0:T(8,128)S(1)}, f32[2,768,128]{2,1,0:T(8,128)S(1)}, f32[2,768,128]{2,1,0:T(8,128)S(1)}, bf16[3,448,256]{2,1,0:T(8,128)(2,1...) custom-call(bf16[16,7680]{1,0:T(8,128)(2,1)S(1)} %copy-done, ...), custom_call_target="tpu_custom_call", output_to_operand_aliasing={{0}: (7, {}), {1}: (8, {}), {2}: (9, {}), {3}: (10, {}), {4... | custom-call | flops 8000000 | bytes 8000000 | tf_op jit(solution)/shard_map/pallas_call | solution.py:633
  20.7 0.0 collective-permute-done.2.all_refs_5_
  20.7 0.3 %collective-permute-done.3.all_refs_6_ = bf16[20,2688]{1,0:T(8,128)(2,1)S(1)} collective-permute-done((bf16[20,2688]{1,0:T(8,128)(2,1)S(1)}, bf16[20,2688]{1,0:T(8,128)(2,1)S(1)}, u32[]{:S(2)}, u32[]{:S(2)}) %collective-permute-start.3) | collective-permute-done | bytes 107552 | tf_op jit(solution)/shard_map/ppermute | solution.py:697
  21.0 0.0 copy-done.8
  21.0 0.0 copy-done.9
  21.0 0.0 copy-done.10
  21.0 7.4 %shard_map.116 = (bf16[32,7680]{1,0:T(8,128)(2,1)}, f32[3,384,128]{2,1,0:T(8,128)S(1)}, f32[2,768,128]{2,1,0:T(8,128)S(1)}, f32[2,768,128]{2,1,0:T(8,128)S(1)}, ...) custom-call(bf16[16,7680]{1,0:T(8,128)(2,1)S(1)} %copy-done, ...), custom_call_target="tpu_custom_call", output_to_operand_aliasing={{1}: (15, {}), {2}: (16, {}), {3}: (17, {}), {4}: (18, {}),... | custom-call | tf_op jit(solution)/shard_map/pallas_call | solution.py:633
Async XLA Ops:
  1.9 8.3 %collective-permute-start = (bf16[2,15360]{1,0:T(2,128)(2,1)}, bf16[2,15360]{1,0:T(2,128)(2,1)S(1)}, u32[]{:S(2)}, u32[]{:S(2)}) collective-permute-start(bf16[2,15360]{1,0:T(2,128)(2,1)} %get-tuple-element.28), channel_id=1, source_target_pairs={{4,8},{8,4},{5,9},{9,5},{6,10},{10,6},{7,11},{11,7},{20,24},{24,20... | collective-permute-start | bytes 184328 | tf_op jit(solution)/shard_map/ppermute | solution.py:681
  2.5 7.6 %copy-start = (bf16[16,7680]{1,0:T(8,128)(2,1)S(1)}, bf16[16,7680]{1,0:T(8,128)(2,1)}, u32[]{:S(2)}) copy-start(bf16[16,7680]{1,0:T(8,128)(2,1)} %all_refs_0_.5) | copy-start | bytes 737284
  2.5 7.6 %copy-start.1 = (bf16[16,3840]{1,0:T(8,128)(2,1)S(1)}, bf16[16,3840]{1,0:T(8,128)(2,1)}, u32[]{:S(2)}) copy-start(bf16[16,3840]{1,0:T(8,128)(2,1)} %all_refs_1_.5) | copy-start | bytes 368644
  2.6 7.6 %copy-start.2 = (bf16[32,3840]{1,0:T(8,128)(2,1)S(1)}, bf16[32,3840]{1,0:T(8,128)(2,1)}, u32[]{:S(2)}) copy-start(bf16[32,3840]{1,0:T(8,128)(2,1)} %all_refs_2_.1) | copy-start | bytes 737284
  2.6 7.6 %collective-permute-start.1 = (bf16[2,15360]{1,0:T(2,128)(2,1)}, bf16[2,15360]{1,0:T(2,128)(2,1)S(1)}, u32[]{:S(2)}, u32[]{:S(2)}) collective-permute-start(bf16[2,15360]{1,0:T(2,128)(2,1)} %get-tuple-element.29), channel_id=1, source_target_pairs={{0,4},{4,0},{8,12},{12,8},{1,5},{5,1},{9,13},{13,9},{2,6},{6,2},{1... | collective-permute-start | bytes 184328 | tf_op jit(solution)/shard_map/ppermute | solution.py:680
  7.1 1.7 %copy-start.3 = (bf16[27,36864]{1,0:T(8,128)(2,1)S(1)}, bf16[27,36864]{1,0:T(8,128)(2,1)}, u32[]{:S(2)}) copy-start(bf16[27,36864]{1,0:T(8,128)(2,1)} %flat_ref.1) | copy-start | bytes 5971972
  10.1 1.6 %copy-start.6 = (f32[192]{0:T(256)S(1)}, f32[192]{0:T(256)}, u32[]{:S(2)}) copy-start(f32[192]{0:T(256)} %param.13) | copy-start | bytes 2308
  10.1 7.3 %copy-start.4 = (bf16[9,18432]{1,0:T(8,128)(2,1)S(1)}, bf16[9,18432]{1,0:T(8,128)(2,1)}, u32[]{:S(2)}) copy-start(bf16[9,18432]{1,0:T(8,128)(2,1)} %up_ref.1) | copy-start | bytes 995332
  10.1 7.3 %copy-start.5 = (bf16[27,9216]{1,0:T(8,128)(2,1)S(1)}, bf16[27,9216]{1,0:T(8,128)(2,1)}, u32[]{:S(2)}) copy-start(bf16[27,9216]{1,0:T(8,128)(2,1)} %four_ref.1) | copy-start | bytes 1492996
  10.1 8.1 %copy-start.7 = (f32[192]{0:T(256)S(1)}, f32[192]{0:T(256)}, u32[]{:S(2)}) copy-start(f32[192]{0:T(256)} %param.14) | copy-start | bytes 2308
  10.3 10.4 %collective-permute-start.2 = (bf16[20,2688]{1,0:T(8,128)(2,1)S(1)}, bf16[20,2688]{1,0:T(8,128)(2,1)S(1)}, u32[]{:S(2)}, u32[]{:S(2)}) collective-permute-start(bf16[20,2688]{1,0:T(8,128)(2,1)S(1)} %shard_map.111), channel_id=1, source_target_pairs={{0,1},{1,0},{2,3},{3,2},{16,17},{17,16},{18,19},{19,18},{4,5},{5,4... | collective-permute-start | bytes 322568 | tf_op jit(solution)/shard_map/ppermute | solution.py:697
  12.9 8.2 %collective-permute-start.3 = (bf16[20,2688]{1,0:T(8,128)(2,1)S(1)}, bf16[20,2688]{1,0:T(8,128)(2,1)S(1)}, u32[]{:S(2)}, u32[]{:S(2)}) collective-permute-start(bf16[20,2688]{1,0:T(8,128)(2,1)S(1)} %shard_map.113), channel_id=1, source_target_pairs={{1,2},{2,1},{3,16},{16,3},{17,18},{18,17},{5,6},{6,5},{7,20},{20,7... | collective-permute-start | bytes 322568 | tf_op jit(solution)/shard_map/ppermute | solution.py:697
  18.3 2.8 %copy-start.8 = (f32[96]{0:T(128)S(1)}, f32[96]{0:T(128)}, u32[]{:S(2)}) copy-start(f32[96]{0:T(128)} %param.17) | copy-start | bytes 1156
  18.3 2.8 %copy-start.9 = (f32[96]{0:T(128)S(1)}, f32[96]{0:T(128)}, u32[]{:S(2)}) copy-start(f32[96]{0:T(128)} %param.19) | copy-start | bytes 1156
  18.3 2.8 %copy-start.10 = (f32[96]{0:T(128)S(1)}, f32[96]{0:T(128)}, u32[]{:S(2)}) copy-start(f32[96]{0:T(128)} %param.21) | copy-start | bytes 1156

commit v5 on v4

--- a/solution.py
+++ b/solution.py
@@ -308,21 +308,25 @@
             yield lambda place=place: gather_result(p, place)
 
     span = COLS + 1
-    total = [[None, None], [None, None]]
-
-    def conv_up(p, k):
+    total = [{}, {}]
+
+    def conv_up(p, half):
         pieces = []
         for r in range(2):
             for c in range(2):
-                at = (k * MID + c) * ROWS
-                own = res_d[p][r, at : at + span * ROWS, :]
-                last = res_h[p][2 * r + c, k * 16 : (k + 1) * 16, :]
-                pieces.append(jnp.concatenate([own, last], axis=0))
-        total[p][k] = nt_dot(jnp.concatenate(pieces, axis=1), wu_ref[...])
+                parts = []
+                for k in range(2):
+                    at = (k * MID + c) * ROWS
+                    parts.append(res_d[p][r, at : at + span * ROWS, :])
+                    parts.append(res_h[p][2 * r + c, k * 16 : (k + 1) * 16, :])
+                pieces.append(jnp.concatenate(parts, axis=0))
+        got = nt_dot(jnp.concatenate(pieces, axis=1), wu_ref[half * 256 : (half + 1) * 256, :])
+        for k in range(2):
+            total[p][half, k] = got[k * (span + 1) * ROWS : (k + 1) * (span + 1) * ROWS]
 
     def conv_up_steps(p):
-        for k in range(2):
-            yield lambda k=k: conv_up(p, k)
+        for half in range(2):
+            yield lambda half=half: conv_up(p, half)
 
     def padded(name):
         return jnp.concatenate([refs[name][...], jnp.zeros((1, 32), F32)], axis=1)
@@ -336,8 +340,8 @@
 
     def fine_rows(p, a, b, k):
         at = span * ROWS
-        lanes = slice((2 * a + b) * 128, (2 * a + b + 1) * 128)
-        value = rounded(total[p][k][at : at + span, lanes] + bias_up)
+        lanes = slice(b * 128, (b + 1) * 128)
+        value = rounded(total[p][a, k][at : at + span, lanes] + bias_up)
         ext = FROWS if a else FROWS + 1
         rows = pl.ds((0 if b else FEXT) + ext, span, stride=2 * FEXT)
         if a:
@@ -359,8 +363,8 @@
         fx = 2 * j if b else 2 * j + 1
         for k in range(2):
             for a in range(2):
-                lanes = slice((2 * a + b) * 128, (2 * a + b + 1) * 128)
-                value = rounded(total[p][k][j * ROWS : (j + 1) * ROWS, lanes] + bias_up)
+                lanes = slice(b * 128, (b + 1) * 128)
+                value = rounded(total[p][a, k][j * ROWS : (j + 1) * ROWS, lanes] + bias_up)
                 rows = pl.ds(fx * FEXT + 1 - a, ROWS, stride=2)
                 if 1 <= fx <= 2 * COLS:
                     s4[p][k, rows, :] = value
@@ -495,11 +499,8 @@
     weave(do.conv_up_steps(1))
     weave(do.fine_steps(0))
     weave(do.conv_four_steps(0), do.fine_steps(1))
-    later = list(do.conv_four_steps(1))
-    ends = list(do.out_steps(1))
-    weave(later[:1], do.out_steps(0))
-    weave(later[1:], ends[:10])
-    weave(ends[10:])
+    weave(do.conv_four_steps(1), do.out_steps(0))
+    weave(do.out_steps(1))
 
 
 def split_pairs(flat_ref, parts, pairs, taps, stride):

time: 28.7 us -> 28.4 us (0.990)
  no operation moved by 1% of the time
where the time goes in v5:
time: 28.4 us; the launch traced here: 28.2 us
  Pallas kernels  15 us (53%)
  starting transfers between devices  11 us (39%)
  local copies, waits for them, and re-layouts  1.73 us (6%)
  waiting for transfers between devices  0.3 us (1%)
    pallas_call x8, Pallas kernels, call(): pl.pallas_call(kernel, out_shape=shapes, in_specs=[vmem] * (len(operands)...  15 us
    ppermute x2, starting transfers between devices, swap_columns(): lax.ppermute(strip, ('section', 'col'), swap_pairs(col_count, parity))  5.82 us
    ppermute x1, starting transfers between devices, shards(): even_row = lax.ppermute(even_strip, 'row', swap_pairs(row_count, 0))  4.56 us
    unnamed x22, local copies, waits for them, and re-layouts  1.73 us
    ppermute x1, starting transfers between devices, shards(): odd_row = lax.ppermute(odd_strip, 'row', swap_pairs(row_count, 1))  0.66 us
  transfers between devices with their start and end apart: 4, of which 1 were waited for; matrix products, arithmetic and copies ran while one was open for 0% of the time, Pallas kernels for 20%

profile of v5, /device:TPU:1, one launch (start us, length us, event | category | flops | bytes accessed | tf_op | source)
XLA Modules:
  0.0 28.2 jit_solution(16271157966132334909)
XLA Ops:
  0.0 1.9 %shard_map.109 = (bf16[2,15360]{1,0:T(2,128)(2,1)}, bf16[2,15360]{1,0:T(2,128)(2,1)}) custom-call(bf16[16,7680]{1,0:T(8,128)(2,1)} %all_refs_0_.5, bf16[16,3840]{1,0:T(8,128)(2,1)} %all_refs_1_.5, bf16[32,3840]{1,0:T(8,128)(2,1)} %all_refs_2_.1), custom_call_target="tpu_custom_call" | custom-call | tf_op jit(solution)/shard_map/pallas_call | solution.py:634
  1.9 0.7 %collective-permute-start = (bf16[2,15360]{1,0:T(2,128)(2,1)}, bf16[2,15360]{1,0:T(2,128)(2,1)S(1)}, u32[]{:S(2)}, u32[]{:S(2)}) collective-permute-start(bf16[2,15360]{1,0:T(2,128)(2,1)} %get-tuple-element.28), channel_id=1, source_target_pairs={{4,8},{8,4},{5,9},{9,5},{6,10},{10,6},{7,11},{11,7},{20,24},{24,20... | collective-permute-start | bytes 184328 | tf_op jit(solution)/shard_map/ppermute | solution.py:682
  2.5 0.0 copy-start
  2.5 0.0 copy-start.1
  2.6 0.0 copy-start.2
  2.6 4.6 %collective-permute-start.1 = (bf16[2,15360]{1,0:T(2,128)(2,1)}, bf16[2,15360]{1,0:T(2,128)(2,1)S(1)}, u32[]{:S(2)}, u32[]{:S(2)}) collective-permute-start(bf16[2,15360]{1,0:T(2,128)(2,1)} %get-tuple-element.29), channel_id=1, source_target_pairs={{0,4},{4,0},{8,12},{12,8},{1,5},{5,1},{9,13},{13,9},{2,6},{6,2},{1... | collective-permute-start | bytes 184328 | tf_op jit(solution)/shard_map/ppermute | solution.py:681
  7.1 0.0 copy-start.3
  7.1 1.7 %copy-done.3 = bf16[27,36864]{1,0:T(8,128)(2,1)S(1)} copy-done((bf16[27,36864]{1,0:T(8,128)(2,1)S(1)}, bf16[27,36864]{1,0:T(8,128)(2,1)}, u32[]{:S(2)}) %copy-start.3) | copy-done | bytes 1990680
  8.8 1.3 %shard_map.110.refs_5_.all_refs_6_.all_refs_9_ = bf16[9,192,768]{2,1,0:T(8,128)(2,1)S(1)} custom-call(bf16[27,36864]{1,0:T(8,128)(2,1)S(1)} %copy-done.3), custom_call_target="tpu_custom_call" | custom-call | flops 8000000 | bytes 8000000 | tf_op jit(solution)/shard_map/pallas_call | solution.py:634
  10.1 0.0 copy-start.6
  10.1 0.0 copy-start.4
  10.1 0.0 copy-start.5
  10.1 0.0 copy-start.7
  10.1 0.0 collective-permute-done.refs_3_.all_refs_2_.all_refs_3_
  10.1 0.0 collective-permute-done.1.refs_4_.all_refs_3_.all_refs_4_
  10.1 0.0 copy-done
  10.2 0.0 copy-done.1
  10.2 0.0 copy-done.2
  10.2 0.1 shard_map.111
  10.3 1.3 %collective-permute-start.2 = (bf16[20,2688]{1,0:T(8,128)(2,1)S(1)}, bf16[20,2688]{1,0:T(8,128)(2,1)S(1)}, u32[]{:S(2)}, u32[]{:S(2)}) collective-permute-start(bf16[20,2688]{1,0:T(8,128)(2,1)S(1)} %shard_map.111), channel_id=1, source_target_pairs={{0,1},{1,0},{2,3},{3,2},{16,17},{17,16},{18,19},{19,18},{4,5},{5,4... | collective-permute-start | bytes 322568 | tf_op jit(solution)/shard_map/ppermute | solution.py:698
  11.6 0.0 copy-done.6
  11.6 1.1 %shard_map.112 = (f32[3,384,128]{2,1,0:T(8,128)S(1)}, f32[2,768,128]{2,1,0:T(8,128)S(1)}, f32[2,768,128]{2,1,0:T(8,128)S(1)}, bf16[3,448,256]{2,1,0:T(8,128)(2,1...) custom-call(bf16[16,7680]{1,0:T(8,128)(2,1)S(1)} %copy-done, bf16[16,3840]{1,0:T(8,128)(2,1)S(1)} %copy-done.1, ...), custom_call_target="tpu_custom_call" | custom-call | flops 2000000 | bytes 2000000 | tf_op jit(solution)/shard_map/pallas_call | solution.py:634
  12.7 0.1 shard_map.113
  12.9 4.5 %collective-permute-start.3 = (bf16[20,2688]{1,0:T(8,128)(2,1)S(1)}, bf16[20,2688]{1,0:T(8,128)(2,1)S(1)}, u32[]{:S(2)}, u32[]{:S(2)}) collective-permute-start(bf16[20,2688]{1,0:T(8,128)(2,1)S(1)} %shard_map.113), channel_id=1, source_target_pairs={{1,2},{2,1},{3,16},{16,3},{17,18},{18,17},{5,6},{6,5},{7,20},{20,7... | collective-permute-start | bytes 322568 | tf_op jit(solution)/shard_map/ppermute | solution.py:698
  17.4 0.0 copy-done.4
  17.4 0.0 copy-done.5
  17.4 0.8 %shard_map.114 = (bf16[512,1024]{1,0:T(8,128)(2,1)S(1)}, bf16[3,192,1536]{2,1,0:T(8,128)(2,1)S(1)}) custom-call(bf16[9,18432]{1,0:T(8,128)(2,1)S(1)} %copy-done.4, bf16[27,9216]{1,0:T(8,128)(2,1)S(1)} %copy-done.5), custom_call_target="tpu_custom_call" | custom-call | flops 8000000 | bytes 8000000 | tf_op jit(solution)/shard_map/pallas_call | solution.py:634
  18.2 0.0 copy-done.7
  18.3 0.0 copy-start.8
  18.3 0.0 copy-start.9
  18.3 0.0 copy-start.10
  18.3 2.4 %shard_map.115 = (f32[3,384,128]{2,1,0:T(8,128)S(1)}, f32[2,768,128]{2,1,0:T(8,128)S(1)}, f32[2,768,128]{2,1,0:T(8,128)S(1)}, bf16[3,448,256]{2,1,0:T(8,128)(2,1...) custom-call(bf16[16,7680]{1,0:T(8,128)(2,1)S(1)} %copy-done, ...), custom_call_target="tpu_custom_call", output_to_operand_aliasing={{0}: (7, {}), {1}: (8, {}), {2}: (9, {}), {3}: (10, {}), {4... | custom-call | flops 8000000 | bytes 8000000 | tf_op jit(solution)/shard_map/pallas_call | solution.py:634
  20.7 0.0 collective-permute-done.2.all_refs_5_
  20.7 0.3 %collective-permute-done.3.all_refs_6_ = bf16[20,2688]{1,0:T(8,128)(2,1)S(1)} collective-permute-done((bf16[20,2688]{1,0:T(8,128)(2,1)S(1)}, bf16[20,2688]{1,0:T(8,128)(2,1)S(1)}, u32[]{:S(2)}, u32[]{:S(2)}) %collective-permute-start.3) | collective-permute-done | bytes 107552 | tf_op jit(solution)/shard_map/ppermute | solution.py:698
  21.0 0.0 copy-done.8
  21.0 0.0 copy-done.9
  21.0 0.0 copy-done.10
  21.0 7.2 %shard_map.116 = (bf16[32,7680]{1,0:T(8,128)(2,1)}, f32[3,384,128]{2,1,0:T(8,128)S(1)}, f32[2,768,128]{2,1,0:T(8,128)S(1)}, f32[2,768,128]{2,1,0:T(8,128)S(1)}, ...) custom-call(bf16[16,7680]{1,0:T(8,128)(2,1)S(1)} %copy-done, ...), custom_call_target="tpu_custom_call", output_to_operand_aliasing={{1}: (15, {}), {2}: (16, {}), {3}: (17, {}), {4}: (18, {}),... | custom-call | tf_op jit(solution)/shard_map/pallas_call | solution.py:634
Async XLA Ops:
  1.9 8.3 %collective-permute-start = (bf16[2,15360]{1,0:T(2,128)(2,1)}, bf16[2,15360]{1,0:T(2,128)(2,1)S(1)}, u32[]{:S(2)}, u32[]{:S(2)}) collective-permute-start(bf16[2,15360]{1,0:T(2,128)(2,1)} %get-tuple-element.28), channel_id=1, source_target_pairs={{4,8},{8,4},{5,9},{9,5},{6,10},{10,6},{7,11},{11,7},{20,24},{24,20... | collective-permute-start | bytes 184328 | tf_op jit(solution)/shard_map/ppermute | solution.py:682
  2.5 7.6 %copy-start = (bf16[16,7680]{1,0:T(8,128)(2,1)S(1)}, bf16[16,7680]{1,0:T(8,128)(2,1)}, u32[]{:S(2)}) copy-start(bf16[16,7680]{1,0:T(8,128)(2,1)} %all_refs_0_.5) | copy-start | bytes 737284
  2.5 7.6 %copy-start.1 = (bf16[16,3840]{1,0:T(8,128)(2,1)S(1)}, bf16[16,3840]{1,0:T(8,128)(2,1)}, u32[]{:S(2)}) copy-start(bf16[16,3840]{1,0:T(8,128)(2,1)} %all_refs_1_.5) | copy-start | bytes 368644
  2.6 7.6 %copy-start.2 = (bf16[32,3840]{1,0:T(8,128)(2,1)S(1)}, bf16[32,3840]{1,0:T(8,128)(2,1)}, u32[]{:S(2)}) copy-start(bf16[32,3840]{1,0:T(8,128)(2,1)} %all_refs_2_.1) | copy-start | bytes 737284
  2.6 7.6 %collective-permute-start.1 = (bf16[2,15360]{1,0:T(2,128)(2,1)}, bf16[2,15360]{1,0:T(2,128)(2,1)S(1)}, u32[]{:S(2)}, u32[]{:S(2)}) collective-permute-start(bf16[2,15360]{1,0:T(2,128)(2,1)} %get-tuple-element.29), channel_id=1, source_target_pairs={{0,4},{4,0},{8,12},{12,8},{1,5},{5,1},{9,13},{13,9},{2,6},{6,2},{1... | collective-permute-start | bytes 184328 | tf_op jit(solution)/shard_map/ppermute | solution.py:681
  7.1 1.7 %copy-start.3 = (bf16[27,36864]{1,0:T(8,128)(2,1)S(1)}, bf16[27,36864]{1,0:T(8,128)(2,1)}, u32[]{:S(2)}) copy-start(bf16[27,36864]{1,0:T(8,128)(2,1)} %flat_ref.1) | copy-start | bytes 5971972
  10.1 1.6 %copy-start.6 = (f32[192]{0:T(256)S(1)}, f32[192]{0:T(256)}, u32[]{:S(2)}) copy-start(f32[192]{0:T(256)} %param.13) | copy-start | bytes 2308
  10.1 7.3 %copy-start.4 = (bf16[9,18432]{1,0:T(8,128)(2,1)S(1)}, bf16[9,18432]{1,0:T(8,128)(2,1)}, u32[]{:S(2)}) copy-start(bf16[9,18432]{1,0:T(8,128)(2,1)} %up_ref.1) | copy-start | bytes 995332
  10.1 7.3 %copy-start.5 = (bf16[27,9216]{1,0:T(8,128)(2,1)S(1)}, bf16[27,9216]{1,0:T(8,128)(2,1)}, u32[]{:S(2)}) copy-start(bf16[27,9216]{1,0:T(8,128)(2,1)} %four_ref.1) | copy-start | bytes 1492996
  10.1 8.1 %copy-start.7 = (f32[192]{0:T(256)S(1)}, f32[192]{0:T(256)}, u32[]{:S(2)}) copy-start(f32[192]{0:T(256)} %param.14) | copy-start | bytes 2308
  10.3 10.4 %collective-permute-start.2 = (bf16[20,2688]{1,0:T(8,128)(2,1)S(1)}, bf16[20,2688]{1,0:T(8,128)(2,1)S(1)}, u32[]{:S(2)}, u32[]{:S(2)}) collective-permute-start(bf16[20,2688]{1,0:T(8,128)(2,1)S(1)} %shard_map.111), channel_id=1, source_target_pairs={{0,1},{1,0},{2,3},{3,2},{16,17},{17,16},{18,19},{19,18},{4,5},{5,4... | collective-permute-start | bytes 322568 | tf_op jit(solution)/shard_map/ppermute | solution.py:698
  12.9 8.2 %collective-permute-start.3 = (bf16[20,2688]{1,0:T(8,128)(2,1)S(1)}, bf16[20,2688]{1,0:T(8,128)(2,1)S(1)}, u32[]{:S(2)}, u32[]{:S(2)}) collective-permute-start(bf16[20,2688]{1,0:T(8,128)(2,1)S(1)} %shard_map.113), channel_id=1, source_target_pairs={{1,2},{2,1},{3,16},{16,3},{17,18},{18,17},{5,6},{6,5},{7,20},{20,7... | collective-permute-start | bytes 322568 | tf_op jit(solution)/shard_map/ppermute | solution.py:698
  18.3 2.8 %copy-start.8 = (f32[96]{0:T(128)S(1)}, f32[96]{0:T(128)}, u32[]{:S(2)}) copy-start(f32[96]{0:T(128)} %param.17) | copy-start | bytes 1156
  18.3 2.8 %copy-start.9 = (f32[96]{0:T(128)S(1)}, f32[96]{0:T(128)}, u32[]{:S(2)}) copy-start(f32[96]{0:T(128)} %param.19) | copy-start | bytes 1156
  18.3 2.8 %copy-start.10 = (f32[96]{0:T(128)S(1)}, f32[96]{0:T(128)}, u32[]{:S(2)}) copy-start(f32[96]{0:T(128)} %param.21) | copy-start | bytes 1156

commit v6 on v5

--- a/solution.py
+++ b/solution.py
@@ -455,6 +455,7 @@
 
 
 OWN = range(2, WIDE - 2)
+EARLY, LATE = OWN[:6], OWN[6:]
 
 
 def first_inner_kernel(names, sizes, *all_refs):
@@ -464,7 +465,7 @@
     @pl.when(col == sizes[1] // 2)
     def _():
         do = stages(refs, *sizes)
-        weave(do.coarse_steps(0, OWN), do.coarse_steps(1, OWN))
+        weave(do.coarse_steps(0, OWN), do.coarse_steps(1, EARLY))
 
 
 def inner_kernel(names, sizes, *all_refs):
@@ -474,10 +475,11 @@
     @pl.when(col != sizes[1] // 2)
     def _():
         do = stages(refs, *sizes)
-        weave(do.coarse_steps(0, OWN), do.coarse_steps(1, OWN))
+        weave(do.coarse_steps(0, OWN), do.coarse_steps(1, EARLY))
 
     do = stages(refs, *sizes)
-    weave(do.row_steps(0), do.row_steps(1))
+    weave(do.coarse_steps(1, LATE), do.row_steps(0))
+    weave(do.row_steps(1))
     weave(do.conv_three_steps([INNER], [(0, 0), (0, 1)]), do.coarse_steps(2, OWN))
     weave(do.row_steps(2))
     weave(do.conv_three_steps([INNER], [(1, 0), (1, 1)]), do.result_steps(0, [INNER]))
@@ -496,8 +498,7 @@
     weave(do.result_steps(1, RIMS))
     weave(do.gather_steps(1))
     weave(do.conv_up_steps(0))
-    weave(do.conv_up_steps(1))
-    weave(do.fine_steps(0))
+    weave(do.conv_up_steps(1), do.fine_steps(0))
     weave(do.conv_four_steps(0), do.fine_steps(1))
     weave(do.conv_four_steps(1), do.out_steps(0))
     weave(do.out_steps(1))
@@ -570,27 +571,20 @@
             four_out[dy, C4 : 2 * C4, at + (t + 1) * 128 : at + (t + 2) * 128] = kernel
 
 
-def row_strips(refs, low_flag, out_ref):
-    at = 0
-    for ref in refs:
-        rows, width = ref.shape
-        out_ref[:, at : at + width] = jnp.where(low_flag, ref[0:2, :], ref[rows - 2 : rows, :])
-        at += width
-
-
 def row_strips_kernel(x_ref, p_ref, q_ref, even_ref, odd_ref, x_own, p_own, q_own, sems):
-    own = (x_own, p_own, q_own)
+    row_odd = lax.rem(lax.axis_index("row"), 2) == 1
+    parts = ((p_ref, p_own, XW), (x_ref, x_own, 0), (q_ref, q_own, XW + PW))
     copies = [
-        pltpu.make_async_copy(source, target, sems.at[n])
-        for n, (source, target) in enumerate(zip((x_ref, p_ref, q_ref), own))
+        pltpu.make_async_copy(source, own, sems.at[n]) for n, (source, own, _) in enumerate(parts)
     ]
     for copy in copies:
         copy.start()
-    for copy in copies:
+    for copy, (_, own, at) in zip(copies, parts):
         copy.wait()
-    row_odd = lax.rem(lax.axis_index("row"), 2) == 1
-    row_strips(own, row_odd, even_ref)
-    row_strips(own, jnp.logical_not(row_odd), odd_ref)
+        rows, width = own.shape
+        low, high = own[0:2, :], own[rows - 2 : rows, :]
+        even_ref[:, at : at + width] = jnp.where(row_odd, low, high)
+        odd_ref[:, at : at + width] = jnp.where(row_odd, high, low)
 
 
 def col_strips_kernel(x_ref, p_ref, q_ref, odd_row, even_row, _, out_ref, *, col_size, parity):

time: 28.4 us -> 28.4 us (level)
  starting transfers between devices: 11 us -> 11.5 us
  Pallas kernels: 15 us -> 14.7 us
  waiting for transfers between devices: 0.3 us -> 0.01 us
    ppermute x2, starting transfers between devices: 5.82 us -> 6.3 us  [swap_columns(): lax.ppermute(strip, ('section', 'col'), swap_pairs(col_count, parity))]
    ppermute x2, waiting for transfers between devices: 0.29 us -> 0.01 us  [swap_columns(): lax.ppermute(strip, ('section', 'col'), swap_pairs(col_count, parity))]
  transfers between devices with their start and end apart: 4 -> 4, of which waited for: 1 -> 0; matrix products, arithmetic and copies ran while one was open for 0% -> 0% of each run, Pallas kernels for 20% -> 19%
where the time goes in v6:
time: 28.4 us; the launch traced here: 28.2 us
  Pallas kernels  14.7 us (52%)
  starting transfers between devices  11.5 us (40%)
  local copies, waits for them, and re-layouts  1.73 us (6%)
    pallas_call x8, Pallas kernels, call(): pl.pallas_call(kernel, out_shape=shapes, in_specs=[vmem] * (len(operands)...  14.7 us
    ppermute x2, starting transfers between devices, swap_columns(): lax.ppermute(strip, ('section', 'col'), swap_pairs(col_count, parity))  6.3 us
    ppermute x1, starting transfers between devices, shards(): even_row = lax.ppermute(even_strip, 'row', swap_pairs(row_count, 0))  4.56 us
    unnamed x22, local copies, waits for them, and re-layouts  1.73 us
    ppermute x1, starting transfers between devices, shards(): odd_row = lax.ppermute(odd_strip, 'row', swap_pairs(row_count, 1))  0.66 us
  transfers between devices with their start and end apart: 4, of which 0 were waited for; matrix products, arithmetic and copies ran while one was open for 0% of the time, Pallas kernels for 19%

profile of v6, /device:TPU:1, one launch (start us, length us, event | category | flops | bytes accessed | tf_op | source)
XLA Modules:
  0.0 28.2 jit_solution(352416447241605083)
XLA Ops:
  0.0 1.8 %shard_map.109 = (bf16[2,15360]{1,0:T(2,128)(2,1)}, bf16[2,15360]{1,0:T(2,128)(2,1)}) custom-call(bf16[16,7680]{1,0:T(8,128)(2,1)} %all_refs_0_.5, bf16[16,3840]{1,0:T(8,128)(2,1)} %all_refs_1_.5, bf16[32,3840]{1,0:T(8,128)(2,1)} %all_refs_2_.1), custom_call_target="tpu_custom_call" | custom-call | tf_op jit(solution)/shard_map/pallas_call | solution.py:628
  1.8 0.7 %collective-permute-start = (bf16[2,15360]{1,0:T(2,128)(2,1)}, bf16[2,15360]{1,0:T(2,128)(2,1)S(1)}, u32[]{:S(2)}, u32[]{:S(2)}) collective-permute-start(bf16[2,15360]{1,0:T(2,128)(2,1)} %get-tuple-element.28), channel_id=1, source_target_pairs={{4,8},{8,4},{5,9},{9,5},{6,10},{10,6},{7,11},{11,7},{20,24},{24,20... | collective-permute-start | bytes 184328 | tf_op jit(solution)/shard_map/ppermute | solution.py:676
  2.5 0.0 copy-start
  2.5 0.0 copy-start.1
  2.5 0.0 copy-start.2
  2.5 4.6 %collective-permute-start.1 = (bf16[2,15360]{1,0:T(2,128)(2,1)}, bf16[2,15360]{1,0:T(2,128)(2,1)S(1)}, u32[]{:S(2)}, u32[]{:S(2)}) collective-permute-start(bf16[2,15360]{1,0:T(2,128)(2,1)} %get-tuple-element.29), channel_id=1, source_target_pairs={{0,4},{4,0},{8,12},{12,8},{1,5},{5,1},{9,13},{13,9},{2,6},{6,2},{1... | collective-permute-start | bytes 184328 | tf_op jit(solution)/shard_map/ppermute | solution.py:675
  7.1 0.0 copy-start.3
  7.1 1.7 %copy-done.3 = bf16[27,36864]{1,0:T(8,128)(2,1)S(1)} copy-done((bf16[27,36864]{1,0:T(8,128)(2,1)S(1)}, bf16[27,36864]{1,0:T(8,128)(2,1)}, u32[]{:S(2)}) %copy-start.3) | copy-done | bytes 1990680
  8.8 1.3 %shard_map.110.refs_5_.all_refs_6_.all_refs_9_ = bf16[9,192,768]{2,1,0:T(8,128)(2,1)S(1)} custom-call(bf16[27,36864]{1,0:T(8,128)(2,1)S(1)} %copy-done.3), custom_call_target="tpu_custom_call" | custom-call | flops 8000000 | bytes 8000000 | tf_op jit(solution)/shard_map/pallas_call | solution.py:628
  10.0 0.0 copy-start.6
  10.0 0.0 copy-start.4
  10.1 0.0 copy-start.5
  10.1 0.0 copy-start.7
  10.1 0.0 collective-permute-done.refs_3_.all_refs_2_.all_refs_3_
  10.1 0.0 collective-permute-done.1.refs_4_.all_refs_3_.all_refs_4_
  10.1 0.0 copy-done
  10.1 0.0 copy-done.1
  10.1 0.0 copy-done.2
  10.1 0.1 shard_map.111
  10.3 1.3 %collective-permute-start.2 = (bf16[20,2688]{1,0:T(8,128)(2,1)S(1)}, bf16[20,2688]{1,0:T(8,128)(2,1)S(1)}, u32[]{:S(2)}, u32[]{:S(2)}) collective-permute-start(bf16[20,2688]{1,0:T(8,128)(2,1)S(1)} %shard_map.111), channel_id=1, source_target_pairs={{0,1},{1,0},{2,3},{3,2},{16,17},{17,16},{18,19},{19,18},{4,5},{5,4... | collective-permute-start | bytes 322568 | tf_op jit(solution)/shard_map/ppermute | solution.py:692
  11.6 0.0 copy-done.6
  11.6 0.6 %shard_map.112 = (f32[3,384,128]{2,1,0:T(8,128)S(1)}, f32[2,768,128]{2,1,0:T(8,128)S(1)}, f32[2,768,128]{2,1,0:T(8,128)S(1)}, bf16[3,448,256]{2,1,0:T(8,128)(2,1...) custom-call(bf16[16,7680]{1,0:T(8,128)(2,1)S(1)} %copy-done, bf16[16,3840]{1,0:T(8,128)(2,1)S(1)} %copy-done.1, ...), custom_call_target="tpu_custom_call" | custom-call | flops 2000000 | bytes 2000000 | tf_op jit(solution)/shard_map/pallas_call | solution.py:628
  12.2 0.1 shard_map.113
  12.3 5.0 %collective-permute-start.3 = (bf16[20,2688]{1,0:T(8,128)(2,1)S(1)}, bf16[20,2688]{1,0:T(8,128)(2,1)S(1)}, u32[]{:S(2)}, u32[]{:S(2)}) collective-permute-start(bf16[20,2688]{1,0:T(8,128)(2,1)S(1)} %shard_map.113), channel_id=1, source_target_pairs={{1,2},{2,1},{3,16},{16,3},{17,18},{18,17},{5,6},{6,5},{7,20},{20,7... | collective-permute-start | bytes 322568 | tf_op jit(solution)/shard_map/ppermute | solution.py:692
  17.3 0.0 copy-done.4
  17.3 0.0 copy-done.5
  17.3 0.8 %shard_map.114 = (bf16[512,1024]{1,0:T(8,128)(2,1)S(1)}, bf16[3,192,1536]{2,1,0:T(8,128)(2,1)S(1)}) custom-call(bf16[9,18432]{1,0:T(8,128)(2,1)S(1)} %copy-done.4, bf16[27,9216]{1,0:T(8,128)(2,1)S(1)} %copy-done.5), custom_call_target="tpu_custom_call" | custom-call | flops 8000000 | bytes 8000000 | tf_op jit(solution)/shard_map/pallas_call | solution.py:628
  18.2 0.0 copy-done.7
  18.2 0.0 copy-start.8
  18.2 0.0 copy-start.9
  18.2 0.0 copy-start.10
  18.2 2.6 %shard_map.115 = (f32[3,384,128]{2,1,0:T(8,128)S(1)}, f32[2,768,128]{2,1,0:T(8,128)S(1)}, f32[2,768,128]{2,1,0:T(8,128)S(1)}, bf16[3,448,256]{2,1,0:T(8,128)(2,1...) custom-call(bf16[16,7680]{1,0:T(8,128)(2,1)S(1)} %copy-done, ...), custom_call_target="tpu_custom_call", output_to_operand_aliasing={{0}: (7, {}), {1}: (8, {}), {2}: (9, {}), {3}: (10, {}), {4... | custom-call | flops 8000000 | bytes 8000000 | tf_op jit(solution)/shard_map/pallas_call | solution.py:628
  20.9 0.0 collective-permute-done.2.all_refs_5_
  20.9 0.0 collective-permute-done.3.all_refs_6_
  20.9 0.0 copy-done.8
  20.9 0.0 copy-done.9
  20.9 0.0 copy-done.10
  20.9 7.2 %shard_map.116 = (bf16[32,7680]{1,0:T(8,128)(2,1)}, f32[3,384,128]{2,1,0:T(8,128)S(1)}, f32[2,768,128]{2,1,0:T(8,128)S(1)}, f32[2,768,128]{2,1,0:T(8,128)S(1)}, ...) custom-call(bf16[16,7680]{1,0:T(8,128)(2,1)S(1)} %copy-done, ...), custom_call_target="tpu_custom_call", output_to_operand_aliasing={{1}: (15, {}), {2}: (16, {}), {3}: (17, {}), {4}: (18, {}),... | custom-call | tf_op jit(solution)/shard_map/pallas_call | solution.py:628
Async XLA Ops:
  1.8 8.3 %collective-permute-start = (bf16[2,15360]{1,0:T(2,128)(2,1)}, bf16[2,15360]{1,0:T(2,128)(2,1)S(1)}, u32[]{:S(2)}, u32[]{:S(2)}) collective-permute-start(bf16[2,15360]{1,0:T(2,128)(2,1)} %get-tuple-element.28), channel_id=1, source_target_pairs={{4,8},{8,4},{5,9},{9,5},{6,10},{10,6},{7,11},{11,7},{20,24},{24,20... | collective-permute-start | bytes 184328 | tf_op jit(solution)/shard_map/ppermute | solution.py:676
  2.5 7.6 %copy-start = (bf16[16,7680]{1,0:T(8,128)(2,1)S(1)}, bf16[16,7680]{1,0:T(8,128)(2,1)}, u32[]{:S(2)}) copy-start(bf16[16,7680]{1,0:T(8,128)(2,1)} %all_refs_0_.5) | copy-start | bytes 737284
  2.5 7.6 %copy-start.1 = (bf16[16,3840]{1,0:T(8,128)(2,1)S(1)}, bf16[16,3840]{1,0:T(8,128)(2,1)}, u32[]{:S(2)}) copy-start(bf16[16,3840]{1,0:T(8,128)(2,1)} %all_refs_1_.5) | copy-start | bytes 368644
  2.5 7.6 %copy-start.2 = (bf16[32,3840]{1,0:T(8,128)(2,1)S(1)}, bf16[32,3840]{1,0:T(8,128)(2,1)}, u32[]{:S(2)}) copy-start(bf16[32,3840]{1,0:T(8,128)(2,1)} %all_refs_2_.1) | copy-start | bytes 737284
  2.5 7.6 %collective-permute-start.1 = (bf16[2,15360]{1,0:T(2,128)(2,1)}, bf16[2,15360]{1,0:T(2,128)(2,1)S(1)}, u32[]{:S(2)}, u32[]{:S(2)}) collective-permute-start(bf16[2,15360]{1,0:T(2,128)(2,1)} %get-tuple-element.29), channel_id=1, source_target_pairs={{0,4},{4,0},{8,12},{12,8},{1,5},{5,1},{9,13},{13,9},{2,6},{6,2},{1... | collective-permute-start | bytes 184328 | tf_op jit(solution)/shard_map/ppermute | solution.py:675
  7.1 1.7 %copy-start.3 = (bf16[27,36864]{1,0:T(8,128)(2,1)S(1)}, bf16[27,36864]{1,0:T(8,128)(2,1)}, u32[]{:S(2)}) copy-start(bf16[27,36864]{1,0:T(8,128)(2,1)} %flat_ref.1) | copy-start | bytes 5971972
  10.0 1.6 %copy-start.6 = (f32[192]{0:T(256)S(1)}, f32[192]{0:T(256)}, u32[]{:S(2)}) copy-start(f32[192]{0:T(256)} %param.13) | copy-start | bytes 2308
  10.0 7.3 %copy-start.4 = (bf16[9,18432]{1,0:T(8,128)(2,1)S(1)}, bf16[9,18432]{1,0:T(8,128)(2,1)}, u32[]{:S(2)}) copy-start(bf16[9,18432]{1,0:T(8,128)(2,1)} %up_ref.1) | copy-start | bytes 995332
  10.1 7.3 %copy-start.5 = (bf16[27,9216]{1,0:T(8,128)(2,1)S(1)}, bf16[27,9216]{1,0:T(8,128)(2,1)}, u32[]{:S(2)}) copy-start(bf16[27,9216]{1,0:T(8,128)(2,1)} %four_ref.1) | copy-start | bytes 1492996
  10.1 8.1 %copy-start.7 = (f32[192]{0:T(256)S(1)}, f32[192]{0:T(256)}, u32[]{:S(2)}) copy-start(f32[192]{0:T(256)} %param.14) | copy-start | bytes 2308
  10.3 10.6 %collective-permute-start.2 = (bf16[20,2688]{1,0:T(8,128)(2,1)S(1)}, bf16[20,2688]{1,0:T(8,128)(2,1)S(1)}, u32[]{:S(2)}, u32[]{:S(2)}) collective-permute-start(bf16[20,2688]{1,0:T(8,128)(2,1)S(1)} %shard_map.111), channel_id=1, source_target_pairs={{0,1},{1,0},{2,3},{3,2},{16,17},{17,16},{18,19},{19,18},{4,5},{5,4... | collective-permute-start | bytes 322568 | tf_op jit(solution)/shard_map/ppermute | solution.py:692
  12.3 8.6 %collective-permute-start.3 = (bf16[20,2688]{1,0:T(8,128)(2,1)S(1)}, bf16[20,2688]{1,0:T(8,128)(2,1)S(1)}, u32[]{:S(2)}, u32[]{:S(2)}) collective-permute-start(bf16[20,2688]{1,0:T(8,128)(2,1)S(1)} %shard_map.113), channel_id=1, source_target_pairs={{1,2},{2,1},{3,16},{16,3},{17,18},{18,17},{5,6},{6,5},{7,20},{20,7... | collective-permute-start | bytes 322568 | tf_op jit(solution)/shard_map/ppermute | solution.py:692
  18.2 2.7 %copy-start.8 = (f32[96]{0:T(128)S(1)}, f32[96]{0:T(128)}, u32[]{:S(2)}) copy-start(f32[96]{0:T(128)} %param.17) | copy-start | bytes 1156
  18.2 2.7 %copy-start.9 = (f32[96]{0:T(128)S(1)}, f32[96]{0:T(128)}, u32[]{:S(2)}) copy-start(f32[96]{0:T(128)} %param.19) | copy-start | bytes 1156
  18.2 2.7 %copy-start.10 = (f32[96]{0:T(128)S(1)}, f32[96]{0:T(128)}, u32[]{:S(2)}) copy-start(f32[96]{0:T(128)} %param.21) | copy-start | bytes 1156

commit v7 on v6

--- a/solution.py
+++ b/solution.py
@@ -420,21 +420,23 @@
         for fx in range(FINE):
             yield lambda fx=fx: cached_column(fx)
 
-    size = COLS * FROWS
-    done = [[None, None], [None, None]]
-
-    def conv_four(p, half):
+    done = [{}, {}]
+
+    def conv_four(p, start, count):
+        size = count * FROWS
         pieces = []
         for dy in range(3):
             for dx in range(3):
-                at = (dx + half * COLS) * FROWS
+                at = (dx + start) * FROWS
                 pieces += [act4_d[group][dy, at : at + size, :] for group in (p, p + 1)]
         kernel = jnp.concatenate([w4_ref[dy] for dy in range(3)], axis=1)
-        done[p][half] = nt_dot(jnp.concatenate(pieces, axis=1), kernel)
+        got = nt_dot(jnp.concatenate(pieces, axis=1), kernel)
+        for n in range(count):
+            done[p][start + n] = got[n * FROWS : (n + 1) * FROWS]
 
     def conv_four_steps(p):
-        for half in range(2):
-            yield lambda half=half: conv_four(p, half)
+        for start, count in ((0, COLS + 2), (COLS + 2, COLS - 2)):
+            yield lambda start=start, count=count: conv_four(p, start, count)
 
     bias_four = jnp.concatenate([refs["b4"][...]] * 2, axis=1) if "b4" in refs else None
     first = lane_mask(FROWS, C4)
@@ -443,8 +445,7 @@
         rows = slice((fx + 1) * FEXT + 1, (fx + 1) * FEXT + 1 + FROWS)
         other = pltpu.roll(s4[p][1, rows, :], C4, 1)
         skip = jnp.concatenate([jnp.where(first, s4[p][0, rows, :], other), other[:, 0:64]], axis=1)
-        at = fx % COLS * FROWS
-        value = (done[p][fx // COLS][at : at + FROWS] + bias_four + skip).astype(BF16)
+        value = (done[p][fx] + bias_four + skip).astype(BF16)
         out_ref[:, fx * 384 + p * 192 : fx * 384 + (p + 1) * 192] = value
 
     def out_steps(p):

time: 28.4 us -> 28.4 us (level)
  no operation moved by 1% of the time
where the time goes in v7:
time: 28.4 us; the launch traced here: 28.2 us
  Pallas kernels  14.7 us (52%)
  starting transfers between devices  11.5 us (40%)
  local copies, waits for them, and re-layouts  1.73 us (6%)
    pallas_call x8, Pallas kernels, call(): pl.pallas_call(kernel, out_shape=shapes, in_specs=[vmem] * (len(operands)...  14.7 us
    ppermute x2, starting transfers between devices, swap_columns(): lax.ppermute(strip, ('section', 'col'), swap_pairs(col_count, parity))  6.3 us
    ppermute x1, starting transfers between devices, shards(): even_row = lax.ppermute(even_strip, 'row', swap_pairs(row_count, 0))  4.56 us
    unnamed x22, local copies, waits for them, and re-layouts  1.73 us
    ppermute x1, starting transfers between devices, shards(): odd_row = lax.ppermute(odd_strip, 'row', swap_pairs(row_count, 1))  0.66 us
  transfers between devices with their start and end apart: 4, of which 0 were waited for; matrix products, arithmetic and copies ran while one was open for 0% of the time, Pallas kernels for 19%

profile of v7, /device:TPU:1, one launch (start us, length us, event | category | flops | bytes accessed | tf_op | source)
XLA Modules:
  0.0 28.2 jit_solution(17342524000468414749)
XLA Ops:
  0.0 1.8 %shard_map.109 = (bf16[2,15360]{1,0:T(2,128)(2,1)}, bf16[2,15360]{1,0:T(2,128)(2,1)}) custom-call(bf16[16,7680]{1,0:T(8,128)(2,1)} %all_refs_0_.5, bf16[16,3840]{1,0:T(8,128)(2,1)} %all_refs_1_.5, bf16[32,3840]{1,0:T(8,128)(2,1)} %all_refs_2_.1), custom_call_target="tpu_custom_call" | custom-call | tf_op jit(solution)/shard_map/pallas_call | solution.py:629
  1.8 0.7 %collective-permute-start = (bf16[2,15360]{1,0:T(2,128)(2,1)}, bf16[2,15360]{1,0:T(2,128)(2,1)S(1)}, u32[]{:S(2)}, u32[]{:S(2)}) collective-permute-start(bf16[2,15360]{1,0:T(2,128)(2,1)} %get-tuple-element.28), channel_id=1, source_target_pairs={{4,8},{8,4},{5,9},{9,5},{6,10},{10,6},{7,11},{11,7},{20,24},{24,20... | collective-permute-start | bytes 184328 | tf_op jit(solution)/shard_map/ppermute | solution.py:677
  2.5 0.0 copy-start
  2.5 0.0 copy-start.1
  2.5 0.0 copy-start.2
  2.5 4.6 %collective-permute-start.1 = (bf16[2,15360]{1,0:T(2,128)(2,1)}, bf16[2,15360]{1,0:T(2,128)(2,1)S(1)}, u32[]{:S(2)}, u32[]{:S(2)}) collective-permute-start(bf16[2,15360]{1,0:T(2,128)(2,1)} %get-tuple-element.29), channel_id=1, source_target_pairs={{0,4},{4,0},{8,12},{12,8},{1,5},{5,1},{9,13},{13,9},{2,6},{6,2},{1... | collective-permute-start | bytes 184328 | tf_op jit(solution)/shard_map/ppermute | solution.py:676
  7.1 0.0 copy-start.3
  7.1 1.7 %copy-done.3 = bf16[27,36864]{1,0:T(8,128)(2,1)S(1)} copy-done((bf16[27,36864]{1,0:T(8,128)(2,1)S(1)}, bf16[27,36864]{1,0:T(8,128)(2,1)}, u32[]{:S(2)}) %copy-start.3) | copy-done | bytes 1990680
  8.8 1.3 %shard_map.110.refs_5_.all_refs_6_.all_refs_9_ = bf16[9,192,768]{2,1,0:T(8,128)(2,1)S(1)} custom-call(bf16[27,36864]{1,0:T(8,128)(2,1)S(1)} %copy-done.3), custom_call_target="tpu_custom_call" | custom-call | flops 8000000 | bytes 8000000 | tf_op jit(solution)/shard_map/pallas_call | solution.py:629
  10.0 0.0 copy-start.6
  10.0 0.0 copy-start.4
  10.1 0.0 copy-start.5
  10.1 0.0 copy-start.7
  10.1 0.0 collective-permute-done.refs_3_.all_refs_2_.all_refs_3_
  10.1 0.0 collective-permute-done.1.refs_4_.all_refs_3_.all_refs_4_
  10.1 0.0 copy-done
  10.1 0.0 copy-done.1
  10.1 0.0 copy-done.2
  10.1 0.1 shard_map.111
  10.3 1.3 %collective-permute-start.2 = (bf16[20,2688]{1,0:T(8,128)(2,1)S(1)}, bf16[20,2688]{1,0:T(8,128)(2,1)S(1)}, u32[]{:S(2)}, u32[]{:S(2)}) collective-permute-start(bf16[20,2688]{1,0:T(8,128)(2,1)S(1)} %shard_map.111), channel_id=1, source_target_pairs={{0,1},{1,0},{2,3},{3,2},{16,17},{17,16},{18,19},{19,18},{4,5},{5,4... | collective-permute-start | bytes 322568 | tf_op jit(solution)/shard_map/ppermute | solution.py:693
  11.6 0.0 copy-done.6
  11.6 0.6 %shard_map.112 = (f32[3,384,128]{2,1,0:T(8,128)S(1)}, f32[2,768,128]{2,1,0:T(8,128)S(1)}, f32[2,768,128]{2,1,0:T(8,128)S(1)}, bf16[3,448,256]{2,1,0:T(8,128)(2,1...) custom-call(bf16[16,7680]{1,0:T(8,128)(2,1)S(1)} %copy-done, bf16[16,3840]{1,0:T(8,128)(2,1)S(1)} %copy-done.1, ...), custom_call_target="tpu_custom_call" | custom-call | flops 2000000 | bytes 2000000 | tf_op jit(solution)/shard_map/pallas_call | solution.py:629
  12.2 0.1 shard_map.113
  12.3 5.0 %collective-permute-start.3 = (bf16[20,2688]{1,0:T(8,128)(2,1)S(1)}, bf16[20,2688]{1,0:T(8,128)(2,1)S(1)}, u32[]{:S(2)}, u32[]{:S(2)}) collective-permute-start(bf16[20,2688]{1,0:T(8,128)(2,1)S(1)} %shard_map.113), channel_id=1, source_target_pairs={{1,2},{2,1},{3,16},{16,3},{17,18},{18,17},{5,6},{6,5},{7,20},{20,7... | collective-permute-start | bytes 322568 | tf_op jit(solution)/shard_map/ppermute | solution.py:693
  17.3 0.0 copy-done.4
  17.3 0.0 copy-done.5
  17.3 0.8 %shard_map.114 = (bf16[512,1024]{1,0:T(8,128)(2,1)S(1)}, bf16[3,192,1536]{2,1,0:T(8,128)(2,1)S(1)}) custom-call(bf16[9,18432]{1,0:T(8,128)(2,1)S(1)} %copy-done.4, bf16[27,9216]{1,0:T(8,128)(2,1)S(1)} %copy-done.5), custom_call_target="tpu_custom_call" | custom-call | flops 8000000 | bytes 8000000 | tf_op jit(solution)/shard_map/pallas_call | solution.py:629
  18.2 0.0 copy-done.7
  18.2 0.0 copy-start.8
  18.2 0.0 copy-start.9
  18.2 0.0 copy-start.10
  18.2 2.6 %shard_map.115 = (f32[3,384,128]{2,1,0:T(8,128)S(1)}, f32[2,768,128]{2,1,0:T(8,128)S(1)}, f32[2,768,128]{2,1,0:T(8,128)S(1)}, bf16[3,448,256]{2,1,0:T(8,128)(2,1...) custom-call(bf16[16,7680]{1,0:T(8,128)(2,1)S(1)} %copy-done, ...), custom_call_target="tpu_custom_call", output_to_operand_aliasing={{0}: (7, {}), {1}: (8, {}), {2}: (9, {}), {3}: (10, {}), {4... | custom-call | flops 8000000 | bytes 8000000 | tf_op jit(solution)/shard_map/pallas_call | solution.py:629
  20.9 0.0 collective-permute-done.2.all_refs_5_
  20.9 0.0 collective-permute-done.3.all_refs_6_
  20.9 0.0 copy-done.8
  20.9 0.0 copy-done.9
  20.9 0.0 copy-done.10
  20.9 7.2 %shard_map.116 = (bf16[32,7680]{1,0:T(8,128)(2,1)}, f32[3,384,128]{2,1,0:T(8,128)S(1)}, f32[2,768,128]{2,1,0:T(8,128)S(1)}, f32[2,768,128]{2,1,0:T(8,128)S(1)}, ...) custom-call(bf16[16,7680]{1,0:T(8,128)(2,1)S(1)} %copy-done, ...), custom_call_target="tpu_custom_call", output_to_operand_aliasing={{1}: (15, {}), {2}: (16, {}), {3}: (17, {}), {4}: (18, {}),... | custom-call | tf_op jit(solution)/shard_map/pallas_call | solution.py:629
Async XLA Ops:
  1.8 8.3 %collective-permute-start = (bf16[2,15360]{1,0:T(2,128)(2,1)}, bf16[2,15360]{1,0:T(2,128)(2,1)S(1)}, u32[]{:S(2)}, u32[]{:S(2)}) collective-permute-start(bf16[2,15360]{1,0:T(2,128)(2,1)} %get-tuple-element.28), channel_id=1, source_target_pairs={{4,8},{8,4},{5,9},{9,5},{6,10},{10,6},{7,11},{11,7},{20,24},{24,20... | collective-permute-start | bytes 184328 | tf_op jit(solution)/shard_map/ppermute | solution.py:677
  2.5 7.6 %copy-start = (bf16[16,7680]{1,0:T(8,128)(2,1)S(1)}, bf16[16,7680]{1,0:T(8,128)(2,1)}, u32[]{:S(2)}) copy-start(bf16[16,7680]{1,0:T(8,128)(2,1)} %all_refs_0_.5) | copy-start | bytes 737284
  2.5 7.6 %copy-start.1 = (bf16[16,3840]{1,0:T(8,128)(2,1)S(1)}, bf16[16,3840]{1,0:T(8,128)(2,1)}, u32[]{:S(2)}) copy-start(bf16[16,3840]{1,0:T(8,128)(2,1)} %all_refs_1_.5) | copy-start | bytes 368644
  2.5 7.6 %copy-start.2 = (bf16[32,3840]{1,0:T(8,128)(2,1)S(1)}, bf16[32,3840]{1,0:T(8,128)(2,1)}, u32[]{:S(2)}) copy-start(bf16[32,3840]{1,0:T(8,128)(2,1)} %all_refs_2_.1) | copy-start | bytes 737284
  2.5 7.6 %collective-permute-start.1 = (bf16[2,15360]{1,0:T(2,128)(2,1)}, bf16[2,15360]{1,0:T(2,128)(2,1)S(1)}, u32[]{:S(2)}, u32[]{:S(2)}) collective-permute-start(bf16[2,15360]{1,0:T(2,128)(2,1)} %get-tuple-element.29), channel_id=1, source_target_pairs={{0,4},{4,0},{8,12},{12,8},{1,5},{5,1},{9,13},{13,9},{2,6},{6,2},{1... | collective-permute-start | bytes 184328 | tf_op jit(solution)/shard_map/ppermute | solution.py:676
  7.1 1.7 %copy-start.3 = (bf16[27,36864]{1,0:T(8,128)(2,1)S(1)}, bf16[27,36864]{1,0:T(8,128)(2,1)}, u32[]{:S(2)}) copy-start(bf16[27,36864]{1,0:T(8,128)(2,1)} %flat_ref.1) | copy-start | bytes 5971972
  10.0 1.6 %copy-start.6 = (f32[192]{0:T(256)S(1)}, f32[192]{0:T(256)}, u32[]{:S(2)}) copy-start(f32[192]{0:T(256)} %param.13) | copy-start | bytes 2308
  10.0 7.3 %copy-start.4 = (bf16[9,18432]{1,0:T(8,128)(2,1)S(1)}, bf16[9,18432]{1,0:T(8,128)(2,1)}, u32[]{:S(2)}) copy-start(bf16[9,18432]{1,0:T(8,128)(2,1)} %up_ref.1) | copy-start | bytes 995332
  10.1 7.3 %copy-start.5 = (bf16[27,9216]{1,0:T(8,128)(2,1)S(1)}, bf16[27,9216]{1,0:T(8,128)(2,1)}, u32[]{:S(2)}) copy-start(bf16[27,9216]{1,0:T(8,128)(2,1)} %four_ref.1) | copy-start | bytes 1492996
  10.1 8.1 %copy-start.7 = (f32[192]{0:T(256)S(1)}, f32[192]{0:T(256)}, u32[]{:S(2)}) copy-start(f32[192]{0:T(256)} %param.14) | copy-start | bytes 2308
  10.3 10.6 %collective-permute-start.2 = (bf16[20,2688]{1,0:T(8,128)(2,1)S(1)}, bf16[20,2688]{1,0:T(8,128)(2,1)S(1)}, u32[]{:S(2)}, u32[]{:S(2)}) collective-permute-start(bf16[20,2688]{1,0:T(8,128)(2,1)S(1)} %shard_map.111), channel_id=1, source_target_pairs={{0,1},{1,0},{2,3},{3,2},{16,17},{17,16},{18,19},{19,18},{4,5},{5,4... | collective-permute-start | bytes 322568 | tf_op jit(solution)/shard_map/ppermute | solution.py:693
  12.3 8.6 %collective-permute-start.3 = (bf16[20,2688]{1,0:T(8,128)(2,1)S(1)}, bf16[20,2688]{1,0:T(8,128)(2,1)S(1)}, u32[]{:S(2)}, u32[]{:S(2)}) collective-permute-start(bf16[20,2688]{1,0:T(8,128)(2,1)S(1)} %shard_map.113), channel_id=1, source_target_pairs={{1,2},{2,1},{3,16},{16,3},{17,18},{18,17},{5,6},{6,5},{7,20},{20,7... | collective-permute-start | bytes 322568 | tf_op jit(solution)/shard_map/ppermute | solution.py:693
  18.2 2.7 %copy-start.8 = (f32[96]{0:T(128)S(1)}, f32[96]{0:T(128)}, u32[]{:S(2)}) copy-start(f32[96]{0:T(128)} %param.17) | copy-start | bytes 1156
  18.2 2.7 %copy-start.9 = (f32[96]{0:T(128)S(1)}, f32[96]{0:T(128)}, u32[]{:S(2)}) copy-start(f32[96]{0:T(128)} %param.19) | copy-start | bytes 1156
  18.2 2.7 %copy-start.10 = (f32[96]{0:T(128)S(1)}, f32[96]{0:T(128)}, u32[]{:S(2)}) copy-start(f32[96]{0:T(128)} %param.21) | copy-start | bytes 1156
